TPU v7x, 256 devices: a whole 4x4x8 slice. The times are simulated.
256 devices in a mesh: leaf: 64 (over y, z, core), panel: 4 (over x).
Axes of the slice: x: 4, y: 4, z: 8, core: 2. Of those that a mesh axis runs over, the one named last changes fastest.
Arguments:
- inverse_top: float32 [640, 640], P('leaf', 'panel'), may hold values from -1 to 2, as said below
- inverse_second: float32 [1280, 640], P('leaf', 'panel'), may hold values from -1 to 2, as said below
- inverse_third: float32 [2560, 640], P('leaf', 'panel'), may hold values from -1 to 2, as said below
- inverse_bottom: float32 [5120, 640], P('leaf', 'panel'), may hold values from -1 to 2, as said below
- below_second: float32 [1280, 640], P('leaf', 'panel'), may hold values from -0.125 to 0.125
- below_third: float32 [5120, 640], P('leaf', 'panel'), may hold values from -0.078125 to 0.078125
- below_bottom: float32 [15360, 640], P('leaf', 'panel'), may hold values from -0.0625 to 0.0625
Outputs:
- variance_top: float32 [640], P('leaf')
- variance_second: float32 [1280], P('leaf')
- variance_third: float32 [2560], P('leaf')
- variance_bottom: float32 [5120], P('leaf')
Inputs may be any that keep to these rules, and one draw needn't show every extreme that they name: `inverse_top`: each aligned block of 640 rows is lower triangular, with its diagonal entries in 0.5 to 1.6. `inverse_second`: each aligned block of 640 rows is lower triangular, with its diagonal entries in 0.5 to 1.6. `inverse_third`: each aligned block of 640 rows is lower triangular, with its diagonal entries in 0.5 to 1.6. `inverse_bottom`: each aligned block of 640 rows is lower triangular, with its diagonal entries in 0.5 to 1.6.
All inputs are finite; a program needn't handle non-finite values.
Results may differ from a plain program's by a relative error of at most 0.00018.
Values sent between devices are 32-bit elements; how exact they have to be, the bound alone decides.
No kernel may reach another device: no remote copies, remote signals or barrier semaphores. Data moves between devices by JAX's collectives and lax.ppermute only.
A program may use at most 128 MiB of HBM per device.

v0:
```python
import jax
import jax.numpy as jnp
from jax import lax
from jax.sharding import PartitionSpec as P


def swapped(value, axis, stride):
    mask = 2**stride
    pairs = [(source, source ^ mask) for source in range(lax.axis_size(axis))]
    return lax.ppermute(value, axis, pairs)


def product(left_side, right_side):
    return jnp.dot(
        left_side, right_side, precision=lax.Precision.HIGHEST, preferred_element_type=jnp.float32
    )


def inner_columns(left_side, right_side):
    return lax.dot_general(
        left_side,
        right_side,
        (((0,), (0,)), ((), ())),
        precision=lax.Precision.HIGHEST,
        preferred_element_type=jnp.float32,
    )


def leaf_doubling(block_rows, groups):
    for bit_pos in range(groups.bit_length() - 1):
        partner = swapped(block_rows, "leaf", bit_pos)
        upper_bit = lax.axis_index("leaf") // 2**bit_pos % 2
        block_rows = jnp.where(
            upper_bit == 1,
            jnp.concatenate([partner, block_rows], 0),
            jnp.concatenate([block_rows, partner], 0),
        )
    return block_rows


def fetch_node(below_part, inverse_part, height):
    if height == 0:
        stacked = inverse_part
    else:
        stacked = jnp.concatenate([below_part, inverse_part], 0)
    full_cols = lax.all_gather(stacked, "panel", axis=1, tiled=True)
    groups = lax.axis_size("leaf") // 2**height
    rows_dev = full_cols.shape[0]
    block_width = full_cols.shape[1]
    node_rows = leaf_doubling(full_cols, groups).reshape(groups, rows_dev, block_width)
    below_rows = height * block_width // groups
    inverse = node_rows[:, below_rows:].reshape(block_width, block_width)
    if height == 0:
        return (None, inverse)
    below_block = node_rows[:, :below_rows].reshape(height * block_width, block_width)
    return (below_block, inverse)


def shards(
    inverse_top,
    inverse_second,
    inverse_third,
    inverse_bottom,
    below_second,
    below_third,
    below_bottom,
):
    inverses = [inverse_top, inverse_second, inverse_third, inverse_bottom]
    belows = [None, below_second, below_third, below_bottom]
    outputs = []
    path_block = None
    for height in range(4):
        below_block, inverse = fetch_node(belows[height], inverses[height], height)
        groups = lax.axis_size("leaf") // 2**height
        place_idx = lax.axis_index("leaf") % groups
        block_width = inverse.shape[0]
        piece_len = block_width // groups
        col_count = block_width // lax.axis_size("panel")
        col_start = lax.axis_index("panel") * col_count
        if height == 0:
            gram_block = inner_columns(inverse, inverse)
            variance = jnp.diagonal(gram_block)
            path_block = gram_block
        else:
            inverse_cols = lax.dynamic_slice_in_dim(inverse, col_start, col_count, 1)
            mixed_cols = product(below_block, inverse_cols)
            side_cols = -product(path_block, mixed_cols)
            if height < 3:
                mixed_block = lax.all_gather(mixed_cols, "panel", axis=1, tiled=True)
                gram_cols = inner_columns(inverse, inverse_cols) - inner_columns(
                    mixed_block, side_cols
                )
                side_block, gram_block = (
                    lax.all_gather(side_cols, "panel", axis=1, tiled=True),
                    lax.all_gather(gram_cols, "panel", axis=1, tiled=True),
                )
                variance = jnp.diagonal(gram_block)
                upper_half = jnp.concatenate([path_block, side_block], 1)
                lower_half = jnp.concatenate([side_block.T, gram_block], 1)
                path_block = jnp.concatenate([upper_half, lower_half], 0)
            else:
                variance_cols = jnp.sum(inverse_cols * inverse_cols, 0) - jnp.sum(
                    mixed_cols * side_cols, 0
                )
                variance = lax.all_gather(variance_cols, "panel", axis=0, tiled=True)
        outputs.append(lax.dynamic_slice_in_dim(variance, place_idx * piece_len, piece_len, 0))
    return (outputs[0], outputs[1], outputs[2], outputs[3])


def solution(mesh):
    placed = (
        P("leaf", "panel"),
        P("leaf", "panel"),
        P("leaf", "panel"),
        P("leaf", "panel"),
        P("leaf", "panel"),
        P("leaf", "panel"),
        P("leaf", "panel"),
    )
    return jax.shard_map(
        shards,
        mesh=mesh,
        in_specs=placed,
        out_specs=(P("leaf"), P("leaf"), P("leaf"), P("leaf")),
        check_vma=False,
    )
```

profile of v0, /device:TPU:2, one launch (start us, length us, event | category | flops | bytes accessed | tf_op | source)
XLA Modules:
  0.0 712.8 jit_solution(7258954816295112865)
XLA Ops:
  8.0 12.1 %all-gather.1 = f32[4,160,40]{1,2,0:T(8,128)S(1)} all-gather(f32[1,160,40]{1,2,0:T(8,128)S(1)} %maximum_bitcast_fusion), channel_id=1, replica_groups=mesh['leaf'=64,'panel'=4] {'panel'}, dimensions={0}, use_global_device_ids=true | all-gather | bytes 128000 | tf_op jit(solution)/shard_map/all_gather | solution.py:46
  20.4 1.3 collective-permute-done.6
  21.7 2.0 collective-permute-start.7
  23.7 5.4 collective-permute-done.7
  29.2 3.4 collective-permute-start.8
  32.5 17.9 %collective-permute-done.8 = f32[160,640]{1,0:T(8,128)S(1)} collective-permute-done((f32[160,640]{1,0:T(8,128)S(1)}, f32[160,640]{1,0:T(8,128)S(1)}, u32[]{:S(2)}, u32[]{:S(2)}) %collective-permute-start.8) | collective-permute-done | bytes 409632 | tf_op jit(solution)/shard_map/ppermute | solution.py:10
  50.5 6.3 collective-permute-start.9
  56.8 35.8 %collective-permute-done.9 = f32[320,640]{1,0:T(8,128)S(1)} collective-permute-done((f32[320,640]{1,0:T(8,128)S(1)}, f32[320,640]{1,0:T(8,128)S(1)}, u32[]{:S(2)}, u32[]{:S(2)}) %collective-permute-start.9) | collective-permute-done | bytes 819232 | tf_op jit(solution)/shard_map/ppermute | solution.py:10
  92.7 1.7 collective-permute-start.10
  94.3 11.8 %all-gather = f32[4,160,10]{1,2,0:T(8,128)S(1)} all-gather(f32[1,160,10]{1,2,0:T(8,128)S(1)} %bitcast.54), channel_id=1, replica_groups=mesh['leaf'=64,'panel'=4] {'panel'}, dimensions={0}, use_global_device_ids=true | all-gather | bytes 32000 | tf_op jit(solution)/shard_map/all_gather | solution.py:46
  106.5 1.2 collective-permute-done
  107.7 21.6 %collective-permute-done.10 = f32[640,640]{1,0:T(8,128)S(1)} collective-permute-done((f32[640,640]{1,0:T(8,128)S(1)}, f32[640,640]{1,0:T(8,128)S(1)}, u32[]{:S(2)}, u32[]{:S(2)}) %collective-permute-start.10) | collective-permute-done | bytes 1638432 | tf_op jit(solution)/shard_map/ppermute | solution.py:10
  129.5 1.5 fusion.57
  131.1 1.3 reshape.42
  132.4 1.7 reshape.41
  134.4 2.7 fusion.46
  137.3 6.6 collective-permute-done.2
  144.0 3.6 collective-permute-start.3
  147.7 8.6 %collective-permute-done.3 = f32[80,640]{1,0:T(8,128)S(1)} collective-permute-done((f32[80,640]{1,0:T(8,128)S(1)}, f32[80,640]{1,0:T(8,128)S(1)}, u32[]{:S(2)}, u32[]{:S(2)}) %collective-permute-start.3) | collective-permute-done | bytes 204832 | tf_op jit(solution)/shard_map/ppermute | solution.py:10
  156.3 1.7 collective-permute-start.4
  158.0 9.7 %collective-permute-done.4 = f32[160,640]{1,0:T(8,128)S(1)} collective-permute-done((f32[160,640]{1,0:T(8,128)S(1)}, f32[160,640]{1,0:T(8,128)S(1)}, u32[]{:S(2)}, u32[]{:S(2)}) %collective-permute-start.4) | collective-permute-done | bytes 409632 | tf_op jit(solution)/shard_map/ppermute | solution.py:10
  167.7 4.3 collective-permute-start.5
  172.4 12.4 %all_gather.37 = f32[120,640]{0,1:T(8,128)S(1)} all-gather(f32[120,160]{0,1:T(8,128)S(1)} %pad_maximum_fusion.1), channel_id=1, replica_groups=mesh['leaf'=64,'panel'=4] {'panel'}, dimensions={1}, use_global_device_ids=true | all-gather | bytes 384000 | tf_op jit(solution)/shard_map/all_gather | solution.py:46
  185.1 1.6 collective-permute-done.11
  186.6 0.9 maximum_select_fusion.12
  187.8 8.0 %fusion.31 = f32[640,640]{0,1:T(8,128)S(1)} fusion(f32[320,640]{1,0:T(8,128)} %copy-done.4, f32[320,640]{1,0:T(8,128)} %collective-permute-done.5, pred[]{:T(512)S(6)} %eq.53), kind=kOutput, calls=%fused_computation.34 | convolution fusion | flops 3146956800 | bytes 3276801 | tf_op jit(solution)/shard_map/dot_general | solution.py:20
  195.8 2.3 convolution_negate_fusion
  198.1 5.8 collective-permute-done.12
  203.9 1.8 maximum_select_fusion.9
  205.7 1.1 collective-permute-start.13
  206.8 54.4 %collective-permute-done.13 = f32[480,640]{1,0:T(8,128)S(1)} collective-permute-done((f32[480,640]{1,0:T(8,128)S(1)}, f32[480,640]{1,0:T(8,128)S(1)}, u32[]{:S(2)}, u32[]{:S(2)}) %collective-permute-start.13) | collective-permute-done | bytes 1228832 | tf_op jit(solution)/shard_map/ppermute | solution.py:10
  261.2 1.6 maximum_select_fusion.4
  262.9 3.1 collective-permute-start.14
  265.9 3.3 fusion.58
  269.2 2.5 convolution_subtract_fusion.1
  271.8 102.9 %collective-permute-done.14 = f32[960,640]{1,0:T(8,128)} collective-permute-done((f32[960,640]{1,0:T(8,128)}, f32[960,640]{1,0:T(8,128)}, u32[]{:S(2)}, u32[]{:S(2)}) %collective-permute-start.14) | collective-permute-done | bytes 2457632 | tf_op jit(solution)/shard_map/ppermute | solution.py:10
  374.7 4.4 maximum_select_fusion.1
  379.4 4.4 fusion.43
  383.8 8.8 %all-gather.17.cloned.1.call-start = ((), (), s32[]{:S(2)}) async-start(), calls=%async_computation.4 | async-start | bytes 2048000 | tf_op jit(solution)/shard_map/all_gather | solution.py:95
  393.3 1.1 pad_maximum_fusion
  394.4 2.7 copy.40
  397.2 7.8 %fusion.22 = f32[1280,160]{0,1:T(8,128)} fusion(f32[1280,160]{0,1:T(8,128)} %fusion.43, f32[640,640]{0,1:T(8,128)} %all-gather.11.cloned.1.call-done, f32[640,640]{0,1:T(8,128)} %bitcast.48, f32[640,640]{0,1:T(8,128)} %all-gather.15.cloned.1.call-done, f32[640,640]{0,1:T(8,128)S(1)} %fusion.31), kind=kOutput, calls=%fused_computation.29 | convolution fusion | flops 3150848000 | bytes 8192000 | tf_op jit(solution)/shard_map/dot_general | solution.py:14
  405.0 17.2 %all-gather.13.cloned.1.call-done = f32[1280,640]{0,1:T(8,128)} async-done(((f32[1280,160]{0,1:T(8,128)}), f32[1280,640]{0,1:T(8,128)}) %all-gather.13.cloned.1.call-update) | async-done | bytes 3276816 | tf_op jit(solution)/shard_map/all_gather | solution.py:89
  422.2 5.4 fusion.59
  427.6 2.5 convolution_subtract_fusion
  430.1 12.9 %all_gather.41 = f32[320,640]{0,1:T(8,128)S(1)} all-gather(f32[320,160]{0,1:T(8,128)S(1)} %pad_maximum_fusion), channel_id=1, replica_groups=mesh['leaf'=64,'panel'=4] {'panel'}, dimensions={1}, use_global_device_ids=true | all-gather | bytes 1024000 | tf_op jit(solution)/shard_map/all_gather | solution.py:46
  443.5 0.8 copy-done.3
  444.3 1.5 collective-permute-done.15
  445.8 1.6 maximum_select_fusion.8
  447.4 2.0 collective-permute-start.16
  449.4 36.2 %collective-permute-done.16 = f32[640,640]{1,0:T(8,128)} collective-permute-done((f32[640,640]{1,0:T(8,128)S(1)}, f32[640,640]{1,0:T(8,128)}, u32[]{:S(2)}, u32[]{:S(2)}) %collective-permute-start.16) | collective-permute-done | bytes 1638432 | tf_op jit(solution)/shard_map/ppermute | solution.py:10
  485.6 4.2 maximum_select_fusion.3
  489.7 2.9 collective-permute-start.17
  493.9 5.4 gather_fusion
  499.9 133.7 %collective-permute-done.17 = f32[1280,640]{1,0:T(8,128)} collective-permute-done((f32[1280,640]{1,0:T(8,128)}, f32[1280,640]{1,0:T(8,128)}, u32[]{:S(2)}, u32[]{:S(2)}) %collective-permute-start.17) | collective-permute-done | bytes 3276832 | tf_op jit(solution)/shard_map/ppermute | solution.py:10
  633.7 8.3 %maximum_select_fusion = f32[2560,640]{1,0:T(8,128)} fusion(f32[1280,640]{1,0:T(8,128)} %maximum_select_fusion.3, f32[1280,640]{1,0:T(8,128)} %collective-permute-done.17, pred[]{:T(512)S(6)} %eq.56), kind=kLoop, calls=%fused_computation.25 | loop fusion | flops 4915200 | bytes 13107201 | tf_op jit(solution)/shard_map/jit(_where)/select_n | solution.py:33
  641.9 1.5 slice.34
  643.5 2.7 slice.35
  646.4 6.1 fusion.41
  652.5 5.4 gather_fusion.1
  658.5 10.5 %gather_fusion.2 = f32[640]{0:T(1024)S(1)} fusion(f32[640,640]{0,1:T(8,128)} %all-gather.17.cloned.1.call-done, s32[640]{0:T(1024)S(1)} %or_reduce_fusion), kind=kCustom, calls=%fused_computation.2 | custom fusion | bytes 10240 | tf_op jit(solution)/shard_map/jit(diagonal)/cond/branch_0_fun/gather | solution.py:97
  669.7 4.6 copy.45
  674.3 19.8 %fusion.37 = f32[160]{0:T(256)S(1)} fusion(f32[1920,160]{0,1:T(8,128)} %fusion.41, f32[640,640]{0,1:T(8,128)} %all-gather.17.cloned.1.call-done, f32[640,1280]{0,1:T(8,128)} %bitcast.47, f32[1280,640]{0,1:T(8,128)} %all-gather.19.cloned.1.call-done, f32[640,640]{0,1:T(8,128)S(1)} %copy-done, f32[640,640]{0,1:T(8,128)} %bitcast.49, ...), kind=kOutput, calls=%fused_computation.43 | convolution fusion | flops 7100928000 | bytes 15975040 | tf_op jit(solution)/shard_map/dot_general | solution.py:14
  694.2 10.8 %all-reduce = f32[640]{0:T(1024)S(1)} all-reduce(f32[640]{0:T(1024)S(1)} %subtract_dynamic-update-slice_fusion), channel_id=1, replica_groups=mesh['leaf'=64,'panel'=4] {'panel'}, use_global_device_ids=true, to_apply=%add | all-reduce | flops 640 | bytes 5120
  (76 shorter events, 8.3 us)
Async XLA Ops:
  7.2 258.8 %all-gather.9.cloned.1.call-start = ((), (), s32[]{:S(2)}) async-start(), calls=%async_computation | async-start | bytes 2048000 | tf_op jit(solution)/shard_map/all_gather | solution.py:89
  20.3 1.4 collective-permute-start.6
  21.7 7.4 %collective-permute-start.7 = (f32[80,640]{1,0:T(8,128)S(1)}, f32[80,640]{1,0:T(8,128)S(1)}, u32[]{:S(2)}, u32[]{:S(2)}) collective-permute-start(f32[80,640]{1,0:T(8,128)S(1)} %maximum_select_fusion.16), channel_id=1, source_target_pairs={{0,8},{4,12},{8,0},{12,4},{16,24},{20,28},{24,16},{28,20},{32,40},... | collective-permute-start | bytes 614408 | tf_op jit(solution)/shard_map/ppermute | solution.py:10
  29.2 21.3 %collective-permute-start.8 = (f32[160,640]{1,0:T(8,128)S(1)}, f32[160,640]{1,0:T(8,128)S(1)}, u32[]{:S(2)}, u32[]{:S(2)}) collective-permute-start(f32[160,640]{1,0:T(8,128)S(1)} %maximum_select_fusion.14), channel_id=1, source_target_pairs={{0,16},{4,20},{8,24},{12,28},{16,0},{20,4},{24,8},{28,12},{32,48},... | collective-permute-start | bytes 1228808 | tf_op jit(solution)/shard_map/ppermute | solution.py:10
  50.5 42.1 %collective-permute-start.9 = (f32[320,640]{1,0:T(8,128)S(1)}, f32[320,640]{1,0:T(8,128)S(1)}, u32[]{:S(2)}, u32[]{:S(2)}) collective-permute-start(f32[320,640]{1,0:T(8,128)S(1)} %maximum_select_fusion.11), channel_id=1, source_target_pairs={{0,32},{4,36},{8,40},{12,44},{16,48},{20,52},{24,56},{28,60},{32,0... | collective-permute-start | bytes 2457608 | tf_op jit(solution)/shard_map/ppermute | solution.py:10
  56.8 37.6 %copy-start.8 = (f32[10,160]{1,0:T(8,128)S(1)}, f32[10,160]{1,0:T(8,128)}, u32[]{:S(2)}) copy-start(f32[10,160]{1,0:T(8,128)} %param.7) | copy-start | bytes 19204
  92.7 36.6 %collective-permute-start.10 = (f32[640,640]{1,0:T(8,128)S(1)}, f32[640,640]{1,0:T(8,128)S(1)}, u32[]{:S(2)}, u32[]{:S(2)}) collective-permute-start(f32[640,640]{1,0:T(8,128)S(1)} %maximum_select_fusion.7), channel_id=1, source_target_pairs={{0,64},{4,68},{8,72},{12,76},{16,80},{20,84},{24,88},{28,92},{32,9... | collective-permute-start | bytes 4915208 | tf_op jit(solution)/shard_map/ppermute | solution.py:10
  106.3 1.3 collective-permute-start
  107.6 29.6 %collective-permute-start.1 = (f32[20,640]{1,0:T(8,128)S(1)}, f32[20,640]{1,0:T(8,128)S(1)}, u32[]{:S(2)}, u32[]{:S(2)}) collective-permute-start(f32[20,640]{1,0:T(8,128)S(1)} %maximum_select_fusion.18), channel_id=1, source_target_pairs={{0,8},{4,12},{8,0},{12,4},{16,24},{20,28},{24,16},{28,20},{32,40},... | collective-permute-start | bytes 153608 | tf_op jit(solution)/shard_map/ppermute | solution.py:10
  132.4 2.0 copy-start.1
  137.1 34.9 %copy-start.7 = (f32[40,160]{1,0:T(8,128)S(1)}, f32[40,160]{1,0:T(8,128)}, u32[]{:S(2)}) copy-start(f32[40,160]{1,0:T(8,128)} %param.9) | copy-start | bytes 76804
  137.1 35.0 %copy-start.5 = (f32[80,160]{1,0:T(8,128)S(1)}, f32[80,160]{1,0:T(8,128)}, u32[]{:S(2)}) copy-start(f32[80,160]{1,0:T(8,128)} %param.12) | copy-start | bytes 153604
  137.2 257.3 %all-gather.15.cloned.1.call-start = ((), (), s32[]{:S(2)}) async-start(), calls=%async_computation.3 | async-start | bytes 2048000 | tf_op jit(solution)/shard_map/all_gather | solution.py:94
  137.2 6.7 collective-permute-start.2
  144.0 12.3 %collective-permute-start.3 = (f32[80,640]{1,0:T(8,128)S(1)}, f32[80,640]{1,0:T(8,128)S(1)}, u32[]{:S(2)}, u32[]{:S(2)}) collective-permute-start(f32[80,640]{1,0:T(8,128)S(1)} %maximum_select_fusion.15), channel_id=1, source_target_pairs={{0,32},{4,36},{8,40},{12,44},{16,48},{20,52},{24,56},{28,60},{32,0... | collective-permute-start | bytes 614408 | tf_op jit(solution)/shard_map/ppermute | solution.py:10
  156.3 11.4 %collective-permute-start.4 = (f32[160,640]{1,0:T(8,128)S(1)}, f32[160,640]{1,0:T(8,128)S(1)}, u32[]{:S(2)}, u32[]{:S(2)}) collective-permute-start(f32[160,640]{1,0:T(8,128)S(1)} %maximum_select_fusion.13), channel_id=1, source_target_pairs={{0,64},{4,68},{8,72},{12,76},{16,80},{20,84},{24,88},{28,92},{32,9... | collective-permute-start | bytes 1228808 | tf_op jit(solution)/shard_map/ppermute | solution.py:10
  167.7 20.0 %copy-start.4 = (f32[320,640]{1,0:T(8,128)}, f32[320,640]{1,0:T(8,128)S(1)}, u32[]{:S(2)}) copy-start(f32[320,640]{1,0:T(8,128)S(1)} %maximum_select_fusion.10) | copy-start | bytes 2457604
  167.7 20.0 %collective-permute-start.5 = (f32[320,640]{1,0:T(8,128)S(1)}, f32[320,640]{1,0:T(8,128)}, u32[]{:S(2)}, u32[]{:S(2)}) collective-permute-start(f32[320,640]{1,0:T(8,128)S(1)} %maximum_select_fusion.10), channel_id=1, source_target_pairs={{0,128},{4,132},{8,136},{12,140},{16,144},{20,148},{24,152},{28,15... | collective-permute-start | bytes 2457608 | tf_op jit(solution)/shard_map/ppermute | solution.py:10
  184.9 1.7 collective-permute-start.11
  187.5 8.3 %copy-start.2 = (f32[640,160]{0,1:T(8,128)S(1)}, f32[640,160]{0,1:T(8,128)}, u32[]{:S(2)}) copy-start(f32[640,160]{0,1:T(8,128)} %fusion.46) | copy-start | bytes 1228804
  187.5 16.4 %collective-permute-start.12 = (f32[240,640]{1,0:T(8,128)}, f32[240,640]{1,0:T(8,128)}, u32[]{:S(2)}, u32[]{:S(2)}) collective-permute-start(f32[240,640]{1,0:T(8,128)} %maximum_select_fusion.12), channel_id=1, source_target_pairs={{0,8},{4,12},{8,0},{12,4},{16,24},{20,28},{24,16},{28,20},{32,40},... | collective-permute-start | bytes 1843208 | tf_op jit(solution)/shard_map/ppermute | solution.py:10
  198.1 199.1 %all-gather.11.cloned.1.call-start = ((), (), s32[]{:S(2)}) async-start(), calls=%async_computation.1 | async-start | bytes 2048000 | tf_op jit(solution)/shard_map/all_gather | solution.py:95
  205.7 55.6 %collective-permute-start.13 = (f32[480,640]{1,0:T(8,128)S(1)}, f32[480,640]{1,0:T(8,128)S(1)}, u32[]{:S(2)}, u32[]{:S(2)}) collective-permute-start(f32[480,640]{1,0:T(8,128)S(1)} %maximum_select_fusion.9), channel_id=1, source_target_pairs={{0,16},{4,20},{8,24},{12,28},{16,0},{20,4},{24,8},{28,12},{32,48},... | collective-permute-start | bytes 3686408 | tf_op jit(solution)/shard_map/ppermute | solution.py:10
  262.9 111.8 %collective-permute-start.14 = (f32[960,640]{1,0:T(8,128)}, f32[960,640]{1,0:T(8,128)}, u32[]{:S(2)}, u32[]{:S(2)}) collective-permute-start(f32[960,640]{1,0:T(8,128)} %maximum_select_fusion.4), channel_id=1, source_target_pairs={{0,32},{4,36},{8,40},{12,44},{16,48},{20,52},{24,56},{28,60},{32,0... | collective-permute-start | bytes 7372808 | tf_op jit(solution)/shard_map/ppermute | solution.py:10
  271.8 150.5 %all-gather.13.cloned.1.call-start = ((), (), s32[]{:S(2)}) async-start(), calls=%async_computation.2 | async-start | bytes 4096000 | tf_op jit(solution)/shard_map/all_gather | solution.py:89
  379.4 13.2 %copy-start.6 = (f32[80,160]{1,0:T(8,128)S(1)}, f32[80,160]{1,0:T(8,128)}, u32[]{:S(2)}) copy-start(f32[80,160]{1,0:T(8,128)} %param.10) | copy-start | bytes 153604
  383.8 274.7 %all-gather.17.cloned.1.call-start = ((), (), s32[]{:S(2)}) async-start(), calls=%async_computation.4 | async-start | bytes 2048000 | tf_op jit(solution)/shard_map/all_gather | solution.py:95
  430.1 239.6 %all-gather.19.cloned.1.call-start = ((), (), s32[]{:S(2)}) async-start(), calls=%async_computation.5 | async-start | bytes 4096000 | tf_op jit(solution)/shard_map/all_gather | solution.py:94
  443.4 0.9 copy-start.3
  443.4 2.4 collective-permute-start.15
  447.4 38.2 %collective-permute-start.16 = (f32[640,640]{1,0:T(8,128)S(1)}, f32[640,640]{1,0:T(8,128)}, u32[]{:S(2)}, u32[]{:S(2)}) collective-permute-start(f32[640,640]{1,0:T(8,128)S(1)} %maximum_select_fusion.8), channel_id=1, source_target_pairs={{0,8},{4,12},{8,0},{12,4},{16,24},{20,28},{24,16},{28,20},{32,40},... | collective-permute-start | bytes 4915208 | tf_op jit(solution)/shard_map/ppermute | solution.py:10
  449.4 43.3 %copy-start.9 = (u32[256]{0:T(256)S(1)}, u32[256]{0:T(256)}, u32[]{:S(2)}) copy-start(u32[256]{0:T(256)} %constant.258) | copy-start | bytes 3076
  489.7 143.9 %collective-permute-start.17 = (f32[1280,640]{1,0:T(8,128)}, f32[1280,640]{1,0:T(8,128)}, u32[]{:S(2)}, u32[]{:S(2)}) collective-permute-start(f32[1280,640]{1,0:T(8,128)} %maximum_select_fusion.3), channel_id=1, source_target_pairs={{0,16},{4,20},{8,24},{12,28},{16,0},{20,4},{24,8},{28,12},{32,48},... | collective-permute-start | bytes 9830408 | tf_op jit(solution)/shard_map/ppermute | solution.py:10
  646.4 6.1 copy-start
Sparse Core Ops, SparseCore 0:
  137.2 28.1 all-gather.8
  198.2 27.4 all-gather.14
  271.9 24.3 all-gather.10
  383.9 38.2 all-gather.12
  430.2 29.5 all-gather.16
  461.5 43.3 all-gather.18
where the time goes:
time: 722 us; the launch traced here: 713 us
  waiting for transfers between devices  462 us (64%)
  matrix products  64.6 us (9%)
  blocking collectives  60 us (8%)
  local copies, waits for them, and re-layouts  43.7 us (6%)
  starting transfers between devices  41.8 us (6%)
  other arithmetic  25.6 us (4%)
  between operations  15.7 us (2%)
    ppermute x18, waiting for transfers between devices, swapped(): return lax.ppermute(value, axis, pairs)  444 us
    all_gather x4, blocking collectives, fetch_node(): full_cols = lax.all_gather(stacked, 'panel', axis=1, tiled=True)  49.3 us
    dot_general x6, matrix products, product(): jnp.dot(left_side, right_side, precision=lax.Precision.HIGHEST, preferred...  43 us
    ppermute x18, starting transfers between devices, swapped(): return lax.ppermute(value, axis, pairs)  32.8 us
    select_n x17, other arithmetic, leaf_doubling(): jnp.where(upper_bit == 1, jnp.concatenate([partner, block_rows], 0), jnp....  23.2 us
    dot_general x5, matrix products, inner_columns(): lax.dot_general(left_side, right_side, (((0,), (0,)), ((), ())), precisio...  21.6 us
    gather x3, local copies, waits for them, and re-layouts, shards(): variance = jnp.diagonal(gram_block)  21.4 us
    all_gather x2, waiting for transfers between devices, shards(): mixed_block = lax.all_gather(mixed_cols, 'panel', axis=1, tiled=True)  17.2 us
  transfers between devices with their start and end apart: 24, of which 17 were waited for; matrix products, arithmetic and copies ran while one was open for 14% of the time, Pallas kernels for 0%

commit v1 on v0

v1 whole, which is shorter than its diff:
```python
import functools

import jax
import jax.numpy as jnp
import numpy as np
from jax import lax
from jax.experimental import pallas as pl
from jax.experimental.pallas import tpu as pltpu
from jax.sharding import Mesh
from jax.sharding import PartitionSpec as P

W = 640
Q = 160
ALL = ("node", "lane", "panel")
F32 = jnp.float32
VMEM = pl.BlockSpec(memory_space=pltpu.VMEM)
SMEM = pl.BlockSpec(memory_space=pltpu.SMEM)
HBM = pl.BlockSpec(memory_space=pl.ANY)


def device(y, z, c, x):
    return ((y % 4 * 8 + z % 8) * 2 + c) * 4 + x % 4


def pairs_of(move):
    pairs = []
    for y in range(4):
        for z in range(8):
            for c in range(2):
                for x in range(4):
                    pairs.append((device(y, z, c, x), device(*move(y, z, c, x))))
    return pairs


def step_x(parity):
    return pairs_of(lambda y, z, c, x: (y, z, c, x + (1 if (x + c + parity) % 2 == 0 else -1)))


def step_z(parity):
    return pairs_of(lambda y, z, c, x: (y, z + (1 if (z + c + parity) % 2 == 0 else -1), c, x))


def step_y(count):
    return pairs_of(lambda y, z, c, x: (y + count, z, c, x))


SWAP = pairs_of(lambda y, z, c, x: (y, z, 1 - c, x))


def to_owner(y, z, c, x):
    lane = z % 4 * 2 + c
    lane, x = 2 * x + lane // 4, lane % 4
    return (y, z // 4 * 4 + lane // 2, lane % 2, x)


OWNER = pairs_of(to_owner)


def permute(value, pairs):
    return lax.ppermute(value, ALL, pairs)


def permute_ids(ids, pairs):
    moved = np.zeros_like(ids)
    for source, target in pairs:
        moved[target] = ids[source]
    return moved


def gather_x(chunk, move, join):
    pair = join(chunk, move(chunk, step_x(0)))
    return [pair, move(pair, step_x(1))]


def gather_z(chunk, move, join):
    pair = join(chunk, move(chunk, step_z(0)))
    second = move(pair, step_z(1))
    third = move(second, step_z(0))
    return [pair, second, third, move(third, step_z(1))]


def join_rows(first, second):
    return jnp.concatenate([first, second], 0)


def join_ids(first, second):
    return np.concatenate([first, second], 1)


def natural_ids():
    ids = np.zeros((256, 1), np.int32)
    for y in range(4):
        for z in range(8):
            for c in range(2):
                for x in range(4):
                    ids[device(y, z, c, x), 0] = (z * 2 + c) * 4 + x
    return ids


def id_tables():
    own = natural_ids()
    by_x = join_ids(*gather_x(own, permute_ids, join_ids))
    first = gather_z(by_x, permute_ids, join_ids)
    first = first + [permute_ids(part, SWAP) for part in first]
    by_z = functools.reduce(join_ids, gather_z(own, permute_ids, join_ids))
    second = gather_x(by_z, permute_ids, join_ids)
    second = second + [permute_ids(part, SWAP) for part in second]
    return (
        by_x % 4,
        functools.reduce(join_ids, first),
        functools.reduce(join_ids, second),
    )


def split(value):
    high = value.astype(jnp.bfloat16)
    return high, (value - high.astype(F32)).astype(jnp.bfloat16)


def dot(left, right):
    return jnp.dot(left, right, preferred_element_type=F32)


def split_dot(left, right):
    rows = left.shape[0]
    left_high, left_low = split(left)
    right_high, right_low = split(right)
    both = dot(jnp.concatenate([left_high, left_low], 0), right_high)
    return both[:rows] + both[rows:] + dot(left_high, right_low)


def place(pieces, width):
    rows = pieces[0][0].shape[0]
    lane = lax.broadcasted_iota(jnp.int32, (rows, 128), 1)
    tiles = []
    for tile in range(width // 128):
        low = tile * 128
        total = jnp.zeros((rows, 128), F32)
        for value, source, length, target in pieces:
            start, stop = max(target, low), min(target + length, low + 128)
            if start >= stop:
                continue
            shift = (target - source) % 128
            moved = pltpu.roll(value, shift, 1) if shift else value
            inside = (lane >= start - low) & (lane < stop - low)
            total = jnp.where(inside, moved, total)
        tiles.append(total)
    return jnp.concatenate(tiles, 1)


def pack_kernel(d2, b2, b3, d1, b1, d0, x_out, y_out, rows):
    rows[...] = jnp.zeros(rows.shape, F32)
    rows[0:40, 0:Q] = d2[...]
    rows[40:120, 0:Q] = b2[...]
    x_out[0:Q, :] = rows[0:128, :].T[:Q]
    rows[0:240, 0:Q] = b3[...]
    below = rows[...].T
    x_out[Q : 2 * Q, :] = below[:Q, 0:128]
    x_out[2 * Q : 3 * Q, :] = below[:Q, 128:256]
    rows[0:128, :] = jnp.zeros((128, 256), F32)
    rows[0:20, 0:Q] = d1[...]
    rows[20:40, 0:Q] = b1[...]
    rows[40:50, 0:Q] = d0[...]
    y_out[...] = rows[0:128, :].T[:Q]


def merge_kernel(odd, own, one, two, three, out):
    lane = lax.broadcasted_iota(jnp.int32, (Q, 128), 1)
    is_odd = odd[0] == 1
    lower = jnp.where(is_odd, one[...], own[...])
    upper = jnp.where(is_odd, own[...], three[...])
    total = jnp.zeros((Q, 128), F32)
    for value, shift, start, stop in (
        (lower, 0, 0, 20),
        (upper, 20, 20, 40),
        (lower, 20, 40, 60),
        (upper, 40, 60, 80),
        (own[...], 40, 80, 90),
        (one[...], 50, 90, 100),
        (two[...], 60, 100, 110),
        (three[...], 70, 110, 120),
    ):
        moved = pltpu.roll(value, shift, 1) if shift else value
        total = jnp.where((lane >= start) & (lane < stop), moved, total)
    out[...] = total


def bottom_kernel(slots, inverse, pair, other, out, below, wide, sems):
    copies = []
    for slot in range(4):
        source = pair if slot < 2 else other
        column = pl.multiple_of(slots[slot] * Q, Q)
        for half in range(2):
            start = slot % 2 * 3 * Q + (1 + half) * Q
            copies.append(
                pltpu.make_async_copy(
                    source.at[pl.ds(start, Q), :],
                    below.at[half, pl.ds(column, Q), :],
                    sems.at[slot * 2 + half],
                )
            )
    for copy in copies:
        copy.start()
    wide[...] = jnp.zeros(wide.shape, F32)
    wide[:, 0:Q] = inverse[...]
    turned = wide[...].T[:Q]
    squares = jnp.sum(turned * turned, 1, keepdims=True)
    for copy in copies:
        copy.wait()
    mixed = split_dot(turned, jnp.concatenate([below[0], below[1]], 1))
    lane = lax.broadcasted_iota(jnp.int32, (Q, 256), 1)
    mixed = jnp.where(lane == 240, squares, mixed)
    out[...] = jnp.zeros(out.shape, F32)
    for part in range(8):
        out[part, 0:20, :] = mixed[part * 20 : part * 20 + 20]


def start_copies(table, sources, stage, sems):
    each = 64 // len(sources)
    copies = []
    for index, source in enumerate(sources):
        for atom in range(each):
            number = index * each + atom
            row = pl.multiple_of(table[number] * Q, Q)
            copies.append(
                pltpu.make_async_copy(
                    source.at[pl.ds(atom * Q, Q), :], stage.at[pl.ds(row, Q), :], sems.at[number]
                )
            )
    for copy in copies:
        copy.start()
    return copies


def block(stage, z):
    return jnp.concatenate(
        [stage[(2 * z) * W : (2 * z + 1) * W, :], stage[(2 * z + 1) * W : (2 * z + 2) * W, :]], 1
    )


def one_hot(rows, count, base):
    row = lax.broadcasted_iota(jnp.int32, (rows, W), 0)
    lane = lax.broadcasted_iota(jnp.int32, (rows, W), 1)
    return jnp.where((row < count) & (lane == base + row), 1.0, 0.0).astype(F32)


def third_kernel(table, base, mixed, *refs):
    sources = refs[:8]
    out, squares_out, stage, sems = refs[8:]
    copies = start_copies(table, sources, stage, sems)
    pieces = []
    for part in range(8):
        pieces.append((mixed[part, :, 0:128], 0, 128, part * 240))
        pieces.append((mixed[part, :, 128:256], 0, 112, part * 240 + 128))
    path = place(pieces, 3 * W)
    squares = mixed[0, :, 240:241]
    for copy in copies:
        copy.wait()
    cols = jnp.concatenate([path[:, 2 * W :], one_hot(16, 10, base[0])], 0)
    pieces = []
    for z in range(8):
        product = split_dot(cols, block(stage, z))
        for core in range(2):
            piece = product[:, core * 128 : core * 128 + 128]
            pieces.append((piece, 0, 40, z * 80 + core * 40))
    cols = place(pieces, W)
    squares = jnp.concatenate([squares, jnp.zeros((16, 1), F32)], 0)
    squares = squares + jnp.sum(cols * cols, 1, keepdims=True)
    pieces = []
    for z in range(8):
        product = split_dot(cols, block(stage, z))
        for core in range(2):
            piece = product[:, core * 128 : core * 128 + 128]
            pieces.append((piece, 40, 80, z * 160 + core * 80))
    change = place(pieces, 2 * W)
    out[0:24, :] = path[:, : 2 * W] - change[0:24]
    out[24:40, :] = -change[24:40]
    squares_out[...] = jnp.broadcast_to(squares, (40, 128))


def top_kernel(table, base, path, squares_in, *refs):
    sources = refs[:4]
    out, stage, sems = refs[4:]
    copies = start_copies(table, sources, stage, sems)
    for copy in copies:
        copy.wait()
    cols = jnp.concatenate([path[:, W:], one_hot(8, 5, base[1])], 0)
    pieces = []
    for z in range(8):
        product = split_dot(cols, block(stage, z))
        for core in range(2):
            piece = product[:, core * 128 : core * 128 + 128]
            for half in range(2):
                pieces.append((piece, half * 20, 20, half * 320 + z * 40 + core * 20))
    cols = place(pieces, W)
    squares = jnp.concatenate([squares_in[:, 0:1], jnp.zeros((8, 1), F32)], 0)
    squares = squares + jnp.sum(cols * cols, 1, keepdims=True)
    pieces = []
    for z in range(8):
        product = split_dot(cols, block(stage, z))
        for core in range(2):
            piece = product[:, core * 128 : core * 128 + 128]
            for half in range(2):
                pieces.append((piece, 40 + half * 20, 20, half * 320 + z * 40 + core * 20))
    change = place(pieces, W)
    cols = jnp.concatenate(
        [path[:, :W] - change[0:40], -change[40:48], one_hot(16, 10, base[2])], 0
    )
    squares = jnp.concatenate([squares, jnp.zeros((16, 1), F32)], 0)
    lane = lax.broadcasted_iota(jnp.int32, (64, 256), 1) % 128
    used = (lane >= 80) & (lane < 120)
    total = jnp.zeros((64, 256), F32)
    for z in range(8):
        product = split_dot(cols, block(stage, z))
        total = total + jnp.where(used, product * product, 0.0)
    squares = squares + jnp.sum(total, 1, keepdims=True)
    square = jnp.concatenate(
        [jnp.broadcast_to(squares, (64, 128)), jnp.zeros((64, 128), F32)], 0
    )
    out[...] = square.T[0:1, :]


def call(kernel, out_shapes, in_specs, scratch=(), flops=0, moved=0):
    shapes = [jax.ShapeDtypeStruct(shape, F32) for shape in out_shapes]
    return pl.pallas_call(
        kernel,
        out_shape=shapes,
        in_specs=in_specs,
        out_specs=[VMEM] * len(shapes),
        scratch_shapes=list(scratch),
        compiler_params=pltpu.CompilerParams(vmem_limit_bytes=40 * 2**20),
        cost_estimate=pl.CostEstimate(flops=flops, bytes_accessed=moved, transcendentals=0),
    )


def shards(d0, d1, d2, d3, b1, b2, b3):
    leaf = lax.axis_index("node") * 8 + lax.axis_index("lane")
    panel = lax.axis_index("panel")
    own = leaf * 4 + panel
    slots, first_table, second_table = [
        lax.dynamic_index_in_dim(jnp.asarray(table), own, 0, keepdims=False)
        for table in id_tables()
    ]
    base = jnp.stack(
        [leaf % 16 * 40 + panel * 10, leaf % 32 * 20 + panel * 5, leaf * 10]
    ).astype(jnp.int32)
    odd = (leaf // 16 % 2).astype(jnp.int32).reshape(1)

    x_chunk, y_chunk = call(
        pack_kernel,
        [(3 * Q, 128), (Q, 128)],
        [VMEM] * 6,
        [pltpu.VMEM((256, 256), F32)],
        moved=600000,
    )(d2, b2, b3, d1, b1, d0)

    x_parts = gather_x(x_chunk, permute, join_rows)
    others = [permute(y_chunk, step_y(count)) for count in (1, 2, 3)]
    (top_chunk,) = call(merge_kernel, [(Q, 128)], [SMEM] + [VMEM] * 4, moved=400000)(
        odd, y_chunk, *others
    )
    z_chunk = jnp.concatenate(
        [part[start : start + Q] for part in x_parts for start in (0, 3 * Q)], 0
    )
    third_parts = gather_z(z_chunk, permute, join_rows)
    third_parts = third_parts + [permute(part, SWAP) for part in third_parts]
    top_rows = functools.reduce(join_rows, gather_z(top_chunk, permute, join_rows))
    top_parts = gather_x(top_rows, permute, join_rows)
    top_parts = top_parts + [permute(part, SWAP) for part in top_parts]

    inverse = lax.all_gather(d3, "lane", axis=0, tiled=True)
    (mixed,) = call(
        bottom_kernel,
        [(8, 24, 256)],
        [SMEM, VMEM, HBM, HBM],
        [
            pltpu.VMEM((2, W, 128), F32),
            pltpu.VMEM((W, 256), F32),
            pltpu.SemaphoreType.DMA((8,)),
        ],
        flops=2 * 3 * W * 256 * 256,
        moved=2000000,
    )(slots, inverse, *x_parts)
    mixed = lax.all_to_all(mixed, "lane", 0, 0, tiled=True)
    mixed = permute(mixed, OWNER)

    stage = [pltpu.VMEM((16 * W, 128), F32), pltpu.SemaphoreType.DMA((64,))]
    path, squares = call(
        third_kernel,
        [(40, 2 * W), (40, 128)],
        [SMEM, SMEM, VMEM] + [HBM] * 8,
        stage,
        flops=2 * 6 * 40 * W * 16 * 128,
        moved=6000000,
    )(first_table, base, mixed, *third_parts)
    (variances,) = call(
        top_kernel,
        [(1, 128)],
        [SMEM, SMEM, VMEM, VMEM] + [HBM] * 4,
        stage,
        flops=2 * 9 * 48 * W * 16 * 128,
        moved=6000000,
    )(second_table, base, path, squares, *top_parts)
    gathered = lax.all_gather(variances, "panel", axis=0, tiled=True)
    return (
        variances[0, 48:58],
        gathered[:, 40:45].reshape(20),
        gathered[:, 24:34].reshape(40),
        gathered[:, 0:20].reshape(80),
    )


def solution(mesh):
    fine = Mesh(mesh.devices.reshape(8, 8, 4), ALL)
    rows = ("node", "lane")
    return jax.shard_map(
        shards,
        mesh=fine,
        in_specs=(P(rows, "panel"),) * 7,
        out_specs=(P(rows),) * 4,
        check_vma=False,
    )
```

time: 722 us -> 164 us (0.23)
  waiting for transfers between devices: 462 us -> 35.3 us
  matrix products: 64.6 us -> 0 us
  local copies, waits for them, and re-layouts: 43.7 us -> 15.9 us
  other arithmetic: 25.6 us -> 0.11 us
  Pallas kernels: 0 us -> 19.4 us
  between operations: 15.7 us -> 0.84 us
    ppermute x18 -> x22, waiting for transfers between devices: 444 us -> 35.3 us  [permute(): return lax.ppermute(value, ALL, pairs)]
    dot_general x11 -> x0, matrix products: 64.6 us -> none  [the longest x6 43 us: product(): jnp.dot(left_side, right_side, precision=lax.Precision.HIGHEST, preferred...]
    select_n x17 -> x0, other arithmetic: 23.2 us -> none  [leaf_doubling(): jnp.where(upper_bit == 1, jnp.concatenate([partner, block_rows], 0), jnp....]
    gather x3 -> x0, local copies, waits for them, and re-layouts: 21.4 us -> none  [shards(): variance = jnp.diagonal(gram_block)]
    pallas_call x0 -> x5, Pallas kernels: none -> 19.4 us  [the longest x1 10.1 us: shards(): call(top_kernel, [(1, 128)], [SMEM, SMEM, VMEM, VMEM] + [HBM] * 4, stage,...]
    all_gather x6 -> x0, waiting for transfers between devices: 17.2 us -> none  [the longest x2 17.2 us: shards(): mixed_block = lax.all_gather(mixed_cols, 'panel', axis=1, tiled=True)]
    all_to_all x0 -> x1, blocking collectives: none -> 11.7 us  [shards(): mixed = lax.all_to_all(mixed, 'lane', 0, 0, tiled=True)]
    unnamed x1 -> x0, blocking collectives: 10.8 us -> none
  transfers between devices with their start and end apart: 24 -> 22, of which waited for: 17 -> 12; matrix products, arithmetic and copies ran while one was open for 14% -> 4% of each run, Pallas kernels for 0% -> 6%
where the time goes in v1:
time: 164 us; the launch traced here: 161 us
  blocking collectives  53.6 us (33%)
  starting transfers between devices  36 us (22%)
  waiting for transfers between devices  35.3 us (22%)
  Pallas kernels  19.4 us (12%)
  local copies, waits for them, and re-layouts  15.9 us (10%)
    ppermute x22, starting transfers between devices, permute(): return lax.ppermute(value, ALL, pairs)  36 us
    ppermute x22, waiting for transfers between devices, permute(): return lax.ppermute(value, ALL, pairs)  35.3 us
    all_gather x1, blocking collectives, shards(): inverse = lax.all_gather(d3, 'lane', axis=0, tiled=True)  22 us
    all_gather x1, blocking collectives, shards(): gathered = lax.all_gather(variances, 'panel', axis=0, tiled=True)  20 us
    all_to_all x1, blocking collectives, shards(): mixed = lax.all_to_all(mixed, 'lane', 0, 0, tiled=True)  11.7 us
    pallas_call x1, Pallas kernels, shards(): call(top_kernel, [(1, 128)], [SMEM, SMEM, VMEM, VMEM] + [HBM] * 4, stage,...  10.1 us
    unnamed x27, local copies, waits for them, and re-layouts  8.57 us
    pallas_call x1, Pallas kernels, shards(): call(third_kernel, [(40, 2 * W), (40, 128)], [SMEM, SMEM, VMEM] + [HBM] *...  6.75 us
  transfers between devices with their start and end apart: 22, of which 12 were waited for; matrix products, arithmetic and copies ran while one was open for 4% of the time, Pallas kernels for 6%

profile of v1, /device:TPU:2, one launch (start us, length us, event | category | flops | bytes accessed | tf_op | source)
XLA Modules:
  0.0 161.2 jit_solution(5095019309438132819)
XLA Ops:
  0.6 1.0 copy.15.b3
  1.7 0.0 copy-start.4
  1.7 0.9 copy-done.4
  2.6 0.8 copy-done.5
  3.3 0.7 copy-done.6
  4.1 0.7 copy-done.7
  4.8 0.7 copy-done.8
  5.5 0.2 shard_map.129
  5.8 1.7 %collective-permute-start.11 = (f32[160,128]{1,0:T(8,128)S(1)}, f32[160,128]{1,0:T(8,128)S(1)}, u32[]{:S(2)}, u32[]{:S(2)}) collective-permute-start(f32[160,128]{1,0:T(8,128)S(1)} %get-tuple-element.11.own), channel_id=1, source_target_pairs={{0,64},{1,65},{2,66},{3,67},{4,68},{5,69},{6,70},{7,71},{8,72},{9,... | collective-permute-start | bytes 245768 | tf_op jit(solution)/shard_map/ppermute | solution.py:60
  7.4 2.9 %collective-permute-start.12 = (f32[160,128]{1,0:T(8,128)S(1)}, f32[160,128]{1,0:T(8,128)S(1)}, u32[]{:S(2)}, u32[]{:S(2)}) collective-permute-start(f32[160,128]{1,0:T(8,128)S(1)} %get-tuple-element.11.own), channel_id=1, source_target_pairs={{0,128},{1,129},{2,130},{3,131},{4,132},{5,133},{6,134},{7,135},{8... | collective-permute-start | bytes 245768 | tf_op jit(solution)/shard_map/ppermute | solution.py:60
  10.3 1.3 collective-permute-start.13
  11.7 0.5 collective-permute-start
  12.2 0.6 fusion.4
  12.9 1.4 collective-permute-done.12.two
  14.2 0.5 collective-permute-done.13.three
  14.7 0.2 shard_map.132
  15.0 2.0 %collective-permute-start.14 = (f32[160,128]{1,0:T(8,128)S(1)}, f32[160,128]{1,0:T(8,128)S(1)}, u32[]{:S(2)}, u32[]{:S(2)}) collective-permute-start(f32[160,128]{1,0:T(8,128)S(1)} %shard_map.132), channel_id=1, source_target_pairs={{0,8},{1,9},{2,10},{3,11},{4,60},{5,61},{6,62},{7,63},{8,0},{9,1},... | collective-permute-start | bytes 245768 | tf_op jit(solution)/shard_map/ppermute | solution.py:60
  17.0 2.5 %collective-permute-done.14 = f32[160,128]{1,0:T(8,128)S(1)} collective-permute-done((f32[160,128]{1,0:T(8,128)S(1)}, f32[160,128]{1,0:T(8,128)S(1)}, u32[]{:S(2)}, u32[]{:S(2)}) %collective-permute-start.14) | collective-permute-done | bytes 81952 | tf_op jit(solution)/shard_map/ppermute | solution.py:60
  19.5 5.9 %collective-permute-start.15 = (f32[320,128]{1,0:T(8,128)S(1)}, f32[320,128]{1,0:T(8,128)S(1)}, u32[]{:S(2)}, u32[]{:S(2)}) collective-permute-start(f32[320,128]{1,0:T(8,128)S(1)} %pad_maximum_fusion.1), channel_id=1, source_target_pairs={{0,56},{1,57},{2,58},{3,59},{4,12},{5,13},{6,14},{7,15},{8,16},{9,... | collective-permute-start | bytes 491528 | tf_op jit(solution)/shard_map/ppermute | solution.py:60
  25.5 1.6 collective-permute-start.1
  27.1 1.7 %collective-permute-done.15 = f32[320,128]{1,0:T(8,128)S(1)} collective-permute-done((f32[320,128]{1,0:T(8,128)S(1)}, f32[320,128]{1,0:T(8,128)S(1)}, u32[]{:S(2)}, u32[]{:S(2)}) %collective-permute-start.15) | collective-permute-done | bytes 163872 | tf_op jit(solution)/shard_map/ppermute | solution.py:60
  28.8 0.6 fusion.5
  29.4 5.5 %collective-permute-done.16 = f32[320,128]{1,0:T(8,128)S(1)} collective-permute-done((f32[320,128]{1,0:T(8,128)S(1)}, f32[320,128]{1,0:T(8,128)S(1)}, u32[]{:S(2)}, u32[]{:S(2)}) %collective-permute-start.16) | collective-permute-done | bytes 163872 | tf_op jit(solution)/shard_map/ppermute | solution.py:60
  34.9 3.6 %collective-permute-start.17 = (f32[320,128]{1,0:T(8,128)S(1)}, f32[320,128]{1,0:T(8,128)S(1)}, u32[]{:S(2)}, u32[]{:S(2)}) collective-permute-start(f32[320,128]{1,0:T(8,128)S(1)} %collective-permute-done.16), channel_id=1, source_target_pairs={{0,56},{1,57},{2,58},{3,59},{4,12},{5,13},{6,14},{7,15},{8,16},{9,... | collective-permute-start | bytes 491528 | tf_op jit(solution)/shard_map/ppermute | solution.py:60
  38.5 3.2 %collective-permute-done.17 = f32[320,128]{1,0:T(8,128)S(1)} collective-permute-done((f32[320,128]{1,0:T(8,128)S(1)}, f32[320,128]{1,0:T(8,128)S(1)}, u32[]{:S(2)}, u32[]{:S(2)}) %collective-permute-start.17) | collective-permute-done | bytes 163872 | tf_op jit(solution)/shard_map/ppermute | solution.py:60
  41.7 0.1 collective-permute-start.18
  41.8 0.7 fusion.3
  42.5 0.1 collective-permute-start.3
  42.6 0.6 constant_dynamic-update-slice_fusion.3
  43.3 7.3 %collective-permute-done.3 = f32[640,128]{1,0:T(8,128)S(1)} collective-permute-done((f32[640,128]{1,0:T(8,128)S(1)}, f32[640,128]{1,0:T(8,128)S(1)}, u32[]{:S(2)}, u32[]{:S(2)}) %collective-permute-start.3) | collective-permute-done | bytes 327712 | tf_op jit(solution)/shard_map/ppermute | solution.py:60
  50.6 0.8 constant_dynamic-update-slice_fusion.2.refs_0_
  51.3 3.5 %collective-permute-start.4 = (f32[1280,128]{1,0:T(8,128)}, f32[1280,128]{1,0:T(8,128)}, u32[]{:S(2)}, u32[]{:S(2)}) collective-permute-start(f32[1280,128]{1,0:T(8,128)} %constant_dynamic-update-slice_fusion.2.refs_0_), channel_id=1, source_target_pairs={{0,56},{1,57},{2,58},{3,59},{4,12},{5,13},{6,14},{7,15},{8,16},{9,... | collective-permute-start | bytes 1966088 | tf_op jit(solution)/shard_map/ppermute | solution.py:60
  54.9 1.2 collective-permute-done.18
  56.1 3.7 %collective-permute-start.19 = (f32[2560,128]{1,0:T(8,128)S(1)}, f32[2560,128]{1,0:T(8,128)S(1)}, u32[]{:S(2)}, u32[]{:S(2)}) collective-permute-start(f32[2560,128]{1,0:T(8,128)S(1)} %constant_dynamic-update-slice_fusion.12.refs_0_), channel_id=1, source_target_pairs={{0,3},{1,2},{2,1},{3,0},{4,5},{5,4},{6,7},{7,6},{8,11},{9,10},{10,... | collective-permute-start | bytes 3932168 | tf_op jit(solution)/shard_map/ppermute | solution.py:60
  59.8 6.2 %collective-permute-done.4.refs_1_ = f32[1280,128]{1,0:T(8,128)} collective-permute-done((f32[1280,128]{1,0:T(8,128)}, f32[1280,128]{1,0:T(8,128)}, u32[]{:S(2)}, u32[]{:S(2)}) %collective-permute-start.4) | collective-permute-done | bytes 655392 | tf_op jit(solution)/shard_map/ppermute | solution.py:60
  66.0 22.0 %all_gather.6.inverse = f32[640,160]{1,0:T(8,128)S(1)} all-gather(f32[80,160]{1,0:T(8,128)S(1)} %copy-done.9), channel_id=1, replica_groups=mesh['node'=8,'lane'=8,'panel'=4] {'lane'}, dimensions={0}, use_global_device_ids=true | all-gather | bytes 460800 | tf_op jit(solution)/shard_map/all_gather | solution.py:371
  88.0 0.3 collective-permute-start.7
  88.3 0.2 collective-permute-start.20
  88.5 3.3 %collective-permute-start.6 = (f32[1280,128]{1,0:T(8,128)}, f32[1280,128]{1,0:T(8,128)}, u32[]{:S(2)}, u32[]{:S(2)}) collective-permute-start(f32[1280,128]{1,0:T(8,128)} %collective-permute-done.5.refs_2_), channel_id=1, source_target_pairs={{0,56},{1,57},{2,58},{3,59},{4,12},{5,13},{6,14},{7,15},{8,16},{9,... | collective-permute-start | bytes 1966088 | tf_op jit(solution)/shard_map/ppermute | solution.py:60
  91.8 0.0 collective-permute-start.21
  91.8 0.7 fusion.2.slots
  92.5 1.0 copy-done.1
  93.5 2.2 %shard_map.130 = f32[8,24,256]{2,1,0:T(8,128)S(1)} custom-call(s32[4]{0:T(128)S(1)} %fusion.2.slots, f32[640,160]{1,0:T(8,128)S(1)} %all_gather.6.inverse, f32[960,128]{1,0:T(8,128)S(1)} %copy-done.1, f32[960,128]{1,0:T(8,128)S(1)} %collective-permute-done.1.other), custom_call_target="tpu_custom_call" | custom-call | flops 251658240 | bytes 2000000 | tf_op jit(solution)/shard_map/pallas_call | solution.py:372
  95.7 11.7 %all_to_all.5 = f32[8,24,256]{2,1,0:T(8,128)S(1)} all-to-all(f32[8,24,256]{2,1,0:T(8,128)S(1)} %shard_map.130), channel_id=1, replica_groups=mesh['node'=8,'lane'=8,'panel'=4] {'lane'}, dimensions={0} | all-to-all | bytes 393216 | tf_op jit(solution)/shard_map/all_to_all | solution.py:384
  107.4 4.7 %collective-permute-start.2 = (f32[8,24,256]{2,1,0:T(8,128)S(1)}, f32[8,24,256]{2,1,0:T(8,128)S(1)}, u32[]{:S(2)}, u32[]{:S(2)}) collective-permute-start(f32[8,24,256]{2,1,0:T(8,128)S(1)} %all_to_all.5), channel_id=1, source_target_pairs={{0,0},{1,8},{2,16},{3,24},{4,1},{5,9},{6,17},{7,25},{8,2},{9,10},{... | collective-permute-start | bytes 589832 | tf_op jit(solution)/shard_map/ppermute | solution.py:60
  112.1 4.3 %collective-permute-done.2.mixed = f32[8,24,256]{2,1,0:T(8,128)S(1)} collective-permute-done((f32[8,24,256]{2,1,0:T(8,128)S(1)}, f32[8,24,256]{2,1,0:T(8,128)S(1)}, u32[]{:S(2)}, u32[]{:S(2)}) %collective-permute-start.2) | collective-permute-done | bytes 196640 | tf_op jit(solution)/shard_map/ppermute | solution.py:60
  116.5 0.8 copy-done.2
  117.3 0.5 collective-permute-start.9
  117.8 0.0 collective-permute-start.10
  117.8 0.7 fusion.table
  118.5 0.7 fusion.1.table
  119.2 0.1 pad_add_fusion.base
  119.3 0.6 collective-permute-done.9.refs_6_
  119.9 0.9 collective-permute-done.10.refs_7_
  120.8 1.1 copy-done.3
  121.9 6.8 %shard_map.131 = (f32[40,1280]{1,0:T(8,128)S(1)}, f32[40,128]{1,0:T(8,128)S(1)}) custom-call(s32[64]{0:T(128)S(1)} %fusion.1.table, s32[3]{0:T(128)S(1)} %pad_add_fusion.base, f32[8,24,256]{2,1,0:T(8,128)S(1)} %collective-permute-done.2.mixed, f32[1280,128]{1,0:T(8,128)} %constant_dynamic-update-slice_fusion.2.refs_0_, ...), custom_call_target="tpu_custom_call" | custom-call | flops 629145600 | bytes 6000000 | tf_op jit(solution)/shard_map/pallas_call | solution.py:388
  128.7 10.1 %shard_map.133 = f32[1,128]{1,0:T(1,128)S(1)} custom-call(s32[64]{0:T(128)S(1)} %fusion.table, s32[3]{0:T(128)S(1)} %pad_add_fusion.base, f32[40,1280]{1,0:T(8,128)S(1)} %get-tuple-element.9.path, f32[40,128]{1,0:T(8,128)S(1)} %get-tuple-element.10.squares_in, f32[2560,128]{1,0:T(8,128)S(1)} %constant_dynamic-update-slice_fusion.12.refs_0_, ...), custom_call_target="tpu_custom_call" | custom-call | flops 1132462080 | bytes 6000000 | tf_op jit(solution)/shard_map/pallas_call | solution.py:396
  138.8 0.6 slice_bitcast_fusion
  139.3 20.0 %all-gather = f32[4,1,128]{2,1,0:T(1,128)S(1)} all-gather(f32[1,1,128]{2,1,0:T(1,128)S(1)} %bitcast.15), channel_id=1, replica_groups=mesh['node'=8,'lane'=8,'panel'=4] {'panel'}, dimensions={0}, use_global_device_ids=true | all-gather | bytes 2560 | tf_op jit(solution)/shard_map/all_gather | solution.py:404
  159.3 0.1 slice.29
  159.4 0.1 slice.30
  159.4 0.6 reshape.21
  160.0 0.6 reshape.22
  160.6 0.6 reshape.23
  (34 shorter events, 0.3 us)
Async XLA Ops:
  1.7 0.9 copy-start.4
  2.6 0.8 copy-start.5
  3.3 0.7 copy-start.6
  4.1 0.7 copy-start.7
  4.8 0.7 copy-start.8
  5.8 7.1 %collective-permute-start.11 = (f32[160,128]{1,0:T(8,128)S(1)}, f32[160,128]{1,0:T(8,128)S(1)}, u32[]{:S(2)}, u32[]{:S(2)}) collective-permute-start(f32[160,128]{1,0:T(8,128)S(1)} %get-tuple-element.11.own), channel_id=1, source_target_pairs={{0,64},{1,65},{2,66},{3,67},{4,68},{5,69},{6,70},{7,71},{8,72},{9,... | collective-permute-start | bytes 245768 | tf_op jit(solution)/shard_map/ppermute | solution.py:60
  7.4 6.8 %collective-permute-start.12 = (f32[160,128]{1,0:T(8,128)S(1)}, f32[160,128]{1,0:T(8,128)S(1)}, u32[]{:S(2)}, u32[]{:S(2)}) collective-permute-start(f32[160,128]{1,0:T(8,128)S(1)} %get-tuple-element.11.own), channel_id=1, source_target_pairs={{0,128},{1,129},{2,130},{3,131},{4,132},{5,133},{6,134},{7,135},{8... | collective-permute-start | bytes 245768 | tf_op jit(solution)/shard_map/ppermute | solution.py:60
  10.3 4.4 %collective-permute-start.13 = (f32[160,128]{1,0:T(8,128)S(1)}, f32[160,128]{1,0:T(8,128)S(1)}, u32[]{:S(2)}, u32[]{:S(2)}) collective-permute-start(f32[160,128]{1,0:T(8,128)S(1)} %get-tuple-element.11.own), channel_id=1, source_target_pairs={{0,192},{1,193},{2,194},{3,195},{4,196},{5,197},{6,198},{7,199},{8... | collective-permute-start | bytes 245768 | tf_op jit(solution)/shard_map/ppermute | solution.py:60
  11.7 13.8 %collective-permute-start = (f32[480,128]{1,0:T(8,128)S(1)}, f32[480,128]{1,0:T(8,128)S(1)}, u32[]{:S(2)}, u32[]{:S(2)}) collective-permute-start(f32[480,128]{1,0:T(8,128)S(1)} %get-tuple-element.8), channel_id=1, source_target_pairs={{0,1},{1,0},{2,3},{3,2},{4,7},{5,6},{6,5},{7,4},{8,9},{9,8},{10,11... | collective-permute-start | bytes 737288 | tf_op jit(solution)/shard_map/ppermute | solution.py:60
  15.0 4.5 %collective-permute-start.14 = (f32[160,128]{1,0:T(8,128)S(1)}, f32[160,128]{1,0:T(8,128)S(1)}, u32[]{:S(2)}, u32[]{:S(2)}) collective-permute-start(f32[160,128]{1,0:T(8,128)S(1)} %shard_map.132), channel_id=1, source_target_pairs={{0,8},{1,9},{2,10},{3,11},{4,60},{5,61},{6,62},{7,63},{8,0},{9,1},... | collective-permute-start | bytes 245768 | tf_op jit(solution)/shard_map/ppermute | solution.py:60
  19.5 9.2 %collective-permute-start.15 = (f32[320,128]{1,0:T(8,128)S(1)}, f32[320,128]{1,0:T(8,128)S(1)}, u32[]{:S(2)}, u32[]{:S(2)}) collective-permute-start(f32[320,128]{1,0:T(8,128)S(1)} %pad_maximum_fusion.1), channel_id=1, source_target_pairs={{0,56},{1,57},{2,58},{3,59},{4,12},{5,13},{6,14},{7,15},{8,16},{9,... | collective-permute-start | bytes 491528 | tf_op jit(solution)/shard_map/ppermute | solution.py:60
  25.5 17.0 %copy-start = (f32[960,128]{1,0:T(8,128)}, f32[960,128]{1,0:T(8,128)S(1)}, u32[]{:S(2)}) copy-start(f32[960,128]{1,0:T(8,128)S(1)} %constant_dynamic-update-slice_fusion.pair) | copy-start | bytes 1474564
  25.5 16.3 %collective-permute-start.1 = (f32[960,128]{1,0:T(8,128)S(1)}, f32[960,128]{1,0:T(8,128)S(1)}, u32[]{:S(2)}, u32[]{:S(2)}) collective-permute-start(f32[960,128]{1,0:T(8,128)S(1)} %constant_dynamic-update-slice_fusion.pair), channel_id=1, source_target_pairs={{0,3},{1,2},{2,1},{3,0},{4,5},{5,4},{6,7},{7,6},{8,11},{9,10},{10,... | collective-permute-start | bytes 1474568 | tf_op jit(solution)/shard_map/ppermute | solution.py:60
  28.8 6.1 %collective-permute-start.16 = (f32[320,128]{1,0:T(8,128)S(1)}, f32[320,128]{1,0:T(8,128)S(1)}, u32[]{:S(2)}, u32[]{:S(2)}) collective-permute-start(f32[320,128]{1,0:T(8,128)S(1)} %collective-permute-done.15), channel_id=1, source_target_pairs={{0,8},{1,9},{2,10},{3,11},{4,60},{5,61},{6,62},{7,63},{8,0},{9,1},... | collective-permute-start | bytes 491528 | tf_op jit(solution)/shard_map/ppermute | solution.py:60
  34.9 6.9 %collective-permute-start.17 = (f32[320,128]{1,0:T(8,128)S(1)}, f32[320,128]{1,0:T(8,128)S(1)}, u32[]{:S(2)}, u32[]{:S(2)}) collective-permute-start(f32[320,128]{1,0:T(8,128)S(1)} %collective-permute-done.16), channel_id=1, source_target_pairs={{0,56},{1,57},{2,58},{3,59},{4,12},{5,13},{6,14},{7,15},{8,16},{9,... | collective-permute-start | bytes 491528 | tf_op jit(solution)/shard_map/ppermute | solution.py:60
  41.7 14.3 %collective-permute-start.18 = (f32[1280,128]{1,0:T(8,128)S(1)}, f32[1280,128]{1,0:T(8,128)S(1)}, u32[]{:S(2)}, u32[]{:S(2)}) collective-permute-start(f32[1280,128]{1,0:T(8,128)S(1)} %get-tuple-element.19), channel_id=1, source_target_pairs={{0,1},{1,0},{2,3},{3,2},{4,7},{5,6},{6,5},{7,4},{8,9},{9,8},{10,11... | collective-permute-start | bytes 1966088 | tf_op jit(solution)/shard_map/ppermute | solution.py:60
  42.5 23.5 %copy-start.9 = (f32[80,160]{1,0:T(8,128)S(1)}, f32[80,160]{1,0:T(8,128)}, u32[]{:S(2)}) copy-start(f32[80,160]{1,0:T(8,128)} %param.13) | copy-start | bytes 153604
  42.5 8.1 %collective-permute-start.3 = (f32[640,128]{1,0:T(8,128)S(1)}, f32[640,128]{1,0:T(8,128)S(1)}, u32[]{:S(2)}, u32[]{:S(2)}) collective-permute-start(f32[640,128]{1,0:T(8,128)S(1)} %pad_maximum_fusion), channel_id=1, source_target_pairs={{0,8},{1,9},{2,10},{3,11},{4,60},{5,61},{6,62},{7,63},{8,0},{9,1},... | collective-permute-start | bytes 983048 | tf_op jit(solution)/shard_map/ppermute | solution.py:60
  51.3 14.7 %collective-permute-start.4 = (f32[1280,128]{1,0:T(8,128)}, f32[1280,128]{1,0:T(8,128)}, u32[]{:S(2)}, u32[]{:S(2)}) collective-permute-start(f32[1280,128]{1,0:T(8,128)} %constant_dynamic-update-slice_fusion.2.refs_0_), channel_id=1, source_target_pairs={{0,56},{1,57},{2,58},{3,59},{4,12},{5,13},{6,14},{7,15},{8,16},{9,... | collective-permute-start | bytes 1966088 | tf_op jit(solution)/shard_map/ppermute | solution.py:60
  56.1 35.7 %collective-permute-start.19 = (f32[2560,128]{1,0:T(8,128)S(1)}, f32[2560,128]{1,0:T(8,128)S(1)}, u32[]{:S(2)}, u32[]{:S(2)}) collective-permute-start(f32[2560,128]{1,0:T(8,128)S(1)} %constant_dynamic-update-slice_fusion.12.refs_0_), channel_id=1, source_target_pairs={{0,3},{1,2},{2,1},{3,0},{4,5},{5,4},{6,7},{7,6},{8,11},{9,10},{10,... | collective-permute-start | bytes 3932168 | tf_op jit(solution)/shard_map/ppermute | solution.py:60
  66.0 22.5 %collective-permute-start.5 = (f32[1280,128]{1,0:T(8,128)}, f32[1280,128]{1,0:T(8,128)}, u32[]{:S(2)}, u32[]{:S(2)}) collective-permute-start(f32[1280,128]{1,0:T(8,128)} %collective-permute-done.4.refs_1_), channel_id=1, source_target_pairs={{0,8},{1,9},{2,10},{3,11},{4,60},{5,61},{6,62},{7,63},{8,0},{9,1},... | collective-permute-start | bytes 1966088 | tf_op jit(solution)/shard_map/ppermute | solution.py:60
  88.0 28.5 %collective-permute-start.7 = (f32[1280,128]{1,0:T(8,128)}, f32[1280,128]{1,0:T(8,128)S(1)}, u32[]{:S(2)}, u32[]{:S(2)}) collective-permute-start(f32[1280,128]{1,0:T(8,128)} %constant_dynamic-update-slice_fusion.2.refs_0_), channel_id=1, source_target_pairs={{0,4},{1,5},{2,6},{3,7},{4,0},{5,1},{6,2},{7,3},{8,12},{9,13},{10,... | collective-permute-start | bytes 1966088 | tf_op jit(solution)/shard_map/ppermute | solution.py:60
  88.3 40.3 %collective-permute-start.20 = (f32[2560,128]{1,0:T(8,128)S(1)}, f32[2560,128]{1,0:T(8,128)}, u32[]{:S(2)}, u32[]{:S(2)}) collective-permute-start(f32[2560,128]{1,0:T(8,128)S(1)} %constant_dynamic-update-slice_fusion.12.refs_0_), channel_id=1, source_target_pairs={{0,4},{1,5},{2,6},{3,7},{4,0},{5,1},{6,2},{7,3},{8,12},{9,13},{10,... | collective-permute-start | bytes 3932168 | tf_op jit(solution)/shard_map/ppermute | solution.py:60
  88.5 29.3 %collective-permute-start.6 = (f32[1280,128]{1,0:T(8,128)}, f32[1280,128]{1,0:T(8,128)}, u32[]{:S(2)}, u32[]{:S(2)}) collective-permute-start(f32[1280,128]{1,0:T(8,128)} %collective-permute-done.5.refs_2_), channel_id=1, source_target_pairs={{0,56},{1,57},{2,58},{3,59},{4,12},{5,13},{6,14},{7,15},{8,16},{9,... | collective-permute-start | bytes 1966088 | tf_op jit(solution)/shard_map/ppermute | solution.py:60
  91.8 36.9 %collective-permute-start.21 = (f32[2560,128]{1,0:T(8,128)S(1)}, f32[2560,128]{1,0:T(8,128)}, u32[]{:S(2)}, u32[]{:S(2)}) collective-permute-start(f32[2560,128]{1,0:T(8,128)S(1)} %collective-permute-done.19.refs_1_), channel_id=1, source_target_pairs={{0,4},{1,5},{2,6},{3,7},{4,0},{5,1},{6,2},{7,3},{8,12},{9,13},{10,... | collective-permute-start | bytes 3932168 | tf_op jit(solution)/shard_map/ppermute | solution.py:60
  92.5 1.0 copy-start.1
  107.4 9.1 %collective-permute-start.2 = (f32[8,24,256]{2,1,0:T(8,128)S(1)}, f32[8,24,256]{2,1,0:T(8,128)S(1)}, u32[]{:S(2)}, u32[]{:S(2)}) collective-permute-start(f32[8,24,256]{2,1,0:T(8,128)S(1)} %all_to_all.5), channel_id=1, source_target_pairs={{0,0},{1,8},{2,16},{3,24},{4,1},{5,9},{6,17},{7,25},{8,2},{9,10},{... | collective-permute-start | bytes 589832 | tf_op jit(solution)/shard_map/ppermute | solution.py:60
  116.4 2.8 %collective-permute-start.8 = (f32[1280,128]{1,0:T(8,128)}, f32[1280,128]{1,0:T(8,128)S(1)}, u32[]{:S(2)}, u32[]{:S(2)}) collective-permute-start(f32[1280,128]{1,0:T(8,128)} %collective-permute-done.4.refs_1_), channel_id=1, source_target_pairs={{0,4},{1,5},{2,6},{3,7},{4,0},{5,1},{6,2},{7,3},{8,12},{9,13},{10,... | collective-permute-start | bytes 1966088 | tf_op jit(solution)/shard_map/ppermute | solution.py:60
  116.5 0.8 copy-start.2
  117.3 2.6 %collective-permute-start.9 = (f32[1280,128]{1,0:T(8,128)}, f32[1280,128]{1,0:T(8,128)}, u32[]{:S(2)}, u32[]{:S(2)}) collective-permute-start(f32[1280,128]{1,0:T(8,128)} %collective-permute-done.5.refs_2_), channel_id=1, source_target_pairs={{0,4},{1,5},{2,6},{3,7},{4,0},{5,1},{6,2},{7,3},{8,12},{9,13},{10,... | collective-permute-start | bytes 1966088 | tf_op jit(solution)/shard_map/ppermute | solution.py:60
  117.8 3.0 %collective-permute-start.10 = (f32[1280,128]{1,0:T(8,128)}, f32[1280,128]{1,0:T(8,128)}, u32[]{:S(2)}, u32[]{:S(2)}) collective-permute-start(f32[1280,128]{1,0:T(8,128)} %collective-permute-done.6.refs_3_), channel_id=1, source_target_pairs={{0,4},{1,5},{2,6},{3,7},{4,0},{5,1},{6,2},{7,3},{8,12},{9,13},{10,... | collective-permute-start | bytes 1966088 | tf_op jit(solution)/shard_map/ppermute | solution.py:60
  120.8 1.1 copy-start.3

commit v2 on v1

v2 whole, which is shorter than its diff:
```python
import jax
import jax.numpy as jnp
from jax import lax
from jax.experimental import pallas as pl
from jax.experimental.pallas import tpu as pltpu
from jax.sharding import Mesh
from jax.sharding import PartitionSpec as P

W = 640
Q = 160
ALL = ("row", "high", "deep", "core", "panel")
F32 = jnp.float32
VMEM = pl.BlockSpec(memory_space=pltpu.VMEM)
HBM = pl.BlockSpec(memory_space=pl.ANY)


def device(y, z, c, x):
    return ((y % 4 * 8 + z % 8) * 2 + c) * 4 + x % 4


def pairs_of(move):
    pairs = []
    for y in range(4):
        for z in range(8):
            for c in range(2):
                for x in range(4):
                    pairs.append((device(y, z, c, x), device(*move(y, z, c, x))))
    return pairs


def step_x(parity):
    return pairs_of(lambda y, z, c, x: (y, z, c, x + (1 if (x + c + parity) % 2 == 0 else -1)))


def step_z(parity):
    return pairs_of(lambda y, z, c, x: (y, z + (1 if (z + c + parity) % 2 == 0 else -1), c, x))


def step_y(count):
    return pairs_of(lambda y, z, c, x: (y + count, z, c, x))


def step_near(mask):
    return pairs_of(lambda y, z, c, x: (y, z ^ mask, c, x))


SWAP = pairs_of(lambda y, z, c, x: (y, z, 1 - c, x))


ORDER = (0, 1, -1, -2, 2, 3, -3, -4)


def join(first, second):
    return jnp.concatenate([first, second], 0)


def tie(value, *others):
    return lax.optimization_barrier((value, *others))[0]


def permute(value, pairs, name):
    with jax.named_scope(name):
        return lax.ppermute(value, ALL, pairs)


def here():
    depth = lax.axis_index("high") * 4 + lax.axis_index("deep")
    return lax.axis_index("row"), depth, lax.axis_index("core"), lax.axis_index("panel")


def turn(place, core):
    return 1 - 2 * ((place + core) & 1)


def third_rows(z, c, x):
    panels = [(x + turn(x, c) * step & 3) + c * 4 for step in (0, 1, -1, -2)]
    depths = [(z + turn(z, c) * step & 7) * 8 for step in ORDER]
    return [depth + panel for panel in panels for depth in depths]


def top_rows(z, c, x):
    panels = [(x + turn(x, c) * step & 3) + c * 4 for step in (0, 1, -1, -2)]
    depths = [(z + turn(z, c) * step & 7) * 8 for step in ORDER]
    return [depth + panel for depth in depths for panel in panels]


def split(value):
    high = value.astype(jnp.bfloat16)
    return high, (value - high.astype(F32)).astype(jnp.bfloat16)


def dot(left, right):
    return jnp.dot(left, right, preferred_element_type=F32)


def split_dot(left, right):
    rows = left.shape[0]
    left_high, left_low = split(left)
    right_high, right_low = split(right)
    both = dot(jnp.concatenate([left_high, left_low], 0), right_high)
    return both[:rows] + both[rows:] + dot(left_high, right_low)


def place(pieces, width):
    rows = pieces[0][0].shape[0]
    lane = lax.broadcasted_iota(jnp.int32, (rows, 128), 1)
    tiles = []
    for tile in range(width // 128):
        low = tile * 128
        total = jnp.zeros((rows, 128), F32)
        for value, source, length, target in pieces:
            start, stop = max(target, low), min(target + length, low + 128)
            if start >= stop:
                continue
            shift = (target - source) % 128
            moved = pltpu.roll(value, shift, 1) if shift else value
            inside = (lane >= start - low) & (lane < stop - low)
            total = jnp.where(inside, moved, total)
        tiles.append(total)
    return jnp.concatenate(tiles, 1)


def pack_kernel(d2, b2, b3, d3, d1, b1, d0, y_out, h_out, b_out, h2, g2, g3, h3, h1, g1, h0, rows, sems):
    copies = [
        pltpu.make_async_copy(source, target, sems.at[index])
        for index, (source, target) in enumerate(
            [(d1, h1), (b1, g1), (d0, h0), (d2, h2), (b2, g2), (b3, g3), (d3, h3)]
        )
    ]
    for copy in copies:
        copy.start()
    rows[...] = jnp.zeros(rows.shape, F32)
    b_out[...] = jnp.zeros(b_out.shape, F32)
    for copy in copies:
        copy.wait()
    rows[0:20, 0:Q] = h1[...]
    rows[20:40, 0:Q] = g1[...]
    rows[40:50, 0:Q] = h0[...]
    y_out[...] = rows[...].T[:Q]
    rows[0:40, 0:Q] = h2[...]
    rows[40:120, 0:Q] = g2[...]
    h_out[...] = rows[...].T[:Q]
    b_out[0:Q, :] = g3[:, 0:128]
    b_out[Q : 2 * Q, 0:112] = g3[:, 128:240]
    rows[0:80, 0:Q] = h3[...]
    rows[80:128, :] = jnp.zeros((48, 256), F32)
    turned = rows[...].T[:Q]
    for panel in range(4):
        for half in range(2):
            target = 2 * Q + panel * 40 + half * 20
            source = half * 80 + panel * 20
            b_out[target : target + 20, :] = turned[source : source + 20]


def merge_kernel(own, one, two, three, out):
    lane = lax.broadcasted_iota(jnp.int32, (Q, 128), 1)
    is_odd = here()[0] & 1 == 1
    lower = jnp.where(is_odd, one[...], own[...])
    upper = jnp.where(is_odd, own[...], three[...])
    total = jnp.zeros((Q, 128), F32)
    for value, shift, start, stop in (
        (lower, 0, 0, 20),
        (upper, 20, 20, 40),
        (lower, 20, 40, 60),
        (upper, 40, 60, 80),
        (own[...], 40, 80, 90),
        (one[...], 50, 90, 100),
        (two[...], 60, 100, 110),
        (three[...], 70, 110, 120),
    ):
        moved = pltpu.roll(value, shift, 1) if shift else value
        total = jnp.where((lane >= start) & (lane < stop), moved, total)
    out[...] = total


def b_panels():
    _, _, c, x = here()
    return [x + turn(x, c) * ORDER[slot] & 3 for slot in range(4)]


def run(copies, sems):
    copies = [
        pltpu.make_async_copy(source, target, sems.at[index])
        for index, (source, target) in enumerate(copies)
    ]
    for copy in copies:
        copy.start()
    for copy in copies:
        copy.wait()


def pick_kernel(pair, last, out, sems):
    _, _, _, x = here()
    copies = []
    for slot, panel in enumerate(b_panels()):
        source = pair if slot < 2 else last
        start = pl.multiple_of(slot % 2 * 3 * Q + 2 * Q + x * 40, 8)
        target = pl.multiple_of(panel * 40, 8)
        copies.append((source.at[pl.ds(start, 40), :], out.at[pl.ds(target, 40), :]))
    run(copies, sems)


def bottom_kernel(near, near_other, pair, last, out, below, inverse, sems):
    _, z, c, x = here()
    copies = []
    for slot, panel in enumerate(b_panels()):
        source = pair if slot < 2 else last
        column = pl.multiple_of(panel * Q, Q)
        for half in range(2):
            start = slot % 2 * 3 * Q + half * Q
            copies.append((source.at[pl.ds(start, Q), :], below.at[half, pl.ds(column, Q), :]))
    for core, source in enumerate((near, near_other)):
        for slot in range(4):
            lane = (z & 3 ^ slot) * 2 + (c ^ core)
            copies.append((source.at[pl.ds(slot * Q, Q), :], inverse.at[lane]))
    run(copies, sems)
    squares = jnp.zeros((Q, 128), F32)
    mixed = jnp.zeros((Q, 256), F32)
    for lane in range(8):
        part = inverse[lane]
        squares = squares + part * part
        rows = slice(lane * 80, lane * 80 + 80)
        mixed = mixed + split_dot(
            part[:, :80], jnp.concatenate([below[0, rows, :], below[1, rows, :]], 1)
        )
    squares = jnp.sum(squares, 1, keepdims=True)
    lane = lax.broadcasted_iota(jnp.int32, (Q, 256), 1)
    mixed = jnp.where(lane == 240, squares, mixed)
    out[...] = jnp.zeros(out.shape, F32)
    for part in range(8):
        out[part, 0:20, :] = mixed[part * 20 : part * 20 + 20]


def start_copies(sources, rows, stage, sems):
    each = 64 // len(sources)
    copies = []
    for number, row in enumerate(rows):
        source, atom = sources[number // each], number % each
        row = pl.multiple_of(row * Q, Q)
        copies.append(
            pltpu.make_async_copy(
                source.at[pl.ds(atom * Q, Q), :], stage.at[pl.ds(row, Q), :], sems.at[number]
            )
        )
    for copy in copies:
        copy.start()
    return copies


def split_stage(stage, high, low):
    for z in range(8):
        for core in range(2):
            rows = slice((2 * z + core) * W, (2 * z + core + 1) * W)
            lanes = slice(core * 128, core * 128 + 128)
            high[z, :, lanes], low[z, :, lanes] = split(stage[rows, :])


def halves(left):
    left_high, left_low = split(left)
    return left_high, jnp.concatenate([left_high, left_low], 0)


def half_dot(left, high, low):
    left_high, left_both = left
    rows = left_high.shape[0]
    both = dot(left_both, high)
    return both[:rows] + both[rows:] + dot(left_high, low)


def one_hot(rows, count, base):
    row = lax.broadcasted_iota(jnp.int32, (rows, W), 0)
    lane = lax.broadcasted_iota(jnp.int32, (rows, W), 1)
    return jnp.where((row < count) & (lane == base + row), 1.0, 0.0).astype(F32)


def chain_kernel(mixed, *refs):
    first, second, third, last = refs[8:12]
    h_parts = [(second, 1), (third, 1), (third, 2), (last, 1)]
    t_parts = [(first, 0), (second, 0), (third, 0), (last, 0)]
    rows = 8 * Q
    third = refs[:4] + tuple(swap.at[pl.ds(part * rows, rows), :] for swap, part in h_parts)
    top = refs[4:8] + tuple(swap.at[pl.ds(part * rows, rows), :] for swap, part in t_parts)
    out, third_stage, top_stage, high, low, third_sems, top_sems = refs[12:]
    y, z, c, x = here()
    leaf = z * 2 + c
    third_copies = start_copies(
        third, third_rows(z, c, x) + third_rows(z, 1 - c, x), third_stage, third_sems
    )
    top_copies = start_copies(
        top, top_rows(z, c, x) + top_rows(z, 1 - c, x), top_stage, top_sems
    )
    pieces = []
    for part in range(8):
        pieces.append((mixed[part, :, 0:128], 0, 128, part * 240))
        pieces.append((mixed[part, :, 128:256], 0, 112, part * 240 + 128))
    path = place(pieces, 3 * W)
    squares = jnp.concatenate([mixed[0, :, 240:241], jnp.zeros((40, 1), F32)], 0)

    def products(cols):
        left = halves(cols)
        for z in range(8):
            product = half_dot(left, high[z], low[z])
            for core in range(2):
                yield z, core, product[:, core * 128 : core * 128 + 128]

    for copy in third_copies:
        copy.wait()
    split_stage(third_stage, high, low)
    cols = jnp.concatenate([path[:, 2 * W :], one_hot(16, 10, leaf * 40 + x * 10)], 0)
    pieces = [(part, 0, 40, z * 80 + core * 40) for z, core, part in products(cols)]
    cols = place(pieces, W)
    squares = squares + jnp.concatenate(
        [jnp.sum(cols * cols, 1, keepdims=True), jnp.zeros((24, 1), F32)], 0
    )
    pieces = [(part, 40, 80, z * 160 + core * 80) for z, core, part in products(cols)]
    change = place(pieces, 2 * W)
    path = jnp.concatenate([path[:, : 2 * W] - change[0:24], -change[24:40]], 0)

    for copy in top_copies:
        copy.wait()
    split_stage(top_stage, high, low)
    cols = jnp.concatenate([path[:, W:], one_hot(8, 5, ((y & 1) * 16 + leaf) * 20 + x * 5)], 0)
    pieces = [
        (part, half * 20, 20, half * 320 + z * 40 + core * 20)
        for z, core, part in products(cols)
        for half in range(2)
    ]
    cols = place(pieces, W)
    squares = squares + jnp.concatenate(
        [jnp.sum(cols * cols, 1, keepdims=True), jnp.zeros((16, 1), F32)], 0
    )
    pieces = [
        (part, 40 + half * 20, 20, half * 320 + z * 40 + core * 20)
        for z, core, part in products(cols)
        for half in range(2)
    ]
    change = place(pieces, W)
    cols = jnp.concatenate(
        [path[:, :W] - change[0:40], -change[40:48], one_hot(16, 10, (y * 16 + leaf) * 10)], 0
    )
    lane = lax.broadcasted_iota(jnp.int32, (64, 128), 1)
    total = jnp.zeros((64, 128), F32)
    for _, _, part in products(cols):
        total = total + part * part
    total = jnp.where((lane >= 80) & (lane < 120), total, 0.0)
    squares = squares + jnp.sum(total, 1, keepdims=True)
    square = jnp.concatenate(
        [jnp.broadcast_to(squares, (64, 128)), jnp.zeros((64, 128), F32)], 0
    )
    out[...] = square.T[0:1, :]


def finish_kernel(own, gathered, *outs):
    for out, start, count in zip(outs, (48, 40, 24, 0), (10, 5, 10, 20)):
        if start == 48:
            out[...] = own[0:1, start : start + count]
            continue
        parts = []
        for panel in range(4):
            row = jnp.broadcast_to(gathered[panel : panel + 1, :], (8, 128))
            parts.append((row, start, count, panel * count))
        out[...] = place(parts, 128)[0:1, : 4 * count]


def call(kernel, out_shapes, in_specs, scratch=(), limit=24):
    shapes = [jax.ShapeDtypeStruct(shape, F32) for shape in out_shapes]
    return pl.pallas_call(
        kernel,
        out_shape=shapes,
        in_specs=in_specs,
        out_specs=[VMEM] * len(shapes),
        scratch_shapes=list(scratch),
        compiler_params=pltpu.CompilerParams(vmem_limit_bytes=limit * 2**20),
        cost_estimate=pl.CostEstimate(flops=0, bytes_accessed=0, transcendentals=0),
    )


def shards(d0, d1, d2, d3, b1, b2, b3):
    b3 = b3.T
    y_chunk, h_chunk, b_chunk = call(
        pack_kernel,
        [(Q, 128), (Q, 128), (3 * Q, 128)],
        [HBM] * 7,
        [pltpu.VMEM(value.shape, F32) for value in (d2, b2, b3, d3, d1, b1, d0)]
        + [pltpu.VMEM((128, 256), F32), pltpu.SemaphoreType.DMA((7,))],
        limit=60,
    )(d2, b2, b3, d3, d1, b1, d0)

    def send(name, pairs, value):
        return permute(value, pairs, name)

    def together(*values):
        return lax.optimization_barrier(values)

    y1 = send("y1", step_y(1), y_chunk)
    y3 = send("y3", step_y(3), y_chunk)
    y2 = send("y2", step_y(2), y_chunk)
    hz = send("hz0", step_z(0), h_chunk)
    bx = send("bx0", step_x(0), b_chunk)
    y1, y2, y3, hz, bx = together(y1, y2, y3, hz, bx)
    (t_chunk,) = call(merge_kernel, [(Q, 128)], [VMEM] * 4)(y_chunk, y1, y2, y3)
    h_pair, b_pair = join(h_chunk, hz), join(b_chunk, bx)
    t_chunk, h_pair, b_pair = together(t_chunk, h_pair, b_pair)

    tx = send("tx0", step_x(0), t_chunk)
    h1 = send("hz1", step_z(1), h_pair)
    b_last = send("bx1", step_x(1), b_pair)
    tx, h1, b_last = together(tx, h1, b_last)
    t_pair = join(t_chunk, tx)
    (near,) = call(
        pick_kernel, [(Q, 128)], [HBM] * 2, [pltpu.SemaphoreType.DMA((4,))]
    )(b_pair, b_last)
    t_pair, h1, near = together(t_pair, h1, near)

    tx = send("tx1", step_x(1), t_pair)
    h2 = send("hz2", step_z(0), h1)
    got = send("near1", step_near(1), near)
    tx, h2, got = together(tx, h2, got)
    t_line, near = join(t_pair, tx), join(near, got)
    t_line, near, h2 = together(t_line, near, h2)

    tz = send("tz0", step_z(0), t_line)
    h3 = send("hz3", step_z(1), h2)
    got = send("near2", step_near(2), near)
    tz, h3, got = together(tz, h3, got)
    t0, near = join(t_line, tz), join(near, got)
    h_rows = jnp.concatenate([h_pair, h1, h2, h3], 0)
    t0, h_rows, near = together(t0, h_rows, near)

    t1 = send("tz1", step_z(1), t0)
    hx = send("hx0", step_x(0), h_rows)
    near_other = send("near_swap", SWAP, near)
    swap0 = send("swap0", SWAP, t0)
    t1, hx, near_other, swap0, h_rows = together(t1, hx, near_other, swap0, h_rows)

    t2 = send("tz2", step_z(0), t1)
    h1 = send("hx1", step_x(1), h_rows)
    swap1 = send("swap1", SWAP, join(t1, h_rows))
    (mixed,) = call(
        bottom_kernel,
        [(8, 24, 256)],
        [HBM] * 4,
        [
            pltpu.VMEM((2, W, 128), F32),
            pltpu.VMEM((8, Q, 128), F32),
            pltpu.SemaphoreType.DMA((16,)),
        ],
    )(near, near_other, b_pair, b_last)
    t2, h1, swap1, mixed, hx = together(t2, h1, swap1, mixed, hx)

    t3 = send("tz3", step_z(1), t2)
    h2 = send("hx2", step_x(1), hx)
    swap2 = send("swap2", SWAP, jnp.concatenate([t2, hx, h1], 0))
    mixed = lax.all_to_all(mixed, ("deep", "core"), 0, 0, tiled=True)
    t3, h2, mixed, swap2 = together(t3, h2, mixed, swap2)

    swap3 = send("swap3", SWAP, join(t3, h2))

    (variances,) = call(
        chain_kernel,
        [(1, 128)],
        [VMEM] + [HBM] * 12,
        [
            pltpu.VMEM((16 * W, 128), F32),
            pltpu.VMEM((16 * W, 128), F32),
            pltpu.VMEM((8, W, 256), jnp.bfloat16),
            pltpu.VMEM((8, W, 256), jnp.bfloat16),
            pltpu.SemaphoreType.DMA((64,)),
            pltpu.SemaphoreType.DMA((64,)),
        ],
        limit=60,
    )(mixed, h_rows, hx, h1, h2, t0, t1, t2, t3, swap0, swap1, swap2, swap3)
    gathered = lax.all_gather(variances, "panel", axis=0, tiled=True)
    outs = call(finish_kernel, [(1, 10), (1, 20), (1, 40), (1, 80)], [VMEM] * 2)(
        variances, gathered
    )
    return tuple(out.reshape(out.shape[1]) for out in outs)


def solution(mesh):
    fine = Mesh(mesh.devices.reshape(4, 2, 4, 2, 4), ALL)
    rows = ALL[:4]
    return jax.shard_map(
        shards,
        mesh=fine,
        in_specs=(P(rows, "panel"),) * 7,
        out_specs=(P(rows),) * 4,
        check_vma=False,
    )
```

time: 164 us -> 123 us (0.75); the launches traced: 161 us -> 122 us
  blocking collectives: 53.6 us -> 20.3 us
  local copies, waits for them, and re-layouts: 15.9 us -> 3.95 us
  waiting for transfers between devices: 35.3 us -> 42.5 us
  starting transfers between devices: 36 us -> 33.5 us
  other arithmetic: 0.11 us -> 2.33 us
    all_gather x1 -> x0, blocking collectives: 22 us -> none  [shards(): inverse = lax.all_gather(d3, 'lane', axis=0, tiled=True)]
    all_gather x1, blocking collectives: 20 us -> 8.86 us  [shards(): gathered = lax.all_gather(variances, 'panel', axis=0, tiled=True)]
    ppermute x22 -> x25, waiting for transfers between devices: 35.3 us -> 42.5 us  [permute(): return lax.ppermute(value, ALL, pairs)]
    unnamed x27 -> x26, local copies, waits for them, and re-layouts: 8.57 us -> 3.95 us
    squeeze x4 -> x0, local copies, waits for them, and re-layouts: 2.66 us -> none  [the longest x3 2.07 us: shards(): lax.dynamic_index_in_dim(jnp.asarray(table), own, 0, keepdims=False)]
    ppermute x22 -> x25, starting transfers between devices: 36 us -> 33.5 us  [permute(): return lax.ppermute(value, ALL, pairs)]
    concatenate x2 -> x10, other arithmetic: 0.03 us -> 2.33 us  [the longest x9 2.21 us: join(): return jnp.concatenate([first, second], 0)]
    slice x5 -> x0, local copies, waits for them, and re-layouts: 2.06 us -> none  [the longest x3 1.92 us: shards(): part[start:start + Q]]
  transfers between devices with their start and end apart: 22 -> 25, of which waited for: 12 -> 13; matrix products, arithmetic and copies ran while one was open for 4% -> 0% of each run, Pallas kernels for 6% -> 2%
where the time goes in v2:
time: 123 us; the launch traced here: 122 us
  waiting for transfers between devices  42.5 us (35%)
  starting transfers between devices  33.5 us (27%)
  blocking collectives  20.3 us (17%)
  Pallas kernels  18.7 us (15%)
  local copies, waits for them, and re-layouts  3.95 us (3%)
  other arithmetic  2.33 us (2%)
    ppermute x25, waiting for transfers between devices, permute(): return lax.ppermute(value, ALL, pairs)  42.5 us
    ppermute x25, starting transfers between devices, permute(): return lax.ppermute(value, ALL, pairs)  33.5 us
    pallas_call x1, Pallas kernels, shards(): call(chain_kernel, [(1, 128)], [VMEM] + [HBM] * 12, [pltpu.VMEM((16 * W,...  13.2 us
    all_to_all x1, blocking collectives, shards(): mixed = lax.all_to_all(mixed, ('deep', 'core'), 0, 0, tiled=True)  11.4 us
    all_gather x1, blocking collectives, shards(): gathered = lax.all_gather(variances, 'panel', axis=0, tiled=True)  8.86 us
    unnamed x26, local copies, waits for them, and re-layouts  3.95 us
    pallas_call x1, Pallas kernels, shards(): call(bottom_kernel, [(8, 24, 256)], [HBM] * 4, [pltpu.VMEM((2, W, 128), F...  2.5 us
  transfers between devices with their start and end apart: 25, of which 13 were waited for; matrix products, arithmetic and copies ran while one was open for 0% of the time, Pallas kernels for 2%

profile of v2, /device:TPU:2, one launch (start us, length us, event | category | flops | bytes accessed | tf_op | source)
XLA Modules:
  0.0 122.1 jit_solution(4526290342911728576)
XLA Ops:
  0.6 2.0 %shard_map.102 = (f32[160,128]{1,0:T(8,128)}, f32[160,128]{1,0:T(8,128)}, f32[480,128]{1,0:T(8,128)}) custom-call(f32[40,160]{1,0:T(8,128)} %d2.1, f32[80,160]{1,0:T(8,128)} %b2.1, f32[160,240]{1,0:T(8,128)} %bitcast.9, f32[80,160]{1,0:T(8,128)} %d3.1, f32[20,160]{1,0:T(8,128)} %d1.1, f32[20,160]{1,0:T(8,128)} %b1.1, f32[10,160]{1,0:T(8,128)} %d0.1), custom_call_target="tpu_custom_call" | custom-call | tf_op jit(solution)/shard_map/pallas_call | solution.py:380
  2.7 2.4 %collective-permute-start.4 = (f32[480,128]{1,0:T(8,128)}, f32[480,128]{1,0:T(8,128)S(1)}, u32[]{:S(2)}, u32[]{:S(2)}) collective-permute-start(f32[480,128]{1,0:T(8,128)} %get-tuple-element.53), channel_id=1, source_target_pairs={{0,1},{1,0},{2,3},{3,2},{4,7},{5,6},{6,5},{7,4},{8,9},{9,8},{10,11... | collective-permute-start | bytes 737288 | tf_op jit(solution)/shard_map/bx0/ppermute | solution.py:63
  5.0 0.2 collective-permute-start.3
  5.2 3.0 %collective-permute-start.2 = (f32[160,128]{1,0:T(8,128)}, f32[160,128]{1,0:T(8,128)S(1)}, u32[]{:S(2)}, u32[]{:S(2)}) collective-permute-start(f32[160,128]{1,0:T(8,128)} %get-tuple-element.51.own), channel_id=1, source_target_pairs={{0,192},{1,193},{2,194},{3,195},{4,196},{5,197},{6,198},{7,199},{8... | collective-permute-start | bytes 245768 | tf_op jit(solution)/shard_map/y3/ppermute | solution.py:63
  8.2 0.6 collective-permute-start.1
  8.8 1.0 collective-permute-start
  9.8 0.0 collective-permute-done.3
  9.8 0.8 collective-permute-done.2.three
  10.6 3.8 %collective-permute-done.1.two = f32[160,128]{1,0:T(8,128)S(1)} collective-permute-done((f32[160,128]{1,0:T(8,128)}, f32[160,128]{1,0:T(8,128)S(1)}, u32[]{:S(2)}, u32[]{:S(2)}) %collective-permute-start.1) | collective-permute-done | bytes 81952 | tf_op jit(solution)/shard_map/y2/ppermute | solution.py:63
  14.4 0.8 collective-permute-done.one
  15.3 0.0 collective-permute-done.4
  15.3 0.9 pad_maximum_fusion.8
  16.2 1.0 pad_maximum_fusion.5.pair
  17.1 0.2 shard_map.103
  17.4 3.5 %collective-permute-start.7 = (f32[960,128]{1,0:T(8,128)S(1)}, f32[960,128]{1,0:T(8,128)S(1)}, u32[]{:S(2)}, u32[]{:S(2)}) collective-permute-start(f32[960,128]{1,0:T(8,128)S(1)} %pad_maximum_fusion.5.pair), channel_id=1, source_target_pairs={{0,3},{1,2},{2,1},{3,0},{4,5},{5,4},{6,7},{7,6},{8,11},{9,10},{10,... | collective-permute-start | bytes 1474568 | tf_op jit(solution)/shard_map/bx1/ppermute | solution.py:63
  20.9 3.7 %collective-permute-start.6 = (f32[320,128]{1,0:T(8,128)S(1)}, f32[320,128]{1,0:T(8,128)S(1)}, u32[]{:S(2)}, u32[]{:S(2)}) collective-permute-start(f32[320,128]{1,0:T(8,128)S(1)} %pad_maximum_fusion.8), channel_id=1, source_target_pairs={{0,56},{1,57},{2,58},{3,59},{4,12},{5,13},{6,14},{7,15},{8,16},{9,... | collective-permute-start | bytes 491528 | tf_op jit(solution)/shard_map/hz1/ppermute | solution.py:63
  24.6 1.4 %collective-permute-start.5 = (f32[160,128]{1,0:T(8,128)S(1)}, f32[160,128]{1,0:T(8,128)S(1)}, u32[]{:S(2)}, u32[]{:S(2)}) collective-permute-start(f32[160,128]{1,0:T(8,128)S(1)} %shard_map.103), channel_id=1, source_target_pairs={{0,1},{1,0},{2,3},{3,2},{4,7},{5,6},{6,5},{7,4},{8,9},{9,8},{10,11... | collective-permute-start | bytes 245768 | tf_op jit(solution)/shard_map/tx0/ppermute | solution.py:63
  26.0 3.0 %collective-permute-done.5 = f32[160,128]{1,0:T(8,128)S(1)} collective-permute-done((f32[160,128]{1,0:T(8,128)S(1)}, f32[160,128]{1,0:T(8,128)S(1)}, u32[]{:S(2)}, u32[]{:S(2)}) %collective-permute-start.5) | collective-permute-done | bytes 81952 | tf_op jit(solution)/shard_map/tx0/ppermute | solution.py:63
  29.0 0.0 collective-permute-done.6
  29.0 0.0 collective-permute-done.7.last
  29.0 0.2 shard_map.104
  29.2 1.7 %collective-permute-start.8 = (f32[320,128]{1,0:T(8,128)S(1)}, f32[320,128]{1,0:T(8,128)S(1)}, u32[]{:S(2)}, u32[]{:S(2)}) collective-permute-start(f32[320,128]{1,0:T(8,128)S(1)} %pad_maximum_fusion.9), channel_id=1, source_target_pairs={{0,3},{1,2},{2,1},{3,0},{4,5},{5,4},{6,7},{7,6},{8,11},{9,10},{10,... | collective-permute-start | bytes 491528 | tf_op jit(solution)/shard_map/tx1/ppermute | solution.py:63
  30.9 0.0 collective-permute-start.9
  30.9 2.0 %collective-permute-start.10 = (f32[160,128]{1,0:T(8,128)S(1)}, f32[160,128]{1,0:T(8,128)S(1)}, u32[]{:S(2)}, u32[]{:S(2)}) collective-permute-start(f32[160,128]{1,0:T(8,128)S(1)} %shard_map.104), channel_id=1, source_target_pairs={{0,8},{1,9},{2,10},{3,11},{4,12},{5,13},{6,14},{7,15},{8,0},{9,1},... | collective-permute-start | bytes 245768 | tf_op jit(solution)/shard_map/near1/ppermute | solution.py:63
  32.9 5.0 %collective-permute-done.10 = f32[160,128]{1,0:T(8,128)S(1)} collective-permute-done((f32[160,128]{1,0:T(8,128)S(1)}, f32[160,128]{1,0:T(8,128)S(1)}, u32[]{:S(2)}, u32[]{:S(2)}) %collective-permute-start.10) | collective-permute-done | bytes 81952 | tf_op jit(solution)/shard_map/near1/ppermute | solution.py:63
  38.0 0.0 collective-permute-done.8
  38.0 0.0 collective-permute-done.9
  38.0 0.1 collective-permute-start.11
  38.1 3.7 %collective-permute-start.12 = (f32[320,128]{1,0:T(8,128)S(1)}, f32[320,128]{1,0:T(8,128)S(1)}, u32[]{:S(2)}, u32[]{:S(2)}) collective-permute-start(f32[320,128]{1,0:T(8,128)S(1)} %collective-permute-done.9), channel_id=1, source_target_pairs={{0,56},{1,57},{2,58},{3,59},{4,12},{5,13},{6,14},{7,15},{8,16},{9,... | collective-permute-start | bytes 491528 | tf_op jit(solution)/shard_map/hz3/ppermute | solution.py:63
  41.8 3.8 %collective-permute-done.12 = f32[320,128]{1,0:T(8,128)S(1)} collective-permute-done((f32[320,128]{1,0:T(8,128)S(1)}, f32[320,128]{1,0:T(8,128)S(1)}, u32[]{:S(2)}, u32[]{:S(2)}) %collective-permute-start.12) | collective-permute-done | bytes 163872 | tf_op jit(solution)/shard_map/hz3/ppermute | solution.py:63
  45.6 5.4 %collective-permute-done.13 = f32[320,128]{1,0:T(8,128)S(1)} collective-permute-done((f32[320,128]{1,0:T(8,128)S(1)}, f32[320,128]{1,0:T(8,128)S(1)}, u32[]{:S(2)}, u32[]{:S(2)}) %collective-permute-start.13) | collective-permute-done | bytes 163872 | tf_op jit(solution)/shard_map/near2/ppermute | solution.py:63
  51.1 0.1 pad_maximum_fusion.3
  51.2 1.7 %collective-permute-start.15 = (f32[1280,128]{1,0:T(8,128)S(1)}, f32[1280,128]{1,0:T(8,128)S(1)}, u32[]{:S(2)}, u32[]{:S(2)}) collective-permute-start(f32[1280,128]{1,0:T(8,128)S(1)} %get-tuple-element.81.refs_0_), channel_id=1, source_target_pairs={{0,1},{1,0},{2,3},{3,2},{4,7},{5,6},{6,5},{7,4},{8,9},{9,8},{10,11... | collective-permute-start | bytes 1966088 | tf_op jit(solution)/shard_map/hx0/ppermute | solution.py:63
  53.0 1.6 %collective-permute-start.14 = (f32[1280,128]{1,0:T(8,128)S(1)}, f32[1280,128]{1,0:T(8,128)S(1)}, u32[]{:S(2)}, u32[]{:S(2)}) collective-permute-start(f32[1280,128]{1,0:T(8,128)S(1)} %get-tuple-element.77.refs_4_), channel_id=1, source_target_pairs={{0,56},{1,57},{2,58},{3,59},{4,12},{5,13},{6,14},{7,15},{8,16},{9,... | collective-permute-start | bytes 1966088 | tf_op jit(solution)/shard_map/tz1/ppermute | solution.py:63
  54.6 1.6 %collective-permute-done.16.near_other = f32[640,128]{1,0:T(8,128)S(1)} collective-permute-done((f32[640,128]{1,0:T(8,128)S(1)}, f32[640,128]{1,0:T(8,128)S(1)}, u32[]{:S(2)}, u32[]{:S(2)}) %collective-permute-start.16) | collective-permute-done | bytes 327712 | tf_op jit(solution)/shard_map/near_swap/ppermute | solution.py:63
  56.2 5.7 %collective-permute-done.15.refs_1_ = f32[1280,128]{1,0:T(8,128)S(1)} collective-permute-done((f32[1280,128]{1,0:T(8,128)S(1)}, f32[1280,128]{1,0:T(8,128)S(1)}, u32[]{:S(2)}, u32[]{:S(2)}) %collective-permute-start.15) | collective-permute-done | bytes 655392 | tf_op jit(solution)/shard_map/hx0/ppermute | solution.py:63
  61.9 0.0 collective-permute-done.17.refs_8_
  61.9 2.9 %collective-permute-done.14.refs_5_ = f32[1280,128]{1,0:T(8,128)S(1)} collective-permute-done((f32[1280,128]{1,0:T(8,128)S(1)}, f32[1280,128]{1,0:T(8,128)S(1)}, u32[]{:S(2)}, u32[]{:S(2)}) %collective-permute-start.14) | collective-permute-done | bytes 655392 | tf_op jit(solution)/shard_map/tz1/ppermute | solution.py:63
  64.8 0.1 pad_maximum_fusion.1
  64.9 0.1 collective-permute-start.20
  65.0 0.3 collective-permute-start.18
  65.3 1.6 %collective-permute-start.19 = (f32[1280,128]{1,0:T(8,128)S(1)}, f32[1280,128]{1,0:T(8,128)S(1)}, u32[]{:S(2)}, u32[]{:S(2)}) collective-permute-start(f32[1280,128]{1,0:T(8,128)S(1)} %get-tuple-element.81.refs_0_), channel_id=1, source_target_pairs={{0,3},{1,2},{2,1},{3,0},{4,5},{5,4},{6,7},{7,6},{8,11},{9,10},{10,... | collective-permute-start | bytes 1966088 | tf_op jit(solution)/shard_map/hx1/ppermute | solution.py:63
  66.9 2.5 %shard_map.105 = f32[8,24,256]{2,1,0:T(8,128)S(1)} custom-call(f32[640,128]{1,0:T(8,128)S(1)} %pad_maximum_fusion.7.near, f32[640,128]{1,0:T(8,128)S(1)} %collective-permute-done.16.near_other, f32[960,128]{1,0:T(8,128)S(1)} %pad_maximum_fusion.5.pair, f32[960,128]{1,0:T(8,128)S(1)} %collective-permute-done.7.last), custom_call_target="tpu_custom_call" | custom-call | tf_op jit(solution)/shard_map/pallas_call | solution.py:439
  69.4 6.4 %collective-permute-done.18.refs_6_ = f32[1280,128]{1,0:T(8,128)S(1)} collective-permute-done((f32[1280,128]{1,0:T(8,128)S(1)}, f32[1280,128]{1,0:T(8,128)S(1)}, u32[]{:S(2)}, u32[]{:S(2)}) %collective-permute-start.18) | collective-permute-done | bytes 655392 | tf_op jit(solution)/shard_map/tz2/ppermute | solution.py:63
  75.8 0.1 collective-permute-done.19.refs_2_
  75.9 0.0 collective-permute-done.20.refs_9_
  76.0 0.1 pad_maximum_fusion
  76.1 0.9 copy-done.9
  76.9 0.4 copy-done.10
  77.3 0.3 collective-permute-start.23
  77.6 2.3 %collective-permute-start.21 = (f32[1280,128]{1,0:T(8,128)S(1)}, f32[1280,128]{1,0:T(8,128)S(1)}, u32[]{:S(2)}, u32[]{:S(2)}) collective-permute-start(f32[1280,128]{1,0:T(8,128)S(1)} %collective-permute-done.18.refs_6_), channel_id=1, source_target_pairs={{0,56},{1,57},{2,58},{3,59},{4,12},{5,13},{6,14},{7,15},{8,16},{9,... | collective-permute-start | bytes 1966088 | tf_op jit(solution)/shard_map/tz3/ppermute | solution.py:63
  79.9 2.2 %collective-permute-start.22 = (f32[1280,128]{1,0:T(8,128)S(1)}, f32[1280,128]{1,0:T(8,128)S(1)}, u32[]{:S(2)}, u32[]{:S(2)}) collective-permute-start(f32[1280,128]{1,0:T(8,128)S(1)} %collective-permute-done.15.refs_1_), channel_id=1, source_target_pairs={{0,3},{1,2},{2,1},{3,0},{4,5},{5,4},{6,7},{7,6},{8,11},{9,10},{10,... | collective-permute-start | bytes 1966088 | tf_op jit(solution)/shard_map/hx2/ppermute | solution.py:63
  82.2 11.4 %all_to_all.5.mixed = f32[8,24,256]{2,1,0:T(8,128)} all-to-all(f32[8,24,256]{2,1,0:T(8,128)S(1)} %shard_map.105), channel_id=1, replica_groups=mesh['row'=4,'high'=2,'deep'=4,'core'=2,'panel'=4] {'deep','core'}, dimensions={0} | all-to-all | bytes 393216 | tf_op jit(solution)/shard_map/all_to_all | solution.py:454
  93.6 0.0 collective-permute-done.23.refs_10_
  93.6 0.1 pad_maximum_fusion.2
  93.7 0.7 copy-done.5
  94.4 0.2 copy-done.6
  94.6 0.0 collective-permute-start.24
  94.6 3.0 %collective-permute-done.24.refs_11_ = f32[2560,128]{1,0:T(8,128)S(1)} collective-permute-done((f32[2560,128]{1,0:T(8,128)S(1)}, f32[2560,128]{1,0:T(8,128)S(1)}, u32[]{:S(2)}, u32[]{:S(2)}) %collective-permute-start.24) | collective-permute-done | bytes 1310752 | tf_op jit(solution)/shard_map/swap3/ppermute | solution.py:63
  97.7 1.1 copy-done.11
  98.8 13.2 %shard_map.106.own = f32[1,128]{1,0:T(1,128)} custom-call(f32[8,24,256]{2,1,0:T(8,128)} %all_to_all.5.mixed, f32[1280,128]{1,0:T(8,128)} %copy-done.2, f32[1280,128]{1,0:T(8,128)} %copy-done.7, f32[1280,128]{1,0:T(8,128)} %copy-done.9, f32[1280,128]{1,0:T(8,128)} %copy-done.6, f32[1280,128]{1,0:T(8,128)} %copy-done.3, f32[1280,128]{1,0:T(8,128)} %copy-done.4, ...), custom_call_target="tpu_custom_call" | custom-call | tf_op jit(solution)/shard_map/pallas_call | solution.py:459
  112.0 8.9 %all-gather = f32[4,1,128]{2,1,0:T(1,128)S(1)} all-gather(f32[1,1,128]{2,1,0:T(1,128)} %bitcast.8), channel_id=1, replica_groups=mesh['row'=4,'high'=2,'deep'=4,'core'=2,'panel'=4] {'panel'}, dimensions={0}, use_global_device_ids=true | all-gather | bytes 2560 | tf_op jit(solution)/shard_map/all_gather | solution.py:473
  120.8 0.7 copy-done.1
  121.5 0.6 shard_map.107
  (30 shorter events, 0.1 us)
Async XLA Ops:
  2.7 14.5 %copy-start = (f32[160,128]{1,0:T(8,128)S(1)}, f32[160,128]{1,0:T(8,128)}, u32[]{:S(2)}) copy-start(f32[160,128]{1,0:T(8,128)} %get-tuple-element.51.own) | copy-start | bytes 245764
  2.7 12.6 %collective-permute-start.4 = (f32[480,128]{1,0:T(8,128)}, f32[480,128]{1,0:T(8,128)S(1)}, u32[]{:S(2)}, u32[]{:S(2)}) collective-permute-start(f32[480,128]{1,0:T(8,128)} %get-tuple-element.53), channel_id=1, source_target_pairs={{0,1},{1,0},{2,3},{3,2},{4,7},{5,6},{6,5},{7,4},{8,9},{9,8},{10,11... | collective-permute-start | bytes 737288 | tf_op jit(solution)/shard_map/bx0/ppermute | solution.py:63
  5.0 4.8 %collective-permute-start.3 = (f32[160,128]{1,0:T(8,128)}, f32[160,128]{1,0:T(8,128)S(1)}, u32[]{:S(2)}, u32[]{:S(2)}) collective-permute-start(f32[160,128]{1,0:T(8,128)} %get-tuple-element.52), channel_id=1, source_target_pairs={{0,8},{1,9},{2,10},{3,11},{4,60},{5,61},{6,62},{7,63},{8,0},{9,1},... | collective-permute-start | bytes 245768 | tf_op jit(solution)/shard_map/hz0/ppermute | solution.py:63
  5.2 5.4 %collective-permute-start.2 = (f32[160,128]{1,0:T(8,128)}, f32[160,128]{1,0:T(8,128)S(1)}, u32[]{:S(2)}, u32[]{:S(2)}) collective-permute-start(f32[160,128]{1,0:T(8,128)} %get-tuple-element.51.own), channel_id=1, source_target_pairs={{0,192},{1,193},{2,194},{3,195},{4,196},{5,197},{6,198},{7,199},{8... | collective-permute-start | bytes 245768 | tf_op jit(solution)/shard_map/y3/ppermute | solution.py:63
  8.2 6.2 %collective-permute-start.1 = (f32[160,128]{1,0:T(8,128)}, f32[160,128]{1,0:T(8,128)S(1)}, u32[]{:S(2)}, u32[]{:S(2)}) collective-permute-start(f32[160,128]{1,0:T(8,128)} %get-tuple-element.51.own), channel_id=1, source_target_pairs={{0,128},{1,129},{2,130},{3,131},{4,132},{5,133},{6,134},{7,135},{8... | collective-permute-start | bytes 245768 | tf_op jit(solution)/shard_map/y2/ppermute | solution.py:63
  8.8 6.4 %collective-permute-start = (f32[160,128]{1,0:T(8,128)}, f32[160,128]{1,0:T(8,128)S(1)}, u32[]{:S(2)}, u32[]{:S(2)}) collective-permute-start(f32[160,128]{1,0:T(8,128)} %get-tuple-element.51.own), channel_id=1, source_target_pairs={{0,64},{1,65},{2,66},{3,67},{4,68},{5,69},{6,70},{7,71},{8,72},{9,... | collective-permute-start | bytes 245768 | tf_op jit(solution)/shard_map/y1/ppermute | solution.py:63
  17.4 11.6 %collective-permute-start.7 = (f32[960,128]{1,0:T(8,128)S(1)}, f32[960,128]{1,0:T(8,128)S(1)}, u32[]{:S(2)}, u32[]{:S(2)}) collective-permute-start(f32[960,128]{1,0:T(8,128)S(1)} %pad_maximum_fusion.5.pair), channel_id=1, source_target_pairs={{0,3},{1,2},{2,1},{3,0},{4,5},{5,4},{6,7},{7,6},{8,11},{9,10},{10,... | collective-permute-start | bytes 1474568 | tf_op jit(solution)/shard_map/bx1/ppermute | solution.py:63
  20.9 8.1 %collective-permute-start.6 = (f32[320,128]{1,0:T(8,128)S(1)}, f32[320,128]{1,0:T(8,128)S(1)}, u32[]{:S(2)}, u32[]{:S(2)}) collective-permute-start(f32[320,128]{1,0:T(8,128)S(1)} %pad_maximum_fusion.8), channel_id=1, source_target_pairs={{0,56},{1,57},{2,58},{3,59},{4,12},{5,13},{6,14},{7,15},{8,16},{9,... | collective-permute-start | bytes 491528 | tf_op jit(solution)/shard_map/hz1/ppermute | solution.py:63
  24.6 4.4 %collective-permute-start.5 = (f32[160,128]{1,0:T(8,128)S(1)}, f32[160,128]{1,0:T(8,128)S(1)}, u32[]{:S(2)}, u32[]{:S(2)}) collective-permute-start(f32[160,128]{1,0:T(8,128)S(1)} %shard_map.103), channel_id=1, source_target_pairs={{0,1},{1,0},{2,3},{3,2},{4,7},{5,6},{6,5},{7,4},{8,9},{9,8},{10,11... | collective-permute-start | bytes 245768 | tf_op jit(solution)/shard_map/tx0/ppermute | solution.py:63
  29.2 8.8 %collective-permute-start.8 = (f32[320,128]{1,0:T(8,128)S(1)}, f32[320,128]{1,0:T(8,128)S(1)}, u32[]{:S(2)}, u32[]{:S(2)}) collective-permute-start(f32[320,128]{1,0:T(8,128)S(1)} %pad_maximum_fusion.9), channel_id=1, source_target_pairs={{0,3},{1,2},{2,1},{3,0},{4,5},{5,4},{6,7},{7,6},{8,11},{9,10},{10,... | collective-permute-start | bytes 491528 | tf_op jit(solution)/shard_map/tx1/ppermute | solution.py:63
  30.9 7.1 %collective-permute-start.9 = (f32[320,128]{1,0:T(8,128)S(1)}, f32[320,128]{1,0:T(8,128)S(1)}, u32[]{:S(2)}, u32[]{:S(2)}) collective-permute-start(f32[320,128]{1,0:T(8,128)S(1)} %collective-permute-done.6), channel_id=1, source_target_pairs={{0,8},{1,9},{2,10},{3,11},{4,60},{5,61},{6,62},{7,63},{8,0},{9,1},... | collective-permute-start | bytes 491528 | tf_op jit(solution)/shard_map/hz2/ppermute | solution.py:63
  30.9 7.1 %collective-permute-start.10 = (f32[160,128]{1,0:T(8,128)S(1)}, f32[160,128]{1,0:T(8,128)S(1)}, u32[]{:S(2)}, u32[]{:S(2)}) collective-permute-start(f32[160,128]{1,0:T(8,128)S(1)} %shard_map.104), channel_id=1, source_target_pairs={{0,8},{1,9},{2,10},{3,11},{4,12},{5,13},{6,14},{7,15},{8,0},{9,1},... | collective-permute-start | bytes 245768 | tf_op jit(solution)/shard_map/near1/ppermute | solution.py:63
  38.0 13.1 %collective-permute-start.11 = (f32[640,128]{1,0:T(8,128)S(1)}, f32[640,128]{1,0:T(8,128)S(1)}, u32[]{:S(2)}, u32[]{:S(2)}) collective-permute-start(f32[640,128]{1,0:T(8,128)S(1)} %pad_maximum_fusion.6), channel_id=1, source_target_pairs={{0,8},{1,9},{2,10},{3,11},{4,60},{5,61},{6,62},{7,63},{8,0},{9,1},... | collective-permute-start | bytes 983048 | tf_op jit(solution)/shard_map/tz0/ppermute | solution.py:63
  38.1 7.5 %collective-permute-start.12 = (f32[320,128]{1,0:T(8,128)S(1)}, f32[320,128]{1,0:T(8,128)S(1)}, u32[]{:S(2)}, u32[]{:S(2)}) collective-permute-start(f32[320,128]{1,0:T(8,128)S(1)} %collective-permute-done.9), channel_id=1, source_target_pairs={{0,56},{1,57},{2,58},{3,59},{4,12},{5,13},{6,14},{7,15},{8,16},{9,... | collective-permute-start | bytes 491528 | tf_op jit(solution)/shard_map/hz3/ppermute | solution.py:63
  41.8 9.3 %collective-permute-start.13 = (f32[320,128]{1,0:T(8,128)S(1)}, f32[320,128]{1,0:T(8,128)S(1)}, u32[]{:S(2)}, u32[]{:S(2)}) collective-permute-start(f32[320,128]{1,0:T(8,128)S(1)} %pad_maximum_fusion.10), channel_id=1, source_target_pairs={{0,16},{1,17},{2,18},{3,19},{4,20},{5,21},{6,22},{7,23},{8,24},{9,... | collective-permute-start | bytes 491528 | tf_op jit(solution)/shard_map/near2/ppermute | solution.py:63
  51.2 13.7 %copy-start.3 = (f32[1280,128]{1,0:T(8,128)}, f32[1280,128]{1,0:T(8,128)S(1)}, u32[]{:S(2)}) copy-start(f32[1280,128]{1,0:T(8,128)S(1)} %get-tuple-element.77.refs_4_) | copy-start | bytes 1966084
  51.2 14.0 %copy-start.2 = (f32[1280,128]{1,0:T(8,128)}, f32[1280,128]{1,0:T(8,128)S(1)}, u32[]{:S(2)}) copy-start(f32[1280,128]{1,0:T(8,128)S(1)} %get-tuple-element.81.refs_0_) | copy-start | bytes 1966084
  51.2 10.7 %collective-permute-start.15 = (f32[1280,128]{1,0:T(8,128)S(1)}, f32[1280,128]{1,0:T(8,128)S(1)}, u32[]{:S(2)}, u32[]{:S(2)}) collective-permute-start(f32[1280,128]{1,0:T(8,128)S(1)} %get-tuple-element.81.refs_0_), channel_id=1, source_target_pairs={{0,1},{1,0},{2,3},{3,2},{4,7},{5,6},{6,5},{7,4},{8,9},{9,8},{10,11... | collective-permute-start | bytes 1966088 | tf_op jit(solution)/shard_map/hx0/ppermute | solution.py:63
  53.0 8.9 %collective-permute-start.17 = (f32[1280,128]{1,0:T(8,128)S(1)}, f32[1280,128]{1,0:T(8,128)S(1)}, u32[]{:S(2)}, u32[]{:S(2)}) collective-permute-start(f32[1280,128]{1,0:T(8,128)S(1)} %get-tuple-element.77.refs_4_), channel_id=1, source_target_pairs={{0,4},{1,5},{2,6},{3,7},{4,0},{5,1},{6,2},{7,3},{8,12},{9,13},{10,... | collective-permute-start | bytes 1966088 | tf_op jit(solution)/shard_map/swap0/ppermute | solution.py:63
  53.0 11.8 %collective-permute-start.14 = (f32[1280,128]{1,0:T(8,128)S(1)}, f32[1280,128]{1,0:T(8,128)S(1)}, u32[]{:S(2)}, u32[]{:S(2)}) collective-permute-start(f32[1280,128]{1,0:T(8,128)S(1)} %get-tuple-element.77.refs_4_), channel_id=1, source_target_pairs={{0,56},{1,57},{2,58},{3,59},{4,12},{5,13},{6,14},{7,15},{8,16},{9,... | collective-permute-start | bytes 1966088 | tf_op jit(solution)/shard_map/tz1/ppermute | solution.py:63
  54.6 1.6 %collective-permute-start.16 = (f32[640,128]{1,0:T(8,128)S(1)}, f32[640,128]{1,0:T(8,128)S(1)}, u32[]{:S(2)}, u32[]{:S(2)}) collective-permute-start(f32[640,128]{1,0:T(8,128)S(1)} %pad_maximum_fusion.7.near), channel_id=1, source_target_pairs={{0,4},{1,5},{2,6},{3,7},{4,0},{5,1},{6,2},{7,3},{8,12},{9,13},{10,... | collective-permute-start | bytes 983048 | tf_op jit(solution)/shard_map/near_swap/ppermute | solution.py:63
  61.9 18.1 %copy-start.7 = (f32[1280,128]{1,0:T(8,128)}, f32[1280,128]{1,0:T(8,128)S(1)}, u32[]{:S(2)}) copy-start(f32[1280,128]{1,0:T(8,128)S(1)} %collective-permute-done.15.refs_1_) | copy-start | bytes 1966084
  61.9 3.4 %copy-start.12 = (f32[1280,128]{1,0:T(8,128)}, f32[1280,128]{1,0:T(8,128)S(1)}, u32[]{:S(2)}) copy-start(f32[1280,128]{1,0:T(8,128)S(1)} %collective-permute-done.17.refs_8_) | copy-start | bytes 1966084
  64.8 4.6 %copy-start.4 = (f32[1280,128]{1,0:T(8,128)}, f32[1280,128]{1,0:T(8,128)S(1)}, u32[]{:S(2)}) copy-start(f32[1280,128]{1,0:T(8,128)S(1)} %collective-permute-done.14.refs_5_) | copy-start | bytes 1966084
  64.9 11.1 %collective-permute-start.20 = (f32[2560,128]{1,0:T(8,128)S(1)}, f32[2560,128]{1,0:T(8,128)S(1)}, u32[]{:S(2)}, u32[]{:S(2)}) collective-permute-start(f32[2560,128]{1,0:T(8,128)S(1)} %pad_maximum_fusion.1), channel_id=1, source_target_pairs={{0,4},{1,5},{2,6},{3,7},{4,0},{5,1},{6,2},{7,3},{8,12},{9,13},{10,... | collective-permute-start | bytes 3932168 | tf_op jit(solution)/shard_map/swap1/ppermute | solution.py:63
  65.0 10.9 %collective-permute-start.18 = (f32[1280,128]{1,0:T(8,128)S(1)}, f32[1280,128]{1,0:T(8,128)S(1)}, u32[]{:S(2)}, u32[]{:S(2)}) collective-permute-start(f32[1280,128]{1,0:T(8,128)S(1)} %collective-permute-done.14.refs_5_), channel_id=1, source_target_pairs={{0,8},{1,9},{2,10},{3,11},{4,60},{5,61},{6,62},{7,63},{8,0},{9,1},... | collective-permute-start | bytes 1966088 | tf_op jit(solution)/shard_map/tz2/ppermute | solution.py:63
  65.3 10.7 %collective-permute-start.19 = (f32[1280,128]{1,0:T(8,128)S(1)}, f32[1280,128]{1,0:T(8,128)S(1)}, u32[]{:S(2)}, u32[]{:S(2)}) collective-permute-start(f32[1280,128]{1,0:T(8,128)S(1)} %get-tuple-element.81.refs_0_), channel_id=1, source_target_pairs={{0,3},{1,2},{2,1},{3,0},{4,5},{5,4},{6,7},{7,6},{8,11},{9,10},{10,... | collective-permute-start | bytes 1966088 | tf_op jit(solution)/shard_map/hx1/ppermute | solution.py:63
  75.8 1.8 %copy-start.8 = (f32[1280,128]{1,0:T(8,128)}, f32[1280,128]{1,0:T(8,128)S(1)}, u32[]{:S(2)}) copy-start(f32[1280,128]{1,0:T(8,128)S(1)} %collective-permute-done.18.refs_6_) | copy-start | bytes 1966084
  75.9 1.0 copy-start.9
  75.9 1.4 %copy-start.10 = (f32[2560,128]{1,0:T(8,128)}, f32[2560,128]{1,0:T(8,128)S(1)}, u32[]{:S(2)}) copy-start(f32[2560,128]{1,0:T(8,128)S(1)} %collective-permute-done.20.refs_9_) | copy-start | bytes 3932164
  77.3 16.3 %collective-permute-start.23 = (f32[3840,128]{1,0:T(8,128)S(1)}, f32[3840,128]{1,0:T(8,128)}, u32[]{:S(2)}, u32[]{:S(2)}) collective-permute-start(f32[3840,128]{1,0:T(8,128)S(1)} %pad_maximum_fusion), channel_id=1, source_target_pairs={{0,4},{1,5},{2,6},{3,7},{4,0},{5,1},{6,2},{7,3},{8,12},{9,13},{10,... | collective-permute-start | bytes 5898248 | tf_op jit(solution)/shard_map/swap2/ppermute | solution.py:63
  77.6 15.9 %collective-permute-start.21 = (f32[1280,128]{1,0:T(8,128)S(1)}, f32[1280,128]{1,0:T(8,128)S(1)}, u32[]{:S(2)}, u32[]{:S(2)}) collective-permute-start(f32[1280,128]{1,0:T(8,128)S(1)} %collective-permute-done.18.refs_6_), channel_id=1, source_target_pairs={{0,56},{1,57},{2,58},{3,59},{4,12},{5,13},{6,14},{7,15},{8,16},{9,... | collective-permute-start | bytes 1966088 | tf_op jit(solution)/shard_map/tz3/ppermute | solution.py:63
  79.9 13.6 %collective-permute-start.22 = (f32[1280,128]{1,0:T(8,128)S(1)}, f32[1280,128]{1,0:T(8,128)S(1)}, u32[]{:S(2)}, u32[]{:S(2)}) collective-permute-start(f32[1280,128]{1,0:T(8,128)S(1)} %collective-permute-done.15.refs_1_), channel_id=1, source_target_pairs={{0,3},{1,2},{2,1},{3,0},{4,5},{5,4},{6,7},{7,6},{8,11},{9,10},{10,... | collective-permute-start | bytes 1966088 | tf_op jit(solution)/shard_map/hx2/ppermute | solution.py:63
  93.6 0.8 copy-start.5
  93.6 1.1 copy-start.6
  94.6 3.0 %collective-permute-start.24 = (f32[2560,128]{1,0:T(8,128)S(1)}, f32[2560,128]{1,0:T(8,128)S(1)}, u32[]{:S(2)}, u32[]{:S(2)}) collective-permute-start(f32[2560,128]{1,0:T(8,128)S(1)} %pad_maximum_fusion.2), channel_id=1, source_target_pairs={{0,4},{1,5},{2,6},{3,7},{4,0},{5,1},{6,2},{7,3},{8,12},{9,13},{10,... | collective-permute-start | bytes 3932168 | tf_op jit(solution)/shard_map/swap3/ppermute | solution.py:63
  97.7 1.1 copy-start.11
  120.8 0.7 copy-start.1

commit v3 on v2

--- a/solution.py
+++ b/solution.py
@@ -104,18 +104,16 @@
 def place(pieces, width):
     rows = pieces[0][0].shape[0]
     lane = lax.broadcasted_iota(jnp.int32, (rows, 128), 1)
+    pieces = sorted(pieces, key=lambda piece: piece[3])
     tiles = []
-    for tile in range(width // 128):
-        low = tile * 128
+    for low in range(0, width, 128):
         total = jnp.zeros((rows, 128), F32)
         for value, source, length, target in pieces:
-            start, stop = max(target, low), min(target + length, low + 128)
-            if start >= stop:
+            if target + length <= low or target >= low + 128:
                 continue
             shift = (target - source) % 128
             moved = pltpu.roll(value, shift, 1) if shift else value
-            inside = (lane >= start - low) & (lane < stop - low)
-            total = jnp.where(inside, moved, total)
+            total = moved if target <= low else jnp.where(lane >= target - low, moved, total)
         tiles.append(total)
     return jnp.concatenate(tiles, 1)
 
@@ -189,15 +187,34 @@
         copy.wait()
 
 
-def pick_kernel(pair, last, out, sems):
+def pick_kernel(pair, last, out, picked, sems):
     _, _, _, x = here()
     copies = []
     for slot, panel in enumerate(b_panels()):
         source = pair if slot < 2 else last
         start = pl.multiple_of(slot % 2 * 3 * Q + 2 * Q + x * 40, 8)
         target = pl.multiple_of(panel * 40, 8)
-        copies.append((source.at[pl.ds(start, 40), :], out.at[pl.ds(target, 40), :]))
+        copies.append((source.at[pl.ds(start, 40), :], picked.at[pl.ds(target, 40), :]))
     run(copies, sems)
+    lane = lax.broadcasted_iota(jnp.int32, (80, 128), 1)
+    out[0:80, :] = jnp.where(lane < 64, picked[0:80, :], pltpu.roll(picked[80:160, :], 64, 1))
+    lane = lax.broadcasted_iota(jnp.int32, (20, 128), 1)
+    total = jnp.zeros((20, 128), F32)
+    for part in range(8):
+        value = picked[part * 20 : part * 20 + 20, :]
+        moved = pltpu.roll(value, (part * 16 - 64) % 128, 1)
+        total = moved if part == 0 else jnp.where(lane >= part * 16, moved, total)
+    out[80:104, :] = jnp.concatenate([total, jnp.zeros((4, 128), F32)], 0)
+
+
+def unpick(packed):
+    lane = lax.broadcasted_iota(jnp.int32, (Q, 128), 1)
+    main, rest = packed[0:80, :], packed[80:100, :]
+    main = jnp.concatenate([main, pltpu.roll(main, 64, 1)], 0)
+    rest = jnp.concatenate(
+        [pltpu.roll(rest, (64 - part * 16) % 128, 1) for part in range(8)], 0
+    )
+    return jnp.where(lane < 64, main, jnp.where(lane < 80, rest, 0.0))
 
 
 def bottom_kernel(near, near_other, pair, last, out, below, inverse, sems):
@@ -212,12 +229,12 @@
     for core, source in enumerate((near, near_other)):
         for slot in range(4):
             lane = (z & 3 ^ slot) * 2 + (c ^ core)
-            copies.append((source.at[pl.ds(slot * Q, Q), :], inverse.at[lane]))
+            copies.append((source.at[pl.ds(slot * 104, 104), :], inverse.at[lane]))
     run(copies, sems)
     squares = jnp.zeros((Q, 128), F32)
     mixed = jnp.zeros((Q, 256), F32)
     for lane in range(8):
-        part = inverse[lane]
+        part = unpick(inverse[lane])
         squares = squares + part * part
         rows = slice(lane * 80, lane * 80 + 80)
         mixed = mixed + split_dot(
@@ -231,28 +248,29 @@
         out[part, 0:20, :] = mixed[part * 20 : part * 20 + 20]
 
 
-def start_copies(sources, rows, stage, sems):
-    each = 64 // len(sources)
-    copies = []
-    for number, row in enumerate(rows):
-        source, atom = sources[number // each], number % each
-        row = pl.multiple_of(row * Q, Q)
-        copies.append(
-            pltpu.make_async_copy(
-                source.at[pl.ds(atom * Q, Q), :], stage.at[pl.ds(row, Q), :], sems.at[number]
-            )
-        )
+def start_copies(sources, stage, sems):
+    copies = [
+        pltpu.make_async_copy(source, stage.at[index], sems.at[index])
+        for index, source in enumerate(sources)
+    ]
     for copy in copies:
         copy.start()
     return copies
 
 
-def split_stage(stage, high, low):
-    for z in range(8):
-        for core in range(2):
-            rows = slice((2 * z + core) * W, (2 * z + core + 1) * W)
-            lanes = slice(core * 128, core * 128 + 128)
-            high[z, :, lanes], low[z, :, lanes] = split(stage[rows, :])
+def split_stage(copies, blocks, stage, high, low):
+    for index, copy in enumerate(copies):
+        copy.wait()
+        for atom in range(8):
+            number = blocks[index * 8 + atom]
+            rows = pl.ds(pl.multiple_of((number & 3) * Q, Q), Q)
+            first, second = split(stage[index, atom * Q : atom * Q + Q, :])
+            high[number >> 2, rows, :] = first
+            low[number >> 2, rows, :] = second
+
+
+def leaf_pair(ref, z):
+    return jnp.concatenate([ref[2 * z], ref[2 * z + 1]], 1)
 
 
 def halves(left):
@@ -274,21 +292,19 @@
 
 
 def chain_kernel(mixed, *refs):
-    first, second, third, last = refs[8:12]
-    h_parts = [(second, 1), (third, 1), (third, 2), (last, 1)]
-    t_parts = [(first, 0), (second, 0), (third, 0), (last, 0)]
+    first, second, t_last, h_last = refs[8:12]
+    h_parts = [(first, 1), (second, 1), (second, 2), (h_last, 0)]
+    t_parts = [(first, 0), (first, 2), (second, 0), (t_last, 0)]
     rows = 8 * Q
     third = refs[:4] + tuple(swap.at[pl.ds(part * rows, rows), :] for swap, part in h_parts)
     top = refs[4:8] + tuple(swap.at[pl.ds(part * rows, rows), :] for swap, part in t_parts)
     out, third_stage, top_stage, high, low, third_sems, top_sems = refs[12:]
     y, z, c, x = here()
     leaf = z * 2 + c
-    third_copies = start_copies(
-        third, third_rows(z, c, x) + third_rows(z, 1 - c, x), third_stage, third_sems
-    )
-    top_copies = start_copies(
-        top, top_rows(z, c, x) + top_rows(z, 1 - c, x), top_stage, top_sems
-    )
+    third_copies = start_copies(third, third_stage, third_sems)
+    top_copies = start_copies(top, top_stage, top_sems)
+    third_blocks = third_rows(z, c, x) + third_rows(z, 1 - c, x)
+    top_blocks = top_rows(z, c, x) + top_rows(z, 1 - c, x)
     pieces = []
     for part in range(8):
         pieces.append((mixed[part, :, 0:128], 0, 128, part * 240))
@@ -299,13 +315,11 @@
     def products(cols):
         left = halves(cols)
         for z in range(8):
-            product = half_dot(left, high[z], low[z])
+            product = half_dot(left, leaf_pair(high, z), leaf_pair(low, z))
             for core in range(2):
                 yield z, core, product[:, core * 128 : core * 128 + 128]
 
-    for copy in third_copies:
-        copy.wait()
-    split_stage(third_stage, high, low)
+    split_stage(third_copies, third_blocks, third_stage, high, low)
     cols = jnp.concatenate([path[:, 2 * W :], one_hot(16, 10, leaf * 40 + x * 10)], 0)
     pieces = [(part, 0, 40, z * 80 + core * 40) for z, core, part in products(cols)]
     cols = place(pieces, W)
@@ -316,9 +330,7 @@
     change = place(pieces, 2 * W)
     path = jnp.concatenate([path[:, : 2 * W] - change[0:24], -change[24:40]], 0)
 
-    for copy in top_copies:
-        copy.wait()
-    split_stage(top_stage, high, low)
+    split_stage(top_copies, top_blocks, top_stage, high, low)
     cols = jnp.concatenate([path[:, W:], one_hot(8, 5, ((y & 1) * 16 + leaf) * 20 + x * 5)], 0)
     pieces = [
         (part, half * 20, 20, half * 320 + z * 40 + core * 20)
@@ -408,7 +420,10 @@
     tx, h1, b_last = together(tx, h1, b_last)
     t_pair = join(t_chunk, tx)
     (near,) = call(
-        pick_kernel, [(Q, 128)], [HBM] * 2, [pltpu.SemaphoreType.DMA((4,))]
+        pick_kernel,
+        [(104, 128)],
+        [HBM] * 2,
+        [pltpu.VMEM((Q, 128), F32), pltpu.SemaphoreType.DMA((4,))],
     )(b_pair, b_last)
     t_pair, h1, near = together(t_pair, h1, near)
 
@@ -430,19 +445,18 @@
     t1 = send("tz1", step_z(1), t0)
     hx = send("hx0", step_x(0), h_rows)
     near_other = send("near_swap", SWAP, near)
-    swap0 = send("swap0", SWAP, t0)
-    t1, hx, near_other, swap0, h_rows = together(t1, hx, near_other, swap0, h_rows)
+    t1, hx, near_other, h_rows, t0 = together(t1, hx, near_other, h_rows, t0)
 
     t2 = send("tz2", step_z(0), t1)
     h1 = send("hx1", step_x(1), h_rows)
-    swap1 = send("swap1", SWAP, join(t1, h_rows))
+    swap1 = send("swap1", SWAP, jnp.concatenate([t0, h_rows, t1], 0))
     (mixed,) = call(
         bottom_kernel,
         [(8, 24, 256)],
         [HBM] * 4,
         [
             pltpu.VMEM((2, W, 128), F32),
-            pltpu.VMEM((8, Q, 128), F32),
+            pltpu.VMEM((8, 104, 128), F32),
             pltpu.SemaphoreType.DMA((16,)),
         ],
     )(near, near_other, b_pair, b_last)
@@ -454,22 +468,23 @@
     mixed = lax.all_to_all(mixed, ("deep", "core"), 0, 0, tiled=True)
     t3, h2, mixed, swap2 = together(t3, h2, mixed, swap2)
 
-    swap3 = send("swap3", SWAP, join(t3, h2))
+    u3 = send("swap_t3", SWAP, t3)
+    g2 = send("swap_h2", SWAP, h2)
 
     (variances,) = call(
         chain_kernel,
         [(1, 128)],
         [VMEM] + [HBM] * 12,
         [
-            pltpu.VMEM((16 * W, 128), F32),
-            pltpu.VMEM((16 * W, 128), F32),
-            pltpu.VMEM((8, W, 256), jnp.bfloat16),
-            pltpu.VMEM((8, W, 256), jnp.bfloat16),
-            pltpu.SemaphoreType.DMA((64,)),
-            pltpu.SemaphoreType.DMA((64,)),
+            pltpu.VMEM((8, 8 * Q, 128), F32),
+            pltpu.VMEM((8, 8 * Q, 128), F32),
+            pltpu.VMEM((16, W, 128), jnp.bfloat16),
+            pltpu.VMEM((16, W, 128), jnp.bfloat16),
+            pltpu.SemaphoreType.DMA((8,)),
+            pltpu.SemaphoreType.DMA((8,)),
         ],
         limit=60,
-    )(mixed, h_rows, hx, h1, h2, t0, t1, t2, t3, swap0, swap1, swap2, swap3)
+    )(mixed, h_rows, hx, h1, h2, t0, t1, t2, t3, swap1, swap2, u3, g2)
     gathered = lax.all_gather(variances, "panel", axis=0, tiled=True)
     outs = call(finish_kernel, [(1, 10), (1, 20), (1, 40), (1, 80)], [VMEM] * 2)(
         variances, gathered

time: 123 us -> 121 us (0.984)
  waiting for transfers between devices: 42.5 us -> 35 us
  starting transfers between devices: 33.5 us -> 40.5 us
  blocking collectives: 20.3 us -> 22.9 us
  Pallas kernels: 18.7 us -> 16.7 us
  local copies, waits for them, and re-layouts: 3.95 us -> 2.43 us
    ppermute x25, waiting for transfers between devices: 42.5 us -> 35 us  [permute(): return lax.ppermute(value, ALL, pairs)]
    ppermute x25, starting transfers between devices: 33.5 us -> 40.5 us  [permute(): return lax.ppermute(value, ALL, pairs)]
    all_gather x1, blocking collectives: 8.86 us -> 10.9 us  [shards(): gathered = lax.all_gather(variances, 'panel', axis=0, tiled=True)]
    pallas_call x2, Pallas kernels: 13.4 us -> 11.6 us  [the longest x1 11.4 us: shards(): call(chain_kernel, [(1, 128)], [VMEM] + [HBM] * 12, [pltpu.VMEM((8, 8 * Q...]
    unnamed x26, local copies, waits for them, and re-layouts: 3.95 us -> 2.43 us
  transfers between devices with their start and end apart: 25 -> 25, of which waited for: 13 -> 14; matrix products, arithmetic and copies ran while one was open for 0% -> 0% of each run, Pallas kernels for 2% -> 2%
where the time goes in v3:
time: 121 us
  starting transfers between devices  40.5 us (33%)
  waiting for transfers between devices  35 us (29%)
  blocking collectives  22.9 us (19%)
  Pallas kernels  16.7 us (14%)
  local copies, waits for them, and re-layouts  2.43 us (2%)
  other arithmetic  2.3 us (2%)
    ppermute x25, starting transfers between devices, permute(): return lax.ppermute(value, ALL, pairs)  40.5 us
    ppermute x25, waiting for transfers between devices, permute(): return lax.ppermute(value, ALL, pairs)  35 us
    all_to_all x1, blocking collectives, shards(): mixed = lax.all_to_all(mixed, ('deep', 'core'), 0, 0, tiled=True)  12 us
    pallas_call x1, Pallas kernels, shards(): call(chain_kernel, [(1, 128)], [VMEM] + [HBM] * 12, [pltpu.VMEM((8, 8 * Q...  11.4 us
    all_gather x1, blocking collectives, shards(): gathered = lax.all_gather(variances, 'panel', axis=0, tiled=True)  10.9 us
    unnamed x26, local copies, waits for them, and re-layouts  2.43 us
  transfers between devices with their start and end apart: 25, of which 14 were waited for; matrix products, arithmetic and copies ran while one was open for 0% of the time, Pallas kernels for 2%

profile of v3, /device:TPU:2, one launch (start us, length us, event | category | flops | bytes accessed | tf_op | source)
XLA Modules:
  0.0 120.7 jit_solution(1474732082887728897)
XLA Ops:
  0.6 2.0 %shard_map.102 = (f32[160,128]{1,0:T(8,128)}, f32[160,128]{1,0:T(8,128)}, f32[480,128]{1,0:T(8,128)}) custom-call(f32[40,160]{1,0:T(8,128)} %d2.1, f32[80,160]{1,0:T(8,128)} %b2.1, f32[160,240]{1,0:T(8,128)} %bitcast.9, f32[80,160]{1,0:T(8,128)} %d3.1, f32[20,160]{1,0:T(8,128)} %d1.1, f32[20,160]{1,0:T(8,128)} %b1.1, f32[10,160]{1,0:T(8,128)} %d0.1), custom_call_target="tpu_custom_call" | custom-call | tf_op jit(solution)/shard_map/pallas_call | solution.py:392
  2.7 2.4 %collective-permute-start.4 = (f32[480,128]{1,0:T(8,128)}, f32[480,128]{1,0:T(8,128)S(1)}, u32[]{:S(2)}, u32[]{:S(2)}) collective-permute-start(f32[480,128]{1,0:T(8,128)} %get-tuple-element.53), channel_id=1, source_target_pairs={{0,1},{1,0},{2,3},{3,2},{4,7},{5,6},{6,5},{7,4},{8,9},{9,8},{10,11... | collective-permute-start | bytes 737288 | tf_op jit(solution)/shard_map/bx0/ppermute | solution.py:63
  5.0 0.0 collective-permute-start
  5.0 2.7 %collective-permute-start.1 = (f32[160,128]{1,0:T(8,128)}, f32[160,128]{1,0:T(8,128)S(1)}, u32[]{:S(2)}, u32[]{:S(2)}) collective-permute-start(f32[160,128]{1,0:T(8,128)} %get-tuple-element.51.own), channel_id=1, source_target_pairs={{0,128},{1,129},{2,130},{3,131},{4,132},{5,133},{6,134},{7,135},{8... | collective-permute-start | bytes 245768 | tf_op jit(solution)/shard_map/y2/ppermute | solution.py:63
  7.8 1.3 %collective-permute-start.2 = (f32[160,128]{1,0:T(8,128)}, f32[160,128]{1,0:T(8,128)S(1)}, u32[]{:S(2)}, u32[]{:S(2)}) collective-permute-start(f32[160,128]{1,0:T(8,128)} %get-tuple-element.51.own), channel_id=1, source_target_pairs={{0,192},{1,193},{2,194},{3,195},{4,196},{5,197},{6,198},{7,199},{8... | collective-permute-start | bytes 245768 | tf_op jit(solution)/shard_map/y3/ppermute | solution.py:63
  9.1 1.9 %collective-permute-start.3 = (f32[160,128]{1,0:T(8,128)}, f32[160,128]{1,0:T(8,128)S(1)}, u32[]{:S(2)}, u32[]{:S(2)}) collective-permute-start(f32[160,128]{1,0:T(8,128)} %get-tuple-element.52), channel_id=1, source_target_pairs={{0,8},{1,9},{2,10},{3,11},{4,60},{5,61},{6,62},{7,63},{8,0},{9,1},... | collective-permute-start | bytes 245768 | tf_op jit(solution)/shard_map/hz0/ppermute | solution.py:63
  11.0 0.2 collective-permute-done.one
  11.3 1.4 %collective-permute-done.1.two = f32[160,128]{1,0:T(8,128)S(1)} collective-permute-done((f32[160,128]{1,0:T(8,128)}, f32[160,128]{1,0:T(8,128)S(1)}, u32[]{:S(2)}, u32[]{:S(2)}) %collective-permute-start.1) | collective-permute-done | bytes 81952 | tf_op jit(solution)/shard_map/y2/ppermute | solution.py:63
  12.6 0.5 collective-permute-done.2.three
  13.1 0.6 collective-permute-done.3
  13.8 0.0 collective-permute-done.4
  13.8 1.0 pad_maximum_fusion.4.pair
  14.7 0.9 pad_maximum_fusion.7
  15.7 0.9 copy-done
  16.5 0.2 shard_map.103
  16.8 2.2 %collective-permute-start.7 = (f32[960,128]{1,0:T(8,128)S(1)}, f32[960,128]{1,0:T(8,128)S(1)}, u32[]{:S(2)}, u32[]{:S(2)}) collective-permute-start(f32[960,128]{1,0:T(8,128)S(1)} %pad_maximum_fusion.4.pair), channel_id=1, source_target_pairs={{0,3},{1,2},{2,1},{3,0},{4,5},{5,4},{6,7},{7,6},{8,11},{9,10},{10,... | collective-permute-start | bytes 1474568 | tf_op jit(solution)/shard_map/bx1/ppermute | solution.py:63
  19.0 5.9 %collective-permute-start.6 = (f32[320,128]{1,0:T(8,128)S(1)}, f32[320,128]{1,0:T(8,128)S(1)}, u32[]{:S(2)}, u32[]{:S(2)}) collective-permute-start(f32[320,128]{1,0:T(8,128)S(1)} %pad_maximum_fusion.7), channel_id=1, source_target_pairs={{0,56},{1,57},{2,58},{3,59},{4,12},{5,13},{6,14},{7,15},{8,16},{9,... | collective-permute-start | bytes 491528 | tf_op jit(solution)/shard_map/hz1/ppermute | solution.py:63
  24.9 1.4 %collective-permute-start.5 = (f32[160,128]{1,0:T(8,128)S(1)}, f32[160,128]{1,0:T(8,128)S(1)}, u32[]{:S(2)}, u32[]{:S(2)}) collective-permute-start(f32[160,128]{1,0:T(8,128)S(1)} %shard_map.103), channel_id=1, source_target_pairs={{0,1},{1,0},{2,3},{3,2},{4,7},{5,6},{6,5},{7,4},{8,9},{9,8},{10,11... | collective-permute-start | bytes 245768 | tf_op jit(solution)/shard_map/tx0/ppermute | solution.py:63
  26.3 3.0 %collective-permute-done.5 = f32[160,128]{1,0:T(8,128)S(1)} collective-permute-done((f32[160,128]{1,0:T(8,128)S(1)}, f32[160,128]{1,0:T(8,128)S(1)}, u32[]{:S(2)}, u32[]{:S(2)}) %collective-permute-start.5) | collective-permute-done | bytes 81952 | tf_op jit(solution)/shard_map/tx0/ppermute | solution.py:63
  29.3 0.0 collective-permute-done.6
  29.3 0.0 collective-permute-done.7.last
  29.3 0.2 shard_map.104
  29.6 0.2 collective-permute-start.8
  29.8 1.2 collective-permute-start.9
  31.0 0.8 collective-permute-start.10
  31.8 4.0 %collective-permute-done.10 = f32[104,128]{1,0:T(8,128)S(1)} collective-permute-done((f32[104,128]{1,0:T(8,128)S(1)}, f32[104,128]{1,0:T(8,128)S(1)}, u32[]{:S(2)}, u32[]{:S(2)}) %collective-permute-start.10) | collective-permute-done | bytes 53280 | tf_op jit(solution)/shard_map/near1/ppermute | solution.py:63
  35.8 0.0 collective-permute-done.8
  35.8 0.0 collective-permute-done.9
  35.8 1.7 %collective-permute-start.11 = (f32[640,128]{1,0:T(8,128)S(1)}, f32[640,128]{1,0:T(8,128)S(1)}, u32[]{:S(2)}, u32[]{:S(2)}) collective-permute-start(f32[640,128]{1,0:T(8,128)S(1)} %pad_maximum_fusion.5), channel_id=1, source_target_pairs={{0,8},{1,9},{2,10},{3,11},{4,60},{5,61},{6,62},{7,63},{8,0},{9,1},... | collective-permute-start | bytes 983048 | tf_op jit(solution)/shard_map/tz0/ppermute | solution.py:63
  37.6 3.5 %collective-permute-start.12 = (f32[320,128]{1,0:T(8,128)S(1)}, f32[320,128]{1,0:T(8,128)S(1)}, u32[]{:S(2)}, u32[]{:S(2)}) collective-permute-start(f32[320,128]{1,0:T(8,128)S(1)} %collective-permute-done.9), channel_id=1, source_target_pairs={{0,56},{1,57},{2,58},{3,59},{4,12},{5,13},{6,14},{7,15},{8,16},{9,... | collective-permute-start | bytes 491528 | tf_op jit(solution)/shard_map/hz3/ppermute | solution.py:63
  41.1 0.0 collective-permute-start.13
  41.1 7.9 %collective-permute-done.13 = f32[208,128]{1,0:T(8,128)S(1)} collective-permute-done((f32[208,128]{1,0:T(8,128)S(1)}, f32[208,128]{1,0:T(8,128)S(1)}, u32[]{:S(2)}, u32[]{:S(2)}) %collective-permute-start.13) | collective-permute-done | bytes 106528 | tf_op jit(solution)/shard_map/near2/ppermute | solution.py:63
  49.0 0.0 collective-permute-done.12
  49.0 0.0 collective-permute-done.11
  49.0 0.1 pad_maximum_fusion.2
  49.2 0.6 collective-permute-start.14
  49.8 3.0 %collective-permute-start.15 = (f32[1280,128]{1,0:T(8,128)S(1)}, f32[1280,128]{1,0:T(8,128)S(1)}, u32[]{:S(2)}, u32[]{:S(2)}) collective-permute-start(f32[1280,128]{1,0:T(8,128)S(1)} %get-tuple-element.81.refs_0_), channel_id=1, source_target_pairs={{0,1},{1,0},{2,3},{3,2},{4,7},{5,6},{6,5},{7,4},{8,9},{9,8},{10,11... | collective-permute-start | bytes 1966088 | tf_op jit(solution)/shard_map/hx0/ppermute | solution.py:63
  52.8 0.0 collective-permute-start.16
  52.8 1.5 %collective-permute-done.16.near_other = f32[416,128]{1,0:T(8,128)S(1)} collective-permute-done((f32[416,128]{1,0:T(8,128)S(1)}, f32[416,128]{1,0:T(8,128)S(1)}, u32[]{:S(2)}, u32[]{:S(2)}) %collective-permute-start.16) | collective-permute-done | bytes 213024 | tf_op jit(solution)/shard_map/near_swap/ppermute | solution.py:63
  54.3 6.8 %collective-permute-done.14.refs_5_ = f32[1280,128]{1,0:T(8,128)S(1)} collective-permute-done((f32[1280,128]{1,0:T(8,128)S(1)}, f32[1280,128]{1,0:T(8,128)S(1)}, u32[]{:S(2)}, u32[]{:S(2)}) %collective-permute-start.14) | collective-permute-done | bytes 655392 | tf_op jit(solution)/shard_map/tz1/ppermute | solution.py:63
  61.1 0.3 collective-permute-done.15.refs_1_
  61.4 0.1 pad_maximum_fusion
  61.5 0.1 collective-permute-start.19
  61.6 0.1 collective-permute-start.17
  61.7 4.8 %collective-permute-start.18 = (f32[1280,128]{1,0:T(8,128)S(1)}, f32[1280,128]{1,0:T(8,128)S(1)}, u32[]{:S(2)}, u32[]{:S(2)}) collective-permute-start(f32[1280,128]{1,0:T(8,128)S(1)} %get-tuple-element.81.refs_0_), channel_id=1, source_target_pairs={{0,3},{1,2},{2,1},{3,0},{4,5},{5,4},{6,7},{7,6},{8,11},{9,10},{10,... | collective-permute-start | bytes 1966088 | tf_op jit(solution)/shard_map/hx1/ppermute | solution.py:63
  66.6 2.3 %shard_map.105 = f32[8,24,256]{2,1,0:T(8,128)S(1)} custom-call(f32[416,128]{1,0:T(8,128)S(1)} %pad_maximum_fusion.6.near, f32[416,128]{1,0:T(8,128)S(1)} %collective-permute-done.16.near_other, f32[960,128]{1,0:T(8,128)S(1)} %pad_maximum_fusion.4.pair, f32[960,128]{1,0:T(8,128)S(1)} %collective-permute-done.7.last), custom_call_target="tpu_custom_call" | custom-call | tf_op jit(solution)/shard_map/pallas_call | solution.py:453
  68.8 3.4 %collective-permute-done.17.refs_6_ = f32[1280,128]{1,0:T(8,128)S(1)} collective-permute-done((f32[1280,128]{1,0:T(8,128)S(1)}, f32[1280,128]{1,0:T(8,128)S(1)}, u32[]{:S(2)}, u32[]{:S(2)}) %collective-permute-start.17) | collective-permute-done | bytes 655392 | tf_op jit(solution)/shard_map/tz2/ppermute | solution.py:63
  72.3 2.8 %collective-permute-done.18.refs_2_ = f32[1280,128]{1,0:T(8,128)S(1)} collective-permute-done((f32[1280,128]{1,0:T(8,128)S(1)}, f32[1280,128]{1,0:T(8,128)S(1)}, u32[]{:S(2)}, u32[]{:S(2)}) %collective-permute-start.18) | collective-permute-done | bytes 655392 | tf_op jit(solution)/shard_map/hx1/ppermute | solution.py:63
  75.1 0.0 collective-permute-done.19.refs_8_
  75.1 0.1 pad_maximum_fusion.1
  75.3 0.1 collective-permute-start.22
  75.4 3.7 %collective-permute-start.20 = (f32[1280,128]{1,0:T(8,128)S(1)}, f32[1280,128]{1,0:T(8,128)S(1)}, u32[]{:S(2)}, u32[]{:S(2)}) collective-permute-start(f32[1280,128]{1,0:T(8,128)S(1)} %collective-permute-done.17.refs_6_), channel_id=1, source_target_pairs={{0,56},{1,57},{2,58},{3,59},{4,12},{5,13},{6,14},{7,15},{8,16},{9,... | collective-permute-start | bytes 1966088 | tf_op jit(solution)/shard_map/tz3/ppermute | solution.py:63
  79.1 2.0 %collective-permute-start.21 = (f32[1280,128]{1,0:T(8,128)S(1)}, f32[1280,128]{1,0:T(8,128)S(1)}, u32[]{:S(2)}, u32[]{:S(2)}) collective-permute-start(f32[1280,128]{1,0:T(8,128)S(1)} %collective-permute-done.15.refs_1_), channel_id=1, source_target_pairs={{0,3},{1,2},{2,1},{3,0},{4,5},{5,4},{6,7},{7,6},{8,11},{9,10},{10,... | collective-permute-start | bytes 1966088 | tf_op jit(solution)/shard_map/hx2/ppermute | solution.py:63
  81.1 12.0 %all_to_all.5.mixed = f32[8,24,256]{2,1,0:T(8,128)} all-to-all(f32[8,24,256]{2,1,0:T(8,128)S(1)} %shard_map.105), channel_id=1, replica_groups=mesh['row'=4,'high'=2,'deep'=4,'core'=2,'panel'=4] {'deep','core'}, dimensions={0} | all-to-all | bytes 393216 | tf_op jit(solution)/shard_map/all_to_all | solution.py:468
  93.2 0.0 collective-permute-done.22.refs_9_
  93.2 0.1 collective-permute-start.23
  93.3 0.5 collective-permute-start.24
  93.8 1.6 %collective-permute-done.23.refs_10_ = f32[1280,128]{1,0:T(8,128)S(1)} collective-permute-done((f32[1280,128]{1,0:T(8,128)S(1)}, f32[1280,128]{1,0:T(8,128)S(1)}, u32[]{:S(2)}, u32[]{:S(2)}) %collective-permute-start.23) | collective-permute-done | bytes 655392 | tf_op jit(solution)/shard_map/swap_t3/ppermute | solution.py:63
  95.4 0.9 collective-permute-done.24.refs_11_
  96.3 0.9 copy-done.12
  97.2 11.4 %shard_map.106.own = f32[1,128]{1,0:T(1,128)} custom-call(f32[8,24,256]{2,1,0:T(8,128)} %all_to_all.5.mixed, f32[1280,128]{1,0:T(8,128)} %copy-done.3, f32[1280,128]{1,0:T(8,128)} %copy-done.5, f32[1280,128]{1,0:T(8,128)} %copy-done.7, f32[1280,128]{1,0:T(8,128)} %copy-done.10, f32[1280,128]{1,0:T(8,128)} %copy-done.2, f32[1280,128]{1,0:T(8,128)} %copy-done.4, ...), custom_call_target="tpu_custom_call" | custom-call | tf_op jit(solution)/shard_map/pallas_call | solution.py:474
  108.6 10.9 %all-gather = f32[4,1,128]{2,1,0:T(1,128)S(1)} all-gather(f32[1,1,128]{2,1,0:T(1,128)} %bitcast.8), channel_id=1, replica_groups=mesh['row'=4,'high'=2,'deep'=4,'core'=2,'panel'=4] {'panel'}, dimensions={0}, use_global_device_ids=true | all-gather | bytes 2560 | tf_op jit(solution)/shard_map/all_gather | solution.py:488
  119.5 0.7 copy-done.1
  120.1 0.6 shard_map.107
  (29 shorter events, 0.1 us)
Async XLA Ops:
  2.7 11.1 %collective-permute-start.4 = (f32[480,128]{1,0:T(8,128)}, f32[480,128]{1,0:T(8,128)S(1)}, u32[]{:S(2)}, u32[]{:S(2)}) collective-permute-start(f32[480,128]{1,0:T(8,128)} %get-tuple-element.53), channel_id=1, source_target_pairs={{0,1},{1,0},{2,3},{3,2},{4,7},{5,6},{6,5},{7,4},{8,9},{9,8},{10,11... | collective-permute-start | bytes 737288 | tf_op jit(solution)/shard_map/bx0/ppermute | solution.py:63
  5.0 6.3 %collective-permute-start = (f32[160,128]{1,0:T(8,128)}, f32[160,128]{1,0:T(8,128)S(1)}, u32[]{:S(2)}, u32[]{:S(2)}) collective-permute-start(f32[160,128]{1,0:T(8,128)} %get-tuple-element.51.own), channel_id=1, source_target_pairs={{0,64},{1,65},{2,66},{3,67},{4,68},{5,69},{6,70},{7,71},{8,72},{9,... | collective-permute-start | bytes 245768 | tf_op jit(solution)/shard_map/y1/ppermute | solution.py:63
  5.0 7.6 %collective-permute-start.1 = (f32[160,128]{1,0:T(8,128)}, f32[160,128]{1,0:T(8,128)S(1)}, u32[]{:S(2)}, u32[]{:S(2)}) collective-permute-start(f32[160,128]{1,0:T(8,128)} %get-tuple-element.51.own), channel_id=1, source_target_pairs={{0,128},{1,129},{2,130},{3,131},{4,132},{5,133},{6,134},{7,135},{8... | collective-permute-start | bytes 245768 | tf_op jit(solution)/shard_map/y2/ppermute | solution.py:63
  7.8 5.4 %collective-permute-start.2 = (f32[160,128]{1,0:T(8,128)}, f32[160,128]{1,0:T(8,128)S(1)}, u32[]{:S(2)}, u32[]{:S(2)}) collective-permute-start(f32[160,128]{1,0:T(8,128)} %get-tuple-element.51.own), channel_id=1, source_target_pairs={{0,192},{1,193},{2,194},{3,195},{4,196},{5,197},{6,198},{7,199},{8... | collective-permute-start | bytes 245768 | tf_op jit(solution)/shard_map/y3/ppermute | solution.py:63
  9.1 4.7 %collective-permute-start.3 = (f32[160,128]{1,0:T(8,128)}, f32[160,128]{1,0:T(8,128)S(1)}, u32[]{:S(2)}, u32[]{:S(2)}) collective-permute-start(f32[160,128]{1,0:T(8,128)} %get-tuple-element.52), channel_id=1, source_target_pairs={{0,8},{1,9},{2,10},{3,11},{4,60},{5,61},{6,62},{7,63},{8,0},{9,1},... | collective-permute-start | bytes 245768 | tf_op jit(solution)/shard_map/hz0/ppermute | solution.py:63
  15.6 0.9 copy-start
  16.8 12.5 %collective-permute-start.7 = (f32[960,128]{1,0:T(8,128)S(1)}, f32[960,128]{1,0:T(8,128)S(1)}, u32[]{:S(2)}, u32[]{:S(2)}) collective-permute-start(f32[960,128]{1,0:T(8,128)S(1)} %pad_maximum_fusion.4.pair), channel_id=1, source_target_pairs={{0,3},{1,2},{2,1},{3,0},{4,5},{5,4},{6,7},{7,6},{8,11},{9,10},{10,... | collective-permute-start | bytes 1474568 | tf_op jit(solution)/shard_map/bx1/ppermute | solution.py:63
  19.0 10.3 %collective-permute-start.6 = (f32[320,128]{1,0:T(8,128)S(1)}, f32[320,128]{1,0:T(8,128)S(1)}, u32[]{:S(2)}, u32[]{:S(2)}) collective-permute-start(f32[320,128]{1,0:T(8,128)S(1)} %pad_maximum_fusion.7), channel_id=1, source_target_pairs={{0,56},{1,57},{2,58},{3,59},{4,12},{5,13},{6,14},{7,15},{8,16},{9,... | collective-permute-start | bytes 491528 | tf_op jit(solution)/shard_map/hz1/ppermute | solution.py:63
  24.9 4.4 %collective-permute-start.5 = (f32[160,128]{1,0:T(8,128)S(1)}, f32[160,128]{1,0:T(8,128)S(1)}, u32[]{:S(2)}, u32[]{:S(2)}) collective-permute-start(f32[160,128]{1,0:T(8,128)S(1)} %shard_map.103), channel_id=1, source_target_pairs={{0,1},{1,0},{2,3},{3,2},{4,7},{5,6},{6,5},{7,4},{8,9},{9,8},{10,11... | collective-permute-start | bytes 245768 | tf_op jit(solution)/shard_map/tx0/ppermute | solution.py:63
  29.6 6.2 %collective-permute-start.8 = (f32[320,128]{1,0:T(8,128)S(1)}, f32[320,128]{1,0:T(8,128)S(1)}, u32[]{:S(2)}, u32[]{:S(2)}) collective-permute-start(f32[320,128]{1,0:T(8,128)S(1)} %pad_maximum_fusion.8), channel_id=1, source_target_pairs={{0,3},{1,2},{2,1},{3,0},{4,5},{5,4},{6,7},{7,6},{8,11},{9,10},{10,... | collective-permute-start | bytes 491528 | tf_op jit(solution)/shard_map/tx1/ppermute | solution.py:63
  29.8 6.0 %collective-permute-start.9 = (f32[320,128]{1,0:T(8,128)S(1)}, f32[320,128]{1,0:T(8,128)S(1)}, u32[]{:S(2)}, u32[]{:S(2)}) collective-permute-start(f32[320,128]{1,0:T(8,128)S(1)} %collective-permute-done.6), channel_id=1, source_target_pairs={{0,8},{1,9},{2,10},{3,11},{4,60},{5,61},{6,62},{7,63},{8,0},{9,1},... | collective-permute-start | bytes 491528 | tf_op jit(solution)/shard_map/hz2/ppermute | solution.py:63
  31.0 4.8 %collective-permute-start.10 = (f32[104,128]{1,0:T(8,128)S(1)}, f32[104,128]{1,0:T(8,128)S(1)}, u32[]{:S(2)}, u32[]{:S(2)}) collective-permute-start(f32[104,128]{1,0:T(8,128)S(1)} %shard_map.104), channel_id=1, source_target_pairs={{0,8},{1,9},{2,10},{3,11},{4,12},{5,13},{6,14},{7,15},{8,0},{9,1},... | collective-permute-start | bytes 159752 | tf_op jit(solution)/shard_map/near1/ppermute | solution.py:63
  35.8 13.2 %collective-permute-start.11 = (f32[640,128]{1,0:T(8,128)S(1)}, f32[640,128]{1,0:T(8,128)S(1)}, u32[]{:S(2)}, u32[]{:S(2)}) collective-permute-start(f32[640,128]{1,0:T(8,128)S(1)} %pad_maximum_fusion.5), channel_id=1, source_target_pairs={{0,8},{1,9},{2,10},{3,11},{4,60},{5,61},{6,62},{7,63},{8,0},{9,1},... | collective-permute-start | bytes 983048 | tf_op jit(solution)/shard_map/tz0/ppermute | solution.py:63
  37.6 11.5 %collective-permute-start.12 = (f32[320,128]{1,0:T(8,128)S(1)}, f32[320,128]{1,0:T(8,128)S(1)}, u32[]{:S(2)}, u32[]{:S(2)}) collective-permute-start(f32[320,128]{1,0:T(8,128)S(1)} %collective-permute-done.9), channel_id=1, source_target_pairs={{0,56},{1,57},{2,58},{3,59},{4,12},{5,13},{6,14},{7,15},{8,16},{9,... | collective-permute-start | bytes 491528 | tf_op jit(solution)/shard_map/hz3/ppermute | solution.py:63
  41.1 7.9 %collective-permute-start.13 = (f32[208,128]{1,0:T(8,128)S(1)}, f32[208,128]{1,0:T(8,128)S(1)}, u32[]{:S(2)}, u32[]{:S(2)}) collective-permute-start(f32[208,128]{1,0:T(8,128)S(1)} %pad_maximum_fusion.9), channel_id=1, source_target_pairs={{0,16},{1,17},{2,18},{3,19},{4,20},{5,21},{6,22},{7,23},{8,24},{9,... | collective-permute-start | bytes 319496 | tf_op jit(solution)/shard_map/near2/ppermute | solution.py:63
  49.2 12.4 %copy-start.2 = (f32[1280,128]{1,0:T(8,128)}, f32[1280,128]{1,0:T(8,128)S(1)}, u32[]{:S(2)}) copy-start(f32[1280,128]{1,0:T(8,128)S(1)} %get-tuple-element.82.refs_4_) | copy-start | bytes 1966084
  49.2 12.6 %copy-start.3 = (f32[1280,128]{1,0:T(8,128)}, f32[1280,128]{1,0:T(8,128)S(1)}, u32[]{:S(2)}) copy-start(f32[1280,128]{1,0:T(8,128)S(1)} %get-tuple-element.81.refs_0_) | copy-start | bytes 1966084
  49.2 11.9 %collective-permute-start.14 = (f32[1280,128]{1,0:T(8,128)S(1)}, f32[1280,128]{1,0:T(8,128)S(1)}, u32[]{:S(2)}, u32[]{:S(2)}) collective-permute-start(f32[1280,128]{1,0:T(8,128)S(1)} %get-tuple-element.82.refs_4_), channel_id=1, source_target_pairs={{0,56},{1,57},{2,58},{3,59},{4,12},{5,13},{6,14},{7,15},{8,16},{9,... | collective-permute-start | bytes 1966088 | tf_op jit(solution)/shard_map/tz1/ppermute | solution.py:63
  49.8 11.6 %collective-permute-start.15 = (f32[1280,128]{1,0:T(8,128)S(1)}, f32[1280,128]{1,0:T(8,128)S(1)}, u32[]{:S(2)}, u32[]{:S(2)}) collective-permute-start(f32[1280,128]{1,0:T(8,128)S(1)} %get-tuple-element.81.refs_0_), channel_id=1, source_target_pairs={{0,1},{1,0},{2,3},{3,2},{4,7},{5,6},{6,5},{7,4},{8,9},{9,8},{10,11... | collective-permute-start | bytes 1966088 | tf_op jit(solution)/shard_map/hx0/ppermute | solution.py:63
  52.8 1.5 %collective-permute-start.16 = (f32[416,128]{1,0:T(8,128)S(1)}, f32[416,128]{1,0:T(8,128)S(1)}, u32[]{:S(2)}, u32[]{:S(2)}) collective-permute-start(f32[416,128]{1,0:T(8,128)S(1)} %pad_maximum_fusion.6.near), channel_id=1, source_target_pairs={{0,4},{1,5},{2,6},{3,7},{4,0},{5,1},{6,2},{7,3},{8,12},{9,13},{10,... | collective-permute-start | bytes 638984 | tf_op jit(solution)/shard_map/near_swap/ppermute | solution.py:63
  61.1 7.8 %copy-start.4 = (f32[1280,128]{1,0:T(8,128)}, f32[1280,128]{1,0:T(8,128)S(1)}, u32[]{:S(2)}) copy-start(f32[1280,128]{1,0:T(8,128)S(1)} %collective-permute-done.14.refs_5_) | copy-start | bytes 1966084
  61.4 17.7 %copy-start.5 = (f32[1280,128]{1,0:T(8,128)}, f32[1280,128]{1,0:T(8,128)S(1)}, u32[]{:S(2)}) copy-start(f32[1280,128]{1,0:T(8,128)S(1)} %collective-permute-done.15.refs_1_) | copy-start | bytes 1966084
  61.5 13.6 %collective-permute-start.19 = (f32[3840,128]{1,0:T(8,128)S(1)}, f32[3840,128]{1,0:T(8,128)S(1)}, u32[]{:S(2)}, u32[]{:S(2)}) collective-permute-start(f32[3840,128]{1,0:T(8,128)S(1)} %pad_maximum_fusion), channel_id=1, source_target_pairs={{0,4},{1,5},{2,6},{3,7},{4,0},{5,1},{6,2},{7,3},{8,12},{9,13},{10,... | collective-permute-start | bytes 5898248 | tf_op jit(solution)/shard_map/swap1/ppermute | solution.py:63
  61.6 10.7 %collective-permute-start.17 = (f32[1280,128]{1,0:T(8,128)S(1)}, f32[1280,128]{1,0:T(8,128)S(1)}, u32[]{:S(2)}, u32[]{:S(2)}) collective-permute-start(f32[1280,128]{1,0:T(8,128)S(1)} %collective-permute-done.14.refs_5_), channel_id=1, source_target_pairs={{0,8},{1,9},{2,10},{3,11},{4,60},{5,61},{6,62},{7,63},{8,0},{9,1},... | collective-permute-start | bytes 1966088 | tf_op jit(solution)/shard_map/tz2/ppermute | solution.py:63
  61.7 13.4 %collective-permute-start.18 = (f32[1280,128]{1,0:T(8,128)S(1)}, f32[1280,128]{1,0:T(8,128)S(1)}, u32[]{:S(2)}, u32[]{:S(2)}) collective-permute-start(f32[1280,128]{1,0:T(8,128)S(1)} %get-tuple-element.81.refs_0_), channel_id=1, source_target_pairs={{0,3},{1,2},{2,1},{3,0},{4,5},{5,4},{6,7},{7,6},{8,11},{9,10},{10,... | collective-permute-start | bytes 1966088 | tf_op jit(solution)/shard_map/hx1/ppermute | solution.py:63
  72.3 20.8 %copy-start.6 = (f32[1280,128]{1,0:T(8,128)}, f32[1280,128]{1,0:T(8,128)S(1)}, u32[]{:S(2)}) copy-start(f32[1280,128]{1,0:T(8,128)S(1)} %collective-permute-done.17.refs_6_) | copy-start | bytes 1966084
  75.1 18.0 %copy-start.7 = (f32[1280,128]{1,0:T(8,128)}, f32[1280,128]{1,0:T(8,128)S(1)}, u32[]{:S(2)}) copy-start(f32[1280,128]{1,0:T(8,128)S(1)} %collective-permute-done.18.refs_2_) | copy-start | bytes 1966084
  75.1 18.0 %copy-start.8 = (f32[3840,128]{1,0:T(8,128)}, f32[3840,128]{1,0:T(8,128)S(1)}, u32[]{:S(2)}) copy-start(f32[3840,128]{1,0:T(8,128)S(1)} %collective-permute-done.19.refs_8_) | copy-start | bytes 5898244
  75.3 17.9 %collective-permute-start.22 = (f32[3840,128]{1,0:T(8,128)S(1)}, f32[3840,128]{1,0:T(8,128)}, u32[]{:S(2)}, u32[]{:S(2)}) collective-permute-start(f32[3840,128]{1,0:T(8,128)S(1)} %pad_maximum_fusion.1), channel_id=1, source_target_pairs={{0,4},{1,5},{2,6},{3,7},{4,0},{5,1},{6,2},{7,3},{8,12},{9,13},{10,... | collective-permute-start | bytes 5898248 | tf_op jit(solution)/shard_map/swap2/ppermute | solution.py:63
  75.4 17.8 %collective-permute-start.20 = (f32[1280,128]{1,0:T(8,128)S(1)}, f32[1280,128]{1,0:T(8,128)S(1)}, u32[]{:S(2)}, u32[]{:S(2)}) collective-permute-start(f32[1280,128]{1,0:T(8,128)S(1)} %collective-permute-done.17.refs_6_), channel_id=1, source_target_pairs={{0,56},{1,57},{2,58},{3,59},{4,12},{5,13},{6,14},{7,15},{8,16},{9,... | collective-permute-start | bytes 1966088 | tf_op jit(solution)/shard_map/tz3/ppermute | solution.py:63
  79.1 14.0 %collective-permute-start.21 = (f32[1280,128]{1,0:T(8,128)S(1)}, f32[1280,128]{1,0:T(8,128)S(1)}, u32[]{:S(2)}, u32[]{:S(2)}) collective-permute-start(f32[1280,128]{1,0:T(8,128)S(1)} %collective-permute-done.15.refs_1_), channel_id=1, source_target_pairs={{0,3},{1,2},{2,1},{3,0},{4,5},{5,4},{6,7},{7,6},{8,11},{9,10},{10,... | collective-permute-start | bytes 1966088 | tf_op jit(solution)/shard_map/hx2/ppermute | solution.py:63
  93.1 3.2 %copy-start.9 = (f32[1280,128]{1,0:T(8,128)}, f32[1280,128]{1,0:T(8,128)S(1)}, u32[]{:S(2)}) copy-start(f32[1280,128]{1,0:T(8,128)S(1)} %collective-permute-done.20.refs_7_) | copy-start | bytes 1966084
  93.1 3.1 %copy-start.10 = (f32[1280,128]{1,0:T(8,128)}, f32[1280,128]{1,0:T(8,128)S(1)}, u32[]{:S(2)}) copy-start(f32[1280,128]{1,0:T(8,128)S(1)} %collective-permute-done.21.refs_3_) | copy-start | bytes 1966084
  93.2 2.2 %collective-permute-start.23 = (f32[1280,128]{1,0:T(8,128)S(1)}, f32[1280,128]{1,0:T(8,128)S(1)}, u32[]{:S(2)}, u32[]{:S(2)}) collective-permute-start(f32[1280,128]{1,0:T(8,128)S(1)} %collective-permute-done.20.refs_7_), channel_id=1, source_target_pairs={{0,4},{1,5},{2,6},{3,7},{4,0},{5,1},{6,2},{7,3},{8,12},{9,13},{10,... | collective-permute-start | bytes 1966088 | tf_op jit(solution)/shard_map/swap_t3/ppermute | solution.py:63
  93.3 3.0 %collective-permute-start.24 = (f32[1280,128]{1,0:T(8,128)S(1)}, f32[1280,128]{1,0:T(8,128)S(1)}, u32[]{:S(2)}, u32[]{:S(2)}) collective-permute-start(f32[1280,128]{1,0:T(8,128)S(1)} %collective-permute-done.21.refs_3_), channel_id=1, source_target_pairs={{0,4},{1,5},{2,6},{3,7},{4,0},{5,1},{6,2},{7,3},{8,12},{9,13},{10,... | collective-permute-start | bytes 1966088 | tf_op jit(solution)/shard_map/swap_h2/ppermute | solution.py:63
  95.4 0.9 copy-start.11
  96.3 0.9 copy-start.12
  119.5 0.7 copy-start.1

commit v4 on v3

--- a/solution.py
+++ b/solution.py
@@ -217,7 +217,7 @@
     return jnp.where(lane < 64, main, jnp.where(lane < 80, rest, 0.0))
 
 
-def bottom_kernel(near, near_other, pair, last, out, below, inverse, sems):
+def bottom_kernel(near, other_one, other_two, pair, last, out, below, inverse, sems):
     _, z, c, x = here()
     copies = []
     for slot, panel in enumerate(b_panels()):
@@ -226,10 +226,11 @@
         for half in range(2):
             start = slot % 2 * 3 * Q + half * Q
             copies.append((source.at[pl.ds(start, Q), :], below.at[half, pl.ds(column, Q), :]))
-    for core, source in enumerate((near, near_other)):
-        for slot in range(4):
-            lane = (z & 3 ^ slot) * 2 + (c ^ core)
-            copies.append((source.at[pl.ds(slot * 104, 104), :], inverse.at[lane]))
+    for slot in range(4):
+        lane = (z & 3 ^ slot) * 2
+        other = other_one if slot < 2 else other_two
+        copies.append((near.at[pl.ds(slot * 104, 104), :], inverse.at[lane + c]))
+        copies.append((other.at[pl.ds(slot % 2 * 104, 104), :], inverse.at[lane + 1 - c]))
     run(copies, sems)
     squares = jnp.zeros((Q, 128), F32)
     mixed = jnp.zeros((Q, 256), F32)
@@ -243,9 +244,10 @@
     squares = jnp.sum(squares, 1, keepdims=True)
     lane = lax.broadcasted_iota(jnp.int32, (Q, 256), 1)
     mixed = jnp.where(lane == 240, squares, mixed)
-    out[...] = jnp.zeros(out.shape, F32)
     for part in range(8):
-        out[part, 0:20, :] = mixed[part * 20 : part * 20 + 20]
+        rows = slice(part * 20, part * 20 + 20)
+        out[part, 0:20, :] = mixed[rows, 0:128]
+        out[part, 20:40, :] = mixed[rows, 128:256]
 
 
 def start_copies(sources, stage, sems):
@@ -307,10 +309,11 @@
     top_blocks = top_rows(z, c, x) + top_rows(z, 1 - c, x)
     pieces = []
     for part in range(8):
-        pieces.append((mixed[part, :, 0:128], 0, 128, part * 240))
-        pieces.append((mixed[part, :, 128:256], 0, 112, part * 240 + 128))
+        tail = jnp.concatenate([mixed[part, 20:40, :], jnp.zeros((4, 128), F32)], 0)
+        pieces.append((mixed[part, 0:24, :], 0, 128, part * 240))
+        pieces.append((tail, 0, 112, part * 240 + 128))
     path = place(pieces, 3 * W)
-    squares = jnp.concatenate([mixed[0, :, 240:241], jnp.zeros((40, 1), F32)], 0)
+    squares = jnp.concatenate([mixed[0, 20:40, 112:113], jnp.zeros((44, 1), F32)], 0)
 
     def products(cols):
         left = halves(cols)
@@ -409,63 +412,62 @@
     y2 = send("y2", step_y(2), y_chunk)
     hz = send("hz0", step_z(0), h_chunk)
     bx = send("bx0", step_x(0), b_chunk)
-    y1, y2, y3, hz, bx = together(y1, y2, y3, hz, bx)
     (t_chunk,) = call(merge_kernel, [(Q, 128)], [VMEM] * 4)(y_chunk, y1, y2, y3)
-    h_pair, b_pair = join(h_chunk, hz), join(b_chunk, bx)
-    t_chunk, h_pair, b_pair = together(t_chunk, h_pair, b_pair)
+    h_pair, b_pair = join(h_chunk, hz), tie(join(b_chunk, bx), hz, y1)
 
     tx = send("tx0", step_x(0), t_chunk)
     h1 = send("hz1", step_z(1), h_pair)
     b_last = send("bx1", step_x(1), b_pair)
-    tx, h1, b_last = together(tx, h1, b_last)
-    t_pair = join(t_chunk, tx)
     (near,) = call(
         pick_kernel,
         [(104, 128)],
         [HBM] * 2,
         [pltpu.VMEM((Q, 128), F32), pltpu.SemaphoreType.DMA((4,))],
     )(b_pair, b_last)
+    got = send("near1", step_near(1), near)
+    tx, h1, got = together(tx, h1, got)
+    t_pair, near = join(t_chunk, tx), join(near, got)
     t_pair, h1, near = together(t_pair, h1, near)
 
     tx = send("tx1", step_x(1), t_pair)
     h2 = send("hz2", step_z(0), h1)
-    got = send("near1", step_near(1), near)
-    tx, h2, got = together(tx, h2, got)
+    got = send("near2", step_near(2), near)
+    other_one = send("near_swap1", SWAP, near)
+    tx, h2, got, other_one = together(tx, h2, got, other_one)
     t_line, near = join(t_pair, tx), join(near, got)
-    t_line, near, h2 = together(t_line, near, h2)
+    t_line, near, got, h2 = together(t_line, near, got, h2)
 
     tz = send("tz0", step_z(0), t_line)
     h3 = send("hz3", step_z(1), h2)
-    got = send("near2", step_near(2), near)
-    tz, h3, got = together(tz, h3, got)
-    t0, near = join(t_line, tz), join(near, got)
+    other_two = send("near_swap2", SWAP, got)
+    tz, h3, other_two = together(tz, h3, other_two)
+    t0 = join(t_line, tz)
     h_rows = jnp.concatenate([h_pair, h1, h2, h3], 0)
-    t0, h_rows, near = together(t0, h_rows, near)
+    t0, h_rows, other_two = together(t0, h_rows, other_two)
 
     t1 = send("tz1", step_z(1), t0)
     hx = send("hx0", step_x(0), h_rows)
-    near_other = send("near_swap", SWAP, near)
-    t1, hx, near_other, h_rows, t0 = together(t1, hx, near_other, h_rows, t0)
-
-    t2 = send("tz2", step_z(0), t1)
-    h1 = send("hx1", step_x(1), h_rows)
-    swap1 = send("swap1", SWAP, jnp.concatenate([t0, h_rows, t1], 0))
     (mixed,) = call(
         bottom_kernel,
-        [(8, 24, 256)],
-        [HBM] * 4,
+        [(8, 40, 128)],
+        [HBM] * 5,
         [
             pltpu.VMEM((2, W, 128), F32),
             pltpu.VMEM((8, 104, 128), F32),
             pltpu.SemaphoreType.DMA((16,)),
         ],
-    )(near, near_other, b_pair, b_last)
+    )(near, other_one, other_two, b_pair, b_last)
+    t1, hx, mixed, h_rows, t0 = together(t1, hx, mixed, h_rows, t0)
+
+    t2 = send("tz2", step_z(0), t1)
+    h1 = send("hx1", step_x(1), h_rows)
+    swap1 = send("swap1", SWAP, jnp.concatenate([t0, h_rows, t1], 0))
+    mixed = lax.all_to_all(mixed, ("deep", "core"), 0, 0, tiled=True)
     t2, h1, swap1, mixed, hx = together(t2, h1, swap1, mixed, hx)
 
     t3 = send("tz3", step_z(1), t2)
     h2 = send("hx2", step_x(1), hx)
     swap2 = send("swap2", SWAP, jnp.concatenate([t2, hx, h1], 0))
-    mixed = lax.all_to_all(mixed, ("deep", "core"), 0, 0, tiled=True)
     t3, h2, mixed, swap2 = together(t3, h2, mixed, swap2)
 
     u3 = send("swap_t3", SWAP, t3)

time: 121 us -> 114 us (0.942); the launches traced: 121 us -> 112 us
  starting transfers between devices: 40.5 us -> 33.9 us
  blocking collectives: 22.9 us -> 19.9 us
    ppermute x25 -> x26, starting transfers between devices: 40.5 us -> 33.9 us  [permute(): return lax.ppermute(value, ALL, pairs)]
    all_gather x1, blocking collectives: 10.9 us -> 9.19 us  [shards(): gathered = lax.all_gather(variances, 'panel', axis=0, tiled=True)]
    all_to_all x1, blocking collectives: 12 us -> 10.8 us  [shards(): mixed = lax.all_to_all(mixed, ('deep', 'core'), 0, 0, tiled=True)]
    ppermute x25 -> x26, waiting for transfers between devices: 35 us -> 36.2 us  [permute(): return lax.ppermute(value, ALL, pairs)]
    unnamed x26 -> x30, local copies, waits for them, and re-layouts: 2.43 us -> 2.48 us
  transfers between devices with their start and end apart: 25 -> 26, of which waited for: 14 -> 13; matrix products, arithmetic and copies ran while one was open for 0% -> 2% of each run, Pallas kernels for 2% -> 2%
where the time goes in v4:
time: 114 us; the launch traced here: 112 us
  waiting for transfers between devices  36.2 us (32%)
  starting transfers between devices  33.9 us (30%)
  blocking collectives  19.9 us (17%)
  Pallas kernels  16.7 us (15%)
  local copies, waits for them, and re-layouts  2.49 us (2%)
  other arithmetic  2.23 us (2%)
    ppermute x26, waiting for transfers between devices, permute(): return lax.ppermute(value, ALL, pairs)  36.2 us
    ppermute x26, starting transfers between devices, permute(): return lax.ppermute(value, ALL, pairs)  33.9 us
    pallas_call x1, Pallas kernels, shards(): call(chain_kernel, [(1, 128)], [VMEM] + [HBM] * 12, [pltpu.VMEM((8, 8 * Q...  11.4 us
    all_to_all x1, blocking collectives, shards(): mixed = lax.all_to_all(mixed, ('deep', 'core'), 0, 0, tiled=True)  10.8 us
    all_gather x1, blocking collectives, shards(): gathered = lax.all_gather(variances, 'panel', axis=0, tiled=True)  9.19 us
    unnamed x30, local copies, waits for them, and re-layouts  2.48 us
  transfers between devices with their start and end apart: 26, of which 13 were waited for; matrix products, arithmetic and copies ran while one was open for 2% of the time, Pallas kernels for 2%

profile of v4, /device:TPU:2, one launch (start us, length us, event | category | flops | bytes accessed | tf_op | source)
XLA Modules:
  0.0 112.4 jit_solution(8358469768337864380)
XLA Ops:
  0.6 2.0 %shard_map.102 = (f32[160,128]{1,0:T(8,128)}, f32[160,128]{1,0:T(8,128)}, f32[480,128]{1,0:T(8,128)}) custom-call(f32[40,160]{1,0:T(8,128)} %d2.1, f32[80,160]{1,0:T(8,128)} %b2.1, f32[160,240]{1,0:T(8,128)} %bitcast.9, f32[80,160]{1,0:T(8,128)} %d3.1, f32[20,160]{1,0:T(8,128)} %d1.1, f32[20,160]{1,0:T(8,128)} %b1.1, f32[10,160]{1,0:T(8,128)} %d0.1), custom_call_target="tpu_custom_call" | custom-call | tf_op jit(solution)/shard_map/pallas_call | solution.py:395
  2.7 2.4 %collective-permute-start.6 = (f32[480,128]{1,0:T(8,128)}, f32[480,128]{1,0:T(8,128)S(1)}, u32[]{:S(2)}, u32[]{:S(2)}) collective-permute-start(f32[480,128]{1,0:T(8,128)} %get-tuple-element.48), channel_id=1, source_target_pairs={{0,1},{1,0},{2,3},{3,2},{4,7},{5,6},{6,5},{7,4},{8,9},{9,8},{10,11... | collective-permute-start | bytes 737288 | tf_op jit(solution)/shard_map/bx0/ppermute | solution.py:63
  5.0 0.0 collective-permute-start
  5.0 1.8 %collective-permute-start.4 = (f32[160,128]{1,0:T(8,128)}, f32[160,128]{1,0:T(8,128)S(1)}, u32[]{:S(2)}, u32[]{:S(2)}) collective-permute-start(f32[160,128]{1,0:T(8,128)} %get-tuple-element.47), channel_id=1, source_target_pairs={{0,8},{1,9},{2,10},{3,11},{4,60},{5,61},{6,62},{7,63},{8,0},{9,1},... | collective-permute-start | bytes 245768 | tf_op jit(solution)/shard_map/hz0/ppermute | solution.py:63
  6.8 2.6 %collective-permute-done.6 = f32[480,128]{1,0:T(8,128)S(1)} collective-permute-done((f32[480,128]{1,0:T(8,128)}, f32[480,128]{1,0:T(8,128)S(1)}, u32[]{:S(2)}, u32[]{:S(2)}) %collective-permute-start.6) | collective-permute-done | bytes 245792 | tf_op jit(solution)/shard_map/bx0/ppermute | solution.py:63
  9.4 1.0 pad_maximum_fusion.3.pair
  10.4 0.5 collective-permute-done.one
  10.9 0.0 collective-permute-done.4
  10.9 0.8 collective-permute-start.7
  11.7 3.2 %collective-permute-start.1 = (f32[160,128]{1,0:T(8,128)}, f32[160,128]{1,0:T(8,128)S(1)}, u32[]{:S(2)}, u32[]{:S(2)}) collective-permute-start(f32[160,128]{1,0:T(8,128)} %get-tuple-element.46.own), channel_id=1, source_target_pairs={{0,128},{1,129},{2,130},{3,131},{4,132},{5,133},{6,134},{7,135},{8... | collective-permute-start | bytes 245768 | tf_op jit(solution)/shard_map/y2/ppermute | solution.py:63
  14.9 1.1 collective-permute-start.2
  16.0 0.9 pad_maximum_fusion.6
  16.9 5.9 %collective-permute-start.5 = (f32[320,128]{1,0:T(8,128)S(1)}, f32[320,128]{1,0:T(8,128)S(1)}, u32[]{:S(2)}, u32[]{:S(2)}) collective-permute-start(f32[320,128]{1,0:T(8,128)S(1)} %pad_maximum_fusion.6), channel_id=1, source_target_pairs={{0,56},{1,57},{2,58},{3,59},{4,12},{5,13},{6,14},{7,15},{8,16},{9,... | collective-permute-start | bytes 491528 | tf_op jit(solution)/shard_map/hz1/ppermute | solution.py:63
  22.8 0.0 collective-permute-done.1.two
  22.8 0.0 collective-permute-done.2.three
  22.8 0.9 copy-done
  23.7 0.2 shard_map.103
  24.0 1.9 %collective-permute-start.3 = (f32[160,128]{1,0:T(8,128)S(1)}, f32[160,128]{1,0:T(8,128)S(1)}, u32[]{:S(2)}, u32[]{:S(2)}) collective-permute-start(f32[160,128]{1,0:T(8,128)S(1)} %shard_map.103), channel_id=1, source_target_pairs={{0,1},{1,0},{2,3},{3,2},{4,7},{5,6},{6,5},{7,4},{8,9},{9,8},{10,11... | collective-permute-start | bytes 245768 | tf_op jit(solution)/shard_map/tx0/ppermute | solution.py:63
  25.8 0.0 collective-permute-done.7.last
  25.8 0.2 shard_map.104
  26.1 0.1 collective-permute-start.8
  26.2 2.3 %collective-permute-done.3 = f32[160,128]{1,0:T(8,128)S(1)} collective-permute-done((f32[160,128]{1,0:T(8,128)S(1)}, f32[160,128]{1,0:T(8,128)S(1)}, u32[]{:S(2)}, u32[]{:S(2)}) %collective-permute-start.3) | collective-permute-done | bytes 81952 | tf_op jit(solution)/shard_map/tx0/ppermute | solution.py:63
  28.5 0.0 collective-permute-done.5
  28.5 1.8 %collective-permute-done.8 = f32[104,128]{1,0:T(8,128)S(1)} collective-permute-done((f32[104,128]{1,0:T(8,128)S(1)}, f32[104,128]{1,0:T(8,128)S(1)}, u32[]{:S(2)}, u32[]{:S(2)}) %collective-permute-start.8) | collective-permute-done | bytes 53280 | tf_op jit(solution)/shard_map/near1/ppermute | solution.py:63
  30.3 0.1 collective-permute-start.10
  30.4 0.2 collective-permute-start.9
  30.6 2.4 %collective-permute-start.11 = (f32[208,128]{1,0:T(8,128)S(1)}, f32[208,128]{1,0:T(8,128)S(1)}, u32[]{:S(2)}, u32[]{:S(2)}) collective-permute-start(f32[208,128]{1,0:T(8,128)S(1)} %pad_maximum_fusion.8), channel_id=1, source_target_pairs={{0,16},{1,17},{2,18},{3,19},{4,20},{5,21},{6,22},{7,23},{8,24},{9,... | collective-permute-start | bytes 319496 | tf_op jit(solution)/shard_map/near2/ppermute | solution.py:63
  33.0 0.0 collective-permute-start.12
  33.0 5.5 %collective-permute-done.11 = f32[208,128]{1,0:T(8,128)S(1)} collective-permute-done((f32[208,128]{1,0:T(8,128)S(1)}, f32[208,128]{1,0:T(8,128)S(1)}, u32[]{:S(2)}, u32[]{:S(2)}) %collective-permute-start.11) | collective-permute-done | bytes 106528 | tf_op jit(solution)/shard_map/near2/ppermute | solution.py:63
  38.5 0.0 collective-permute-done.12.other_one
  38.5 0.0 collective-permute-done.10
  38.5 0.0 collective-permute-done.9
  38.5 0.1 collective-permute-start.13
  38.7 2.6 %collective-permute-start.14 = (f32[320,128]{1,0:T(8,128)S(1)}, f32[320,128]{1,0:T(8,128)S(1)}, u32[]{:S(2)}, u32[]{:S(2)}) collective-permute-start(f32[320,128]{1,0:T(8,128)S(1)} %collective-permute-done.10), channel_id=1, source_target_pairs={{0,56},{1,57},{2,58},{3,59},{4,12},{5,13},{6,14},{7,15},{8,16},{9,... | collective-permute-start | bytes 491528 | tf_op jit(solution)/shard_map/hz3/ppermute | solution.py:63
  41.3 0.1 collective-permute-start.15
  41.4 1.3 %collective-permute-done.15.other_two = f32[208,128]{1,0:T(8,128)S(1)} collective-permute-done((f32[208,128]{1,0:T(8,128)S(1)}, f32[208,128]{1,0:T(8,128)S(1)}, u32[]{:S(2)}, u32[]{:S(2)}) %collective-permute-start.15) | collective-permute-done | bytes 106528 | tf_op jit(solution)/shard_map/near_swap2/ppermute | solution.py:63
  42.7 4.4 %collective-permute-done.14 = f32[320,128]{1,0:T(8,128)S(1)} collective-permute-done((f32[320,128]{1,0:T(8,128)S(1)}, f32[320,128]{1,0:T(8,128)S(1)}, u32[]{:S(2)}, u32[]{:S(2)}) %collective-permute-start.14) | collective-permute-done | bytes 163872 | tf_op jit(solution)/shard_map/hz3/ppermute | solution.py:63
  47.1 0.0 collective-permute-done.13
  47.2 2.0 %collective-permute-start.16 = (f32[1280,128]{1,0:T(8,128)S(1)}, f32[1280,128]{1,0:T(8,128)S(1)}, u32[]{:S(2)}, u32[]{:S(2)}) collective-permute-start(f32[1280,128]{1,0:T(8,128)S(1)} %pad_maximum_fusion.2.refs_4_), channel_id=1, source_target_pairs={{0,56},{1,57},{2,58},{3,59},{4,12},{5,13},{6,14},{7,15},{8,16},{9,... | collective-permute-start | bytes 1966088 | tf_op jit(solution)/shard_map/tz1/ppermute | solution.py:63
  49.2 1.6 %collective-permute-start.17 = (f32[1280,128]{1,0:T(8,128)S(1)}, f32[1280,128]{1,0:T(8,128)S(1)}, u32[]{:S(2)}, u32[]{:S(2)}) collective-permute-start(f32[1280,128]{1,0:T(8,128)S(1)} %constant_dynamic-update-slice_fusion.refs_0_), channel_id=1, source_target_pairs={{0,1},{1,0},{2,3},{3,2},{4,7},{5,6},{6,5},{7,4},{8,9},{9,8},{10,11... | collective-permute-start | bytes 1966088 | tf_op jit(solution)/shard_map/hx0/ppermute | solution.py:63
  50.8 2.3 %shard_map.105 = f32[8,40,128]{2,1,0:T(8,128)S(1)} custom-call(f32[416,128]{1,0:T(8,128)S(1)} %pad_maximum_fusion.5.near, f32[208,128]{1,0:T(8,128)S(1)} %collective-permute-done.12.other_one, f32[208,128]{1,0:T(8,128)S(1)} %collective-permute-done.15.other_two, f32[960,128]{1,0:T(8,128)S(1)} %pad_maximum_fusion.3.pair, ...), custom_call_target="tpu_custom_call" | custom-call | tf_op jit(solution)/shard_map/pallas_call | solution.py:450
  53.0 6.0 %collective-permute-done.16.refs_5_ = f32[1280,128]{1,0:T(8,128)S(1)} collective-permute-done((f32[1280,128]{1,0:T(8,128)S(1)}, f32[1280,128]{1,0:T(8,128)S(1)}, u32[]{:S(2)}, u32[]{:S(2)}) %collective-permute-start.16) | collective-permute-done | bytes 655392 | tf_op jit(solution)/shard_map/tz1/ppermute | solution.py:63
  59.1 0.7 collective-permute-done.17.refs_1_
  59.8 0.1 pad_maximum_fusion
  59.9 0.3 collective-permute-start.20
  60.2 0.1 collective-permute-start.18
  60.3 3.0 %collective-permute-start.19 = (f32[1280,128]{1,0:T(8,128)S(1)}, f32[1280,128]{1,0:T(8,128)S(1)}, u32[]{:S(2)}, u32[]{:S(2)}) collective-permute-start(f32[1280,128]{1,0:T(8,128)S(1)} %constant_dynamic-update-slice_fusion.refs_0_), channel_id=1, source_target_pairs={{0,3},{1,2},{2,1},{3,0},{4,5},{5,4},{6,7},{7,6},{8,11},{9,10},{10,... | collective-permute-start | bytes 1966088 | tf_op jit(solution)/shard_map/hx1/ppermute | solution.py:63
  63.3 10.8 %all_to_all.5.mixed = f32[8,40,128]{2,1,0:T(8,128)} all-to-all(f32[8,40,128]{2,1,0:T(8,128)S(1)} %shard_map.105), channel_id=1, replica_groups=mesh['row'=4,'high'=2,'deep'=4,'core'=2,'panel'=4] {'deep','core'}, dimensions={0} | all-to-all | bytes 327680 | tf_op jit(solution)/shard_map/all_to_all | solution.py:465
  74.1 0.0 collective-permute-done.18.refs_6_
  74.1 0.0 collective-permute-done.20.refs_8_
  74.1 0.1 pad_maximum_fusion.1
  74.2 0.1 collective-permute-start.23
  74.3 1.2 %collective-permute-start.21 = (f32[1280,128]{1,0:T(8,128)S(1)}, f32[1280,128]{1,0:T(8,128)S(1)}, u32[]{:S(2)}, u32[]{:S(2)}) collective-permute-start(f32[1280,128]{1,0:T(8,128)S(1)} %collective-permute-done.18.refs_6_), channel_id=1, source_target_pairs={{0,56},{1,57},{2,58},{3,59},{4,12},{5,13},{6,14},{7,15},{8,16},{9,... | collective-permute-start | bytes 1966088 | tf_op jit(solution)/shard_map/tz3/ppermute | solution.py:63
  75.5 2.6 %collective-permute-start.22 = (f32[1280,128]{1,0:T(8,128)S(1)}, f32[1280,128]{1,0:T(8,128)S(1)}, u32[]{:S(2)}, u32[]{:S(2)}) collective-permute-start(f32[1280,128]{1,0:T(8,128)S(1)} %collective-permute-done.17.refs_1_), channel_id=1, source_target_pairs={{0,3},{1,2},{2,1},{3,0},{4,5},{5,4},{6,7},{7,6},{8,11},{9,10},{10,... | collective-permute-start | bytes 1966088 | tf_op jit(solution)/shard_map/hx2/ppermute | solution.py:63
  78.1 8.1 %collective-permute-done.21.refs_7_ = f32[1280,128]{1,0:T(8,128)S(1)} collective-permute-done((f32[1280,128]{1,0:T(8,128)S(1)}, f32[1280,128]{1,0:T(8,128)S(1)}, u32[]{:S(2)}, u32[]{:S(2)}) %collective-permute-start.21) | collective-permute-done | bytes 655392 | tf_op jit(solution)/shard_map/tz3/ppermute | solution.py:63
  86.2 0.4 collective-permute-done.22.refs_3_
  86.7 0.5 collective-permute-start.25
  87.2 1.6 %collective-permute-done.24.refs_10_ = f32[1280,128]{1,0:T(8,128)S(1)} collective-permute-done((f32[1280,128]{1,0:T(8,128)S(1)}, f32[1280,128]{1,0:T(8,128)S(1)}, u32[]{:S(2)}, u32[]{:S(2)}) %collective-permute-start.24) | collective-permute-done | bytes 655392 | tf_op jit(solution)/shard_map/swap_t3/ppermute | solution.py:63
  88.8 0.9 collective-permute-done.25.refs_11_
  89.7 0.9 copy-done.11
  90.6 11.4 %shard_map.106.own = f32[1,128]{1,0:T(1,128)} custom-call(f32[8,40,128]{2,1,0:T(8,128)} %all_to_all.5.mixed, f32[1280,128]{1,0:T(8,128)} %copy-done.3, f32[1280,128]{1,0:T(8,128)} %copy-done.5, f32[1280,128]{1,0:T(8,128)} %copy-done.7, f32[1280,128]{1,0:T(8,128)} %copy-done.9, f32[1280,128]{1,0:T(8,128)} %copy-done.2, f32[1280,128]{1,0:T(8,128)} %copy-done.4, ...), custom_call_target="tpu_custom_call" | custom-call | tf_op jit(solution)/shard_map/pallas_call | solution.py:476
  102.0 9.2 %all-gather = f32[4,1,128]{2,1,0:T(1,128)S(1)} all-gather(f32[1,1,128]{2,1,0:T(1,128)} %bitcast.8), channel_id=1, replica_groups=mesh['row'=4,'high'=2,'deep'=4,'core'=2,'panel'=4] {'panel'}, dimensions={0}, use_global_device_ids=true | all-gather | bytes 2560 | tf_op jit(solution)/shard_map/all_gather | solution.py:490
  111.2 0.7 copy-done.1
  111.8 0.6 shard_map.107
  (36 shorter events, 0.2 us)
Async XLA Ops:
  2.7 30.3 %copy-start.12 = (f32[160,128]{1,0:T(8,128)S(1)}, f32[160,128]{1,0:T(8,128)}, u32[]{:S(2)}) copy-start(f32[160,128]{1,0:T(8,128)} %get-tuple-element.47) | copy-start | bytes 245764
  2.7 6.7 %collective-permute-start.6 = (f32[480,128]{1,0:T(8,128)}, f32[480,128]{1,0:T(8,128)S(1)}, u32[]{:S(2)}, u32[]{:S(2)}) collective-permute-start(f32[480,128]{1,0:T(8,128)} %get-tuple-element.48), channel_id=1, source_target_pairs={{0,1},{1,0},{2,3},{3,2},{4,7},{5,6},{6,5},{7,4},{8,9},{9,8},{10,11... | collective-permute-start | bytes 737288 | tf_op jit(solution)/shard_map/bx0/ppermute | solution.py:63
  5.0 5.9 %collective-permute-start = (f32[160,128]{1,0:T(8,128)}, f32[160,128]{1,0:T(8,128)S(1)}, u32[]{:S(2)}, u32[]{:S(2)}) collective-permute-start(f32[160,128]{1,0:T(8,128)} %get-tuple-element.46.own), channel_id=1, source_target_pairs={{0,64},{1,65},{2,66},{3,67},{4,68},{5,69},{6,70},{7,71},{8,72},{9,... | collective-permute-start | bytes 245768 | tf_op jit(solution)/shard_map/y1/ppermute | solution.py:63
  5.0 5.9 %collective-permute-start.4 = (f32[160,128]{1,0:T(8,128)}, f32[160,128]{1,0:T(8,128)S(1)}, u32[]{:S(2)}, u32[]{:S(2)}) collective-permute-start(f32[160,128]{1,0:T(8,128)} %get-tuple-element.47), channel_id=1, source_target_pairs={{0,8},{1,9},{2,10},{3,11},{4,60},{5,61},{6,62},{7,63},{8,0},{9,1},... | collective-permute-start | bytes 245768 | tf_op jit(solution)/shard_map/hz0/ppermute | solution.py:63
  10.9 15.0 %collective-permute-start.7 = (f32[960,128]{1,0:T(8,128)S(1)}, f32[960,128]{1,0:T(8,128)S(1)}, u32[]{:S(2)}, u32[]{:S(2)}) collective-permute-start(f32[960,128]{1,0:T(8,128)S(1)} %pad_maximum_fusion.3.pair), channel_id=1, source_target_pairs={{0,3},{1,2},{2,1},{3,0},{4,5},{5,4},{6,7},{7,6},{8,11},{9,10},{10,... | collective-permute-start | bytes 1474568 | tf_op jit(solution)/shard_map/bx1/ppermute | solution.py:63
  11.7 11.1 %collective-permute-start.1 = (f32[160,128]{1,0:T(8,128)}, f32[160,128]{1,0:T(8,128)S(1)}, u32[]{:S(2)}, u32[]{:S(2)}) collective-permute-start(f32[160,128]{1,0:T(8,128)} %get-tuple-element.46.own), channel_id=1, source_target_pairs={{0,128},{1,129},{2,130},{3,131},{4,132},{5,133},{6,134},{7,135},{8... | collective-permute-start | bytes 245768 | tf_op jit(solution)/shard_map/y2/ppermute | solution.py:63
  14.9 7.9 %collective-permute-start.2 = (f32[160,128]{1,0:T(8,128)}, f32[160,128]{1,0:T(8,128)S(1)}, u32[]{:S(2)}, u32[]{:S(2)}) collective-permute-start(f32[160,128]{1,0:T(8,128)} %get-tuple-element.46.own), channel_id=1, source_target_pairs={{0,192},{1,193},{2,194},{3,195},{4,196},{5,197},{6,198},{7,199},{8... | collective-permute-start | bytes 245768 | tf_op jit(solution)/shard_map/y3/ppermute | solution.py:63
  16.9 11.6 %collective-permute-start.5 = (f32[320,128]{1,0:T(8,128)S(1)}, f32[320,128]{1,0:T(8,128)S(1)}, u32[]{:S(2)}, u32[]{:S(2)}) collective-permute-start(f32[320,128]{1,0:T(8,128)S(1)} %pad_maximum_fusion.6), channel_id=1, source_target_pairs={{0,56},{1,57},{2,58},{3,59},{4,12},{5,13},{6,14},{7,15},{8,16},{9,... | collective-permute-start | bytes 491528 | tf_op jit(solution)/shard_map/hz1/ppermute | solution.py:63
  22.8 0.9 copy-start
  24.0 4.5 %collective-permute-start.3 = (f32[160,128]{1,0:T(8,128)S(1)}, f32[160,128]{1,0:T(8,128)S(1)}, u32[]{:S(2)}, u32[]{:S(2)}) collective-permute-start(f32[160,128]{1,0:T(8,128)S(1)} %shard_map.103), channel_id=1, source_target_pairs={{0,1},{1,0},{2,3},{3,2},{4,7},{5,6},{6,5},{7,4},{8,9},{9,8},{10,11... | collective-permute-start | bytes 245768 | tf_op jit(solution)/shard_map/tx0/ppermute | solution.py:63
  26.1 4.2 %collective-permute-start.8 = (f32[104,128]{1,0:T(8,128)S(1)}, f32[104,128]{1,0:T(8,128)S(1)}, u32[]{:S(2)}, u32[]{:S(2)}) collective-permute-start(f32[104,128]{1,0:T(8,128)S(1)} %shard_map.104), channel_id=1, source_target_pairs={{0,8},{1,9},{2,10},{3,11},{4,12},{5,13},{6,14},{7,15},{8,0},{9,1},... | collective-permute-start | bytes 159752 | tf_op jit(solution)/shard_map/near1/ppermute | solution.py:63
  30.3 8.1 %collective-permute-start.10 = (f32[320,128]{1,0:T(8,128)S(1)}, f32[320,128]{1,0:T(8,128)S(1)}, u32[]{:S(2)}, u32[]{:S(2)}) collective-permute-start(f32[320,128]{1,0:T(8,128)S(1)} %collective-permute-done.5), channel_id=1, source_target_pairs={{0,8},{1,9},{2,10},{3,11},{4,60},{5,61},{6,62},{7,63},{8,0},{9,1},... | collective-permute-start | bytes 491528 | tf_op jit(solution)/shard_map/hz2/ppermute | solution.py:63
  30.4 8.1 %collective-permute-start.9 = (f32[320,128]{1,0:T(8,128)S(1)}, f32[320,128]{1,0:T(8,128)S(1)}, u32[]{:S(2)}, u32[]{:S(2)}) collective-permute-start(f32[320,128]{1,0:T(8,128)S(1)} %pad_maximum_fusion.7), channel_id=1, source_target_pairs={{0,3},{1,2},{2,1},{3,0},{4,5},{5,4},{6,7},{7,6},{8,11},{9,10},{10,... | collective-permute-start | bytes 491528 | tf_op jit(solution)/shard_map/tx1/ppermute | solution.py:63
  30.6 7.9 %collective-permute-start.11 = (f32[208,128]{1,0:T(8,128)S(1)}, f32[208,128]{1,0:T(8,128)S(1)}, u32[]{:S(2)}, u32[]{:S(2)}) collective-permute-start(f32[208,128]{1,0:T(8,128)S(1)} %pad_maximum_fusion.8), channel_id=1, source_target_pairs={{0,16},{1,17},{2,18},{3,19},{4,20},{5,21},{6,22},{7,23},{8,24},{9,... | collective-permute-start | bytes 319496 | tf_op jit(solution)/shard_map/near2/ppermute | solution.py:63
  33.0 5.5 %collective-permute-start.12 = (f32[208,128]{1,0:T(8,128)S(1)}, f32[208,128]{1,0:T(8,128)S(1)}, u32[]{:S(2)}, u32[]{:S(2)}) collective-permute-start(f32[208,128]{1,0:T(8,128)S(1)} %pad_maximum_fusion.8), channel_id=1, source_target_pairs={{0,4},{1,5},{2,6},{3,7},{4,0},{5,1},{6,2},{7,3},{8,12},{9,13},{10,... | collective-permute-start | bytes 319496 | tf_op jit(solution)/shard_map/near_swap1/ppermute | solution.py:63
  38.5 8.6 %collective-permute-start.13 = (f32[640,128]{1,0:T(8,128)S(1)}, f32[640,128]{1,0:T(8,128)S(1)}, u32[]{:S(2)}, u32[]{:S(2)}) collective-permute-start(f32[640,128]{1,0:T(8,128)S(1)} %pad_maximum_fusion.4), channel_id=1, source_target_pairs={{0,8},{1,9},{2,10},{3,11},{4,60},{5,61},{6,62},{7,63},{8,0},{9,1},... | collective-permute-start | bytes 983048 | tf_op jit(solution)/shard_map/tz0/ppermute | solution.py:63
  38.7 8.4 %collective-permute-start.14 = (f32[320,128]{1,0:T(8,128)S(1)}, f32[320,128]{1,0:T(8,128)S(1)}, u32[]{:S(2)}, u32[]{:S(2)}) collective-permute-start(f32[320,128]{1,0:T(8,128)S(1)} %collective-permute-done.10), channel_id=1, source_target_pairs={{0,56},{1,57},{2,58},{3,59},{4,12},{5,13},{6,14},{7,15},{8,16},{9,... | collective-permute-start | bytes 491528 | tf_op jit(solution)/shard_map/hz3/ppermute | solution.py:63
  41.3 1.4 %collective-permute-start.15 = (f32[208,128]{1,0:T(8,128)S(1)}, f32[208,128]{1,0:T(8,128)S(1)}, u32[]{:S(2)}, u32[]{:S(2)}) collective-permute-start(f32[208,128]{1,0:T(8,128)S(1)} %collective-permute-done.11), channel_id=1, source_target_pairs={{0,4},{1,5},{2,6},{3,7},{4,0},{5,1},{6,2},{7,3},{8,12},{9,13},{10,... | collective-permute-start | bytes 319496 | tf_op jit(solution)/shard_map/near_swap2/ppermute | solution.py:63
  47.2 12.8 %copy-start.2 = (f32[1280,128]{1,0:T(8,128)}, f32[1280,128]{1,0:T(8,128)S(1)}, u32[]{:S(2)}) copy-start(f32[1280,128]{1,0:T(8,128)S(1)} %pad_maximum_fusion.2.refs_4_) | copy-start | bytes 1966084
  47.2 13.1 %copy-start.3 = (f32[1280,128]{1,0:T(8,128)}, f32[1280,128]{1,0:T(8,128)S(1)}, u32[]{:S(2)}) copy-start(f32[1280,128]{1,0:T(8,128)S(1)} %constant_dynamic-update-slice_fusion.refs_0_) | copy-start | bytes 1966084
  47.2 11.9 %collective-permute-start.16 = (f32[1280,128]{1,0:T(8,128)S(1)}, f32[1280,128]{1,0:T(8,128)S(1)}, u32[]{:S(2)}, u32[]{:S(2)}) collective-permute-start(f32[1280,128]{1,0:T(8,128)S(1)} %pad_maximum_fusion.2.refs_4_), channel_id=1, source_target_pairs={{0,56},{1,57},{2,58},{3,59},{4,12},{5,13},{6,14},{7,15},{8,16},{9,... | collective-permute-start | bytes 1966088 | tf_op jit(solution)/shard_map/tz1/ppermute | solution.py:63
  49.2 10.6 %collective-permute-start.17 = (f32[1280,128]{1,0:T(8,128)S(1)}, f32[1280,128]{1,0:T(8,128)S(1)}, u32[]{:S(2)}, u32[]{:S(2)}) collective-permute-start(f32[1280,128]{1,0:T(8,128)S(1)} %constant_dynamic-update-slice_fusion.refs_0_), channel_id=1, source_target_pairs={{0,1},{1,0},{2,3},{3,2},{4,7},{5,6},{6,5},{7,4},{8,9},{9,8},{10,11... | collective-permute-start | bytes 1966088 | tf_op jit(solution)/shard_map/hx0/ppermute | solution.py:63
  59.1 15.0 %copy-start.4 = (f32[1280,128]{1,0:T(8,128)}, f32[1280,128]{1,0:T(8,128)S(1)}, u32[]{:S(2)}) copy-start(f32[1280,128]{1,0:T(8,128)S(1)} %collective-permute-done.16.refs_5_) | copy-start | bytes 1966084
  59.8 15.8 %copy-start.5 = (f32[1280,128]{1,0:T(8,128)}, f32[1280,128]{1,0:T(8,128)S(1)}, u32[]{:S(2)}) copy-start(f32[1280,128]{1,0:T(8,128)S(1)} %collective-permute-done.17.refs_1_) | copy-start | bytes 1966084
  59.9 14.2 %collective-permute-start.20 = (f32[3840,128]{1,0:T(8,128)S(1)}, f32[3840,128]{1,0:T(8,128)}, u32[]{:S(2)}, u32[]{:S(2)}) collective-permute-start(f32[3840,128]{1,0:T(8,128)S(1)} %pad_maximum_fusion), channel_id=1, source_target_pairs={{0,4},{1,5},{2,6},{3,7},{4,0},{5,1},{6,2},{7,3},{8,12},{9,13},{10,... | collective-permute-start | bytes 5898248 | tf_op jit(solution)/shard_map/swap1/ppermute | solution.py:63
  60.2 13.9 %collective-permute-start.18 = (f32[1280,128]{1,0:T(8,128)S(1)}, f32[1280,128]{1,0:T(8,128)S(1)}, u32[]{:S(2)}, u32[]{:S(2)}) collective-permute-start(f32[1280,128]{1,0:T(8,128)S(1)} %collective-permute-done.16.refs_5_), channel_id=1, source_target_pairs={{0,8},{1,9},{2,10},{3,11},{4,60},{5,61},{6,62},{7,63},{8,0},{9,1},... | collective-permute-start | bytes 1966088 | tf_op jit(solution)/shard_map/tz2/ppermute | solution.py:63
  60.3 13.8 %collective-permute-start.19 = (f32[1280,128]{1,0:T(8,128)S(1)}, f32[1280,128]{1,0:T(8,128)S(1)}, u32[]{:S(2)}, u32[]{:S(2)}) collective-permute-start(f32[1280,128]{1,0:T(8,128)S(1)} %constant_dynamic-update-slice_fusion.refs_0_), channel_id=1, source_target_pairs={{0,3},{1,2},{2,1},{3,0},{4,5},{5,4},{6,7},{7,6},{8,11},{9,10},{10,... | collective-permute-start | bytes 1966088 | tf_op jit(solution)/shard_map/hx1/ppermute | solution.py:63
  74.1 15.6 %copy-start.6 = (f32[1280,128]{1,0:T(8,128)}, f32[1280,128]{1,0:T(8,128)S(1)}, u32[]{:S(2)}) copy-start(f32[1280,128]{1,0:T(8,128)S(1)} %collective-permute-done.18.refs_6_) | copy-start | bytes 1966084
  74.1 15.6 %copy-start.7 = (f32[1280,128]{1,0:T(8,128)}, f32[1280,128]{1,0:T(8,128)S(1)}, u32[]{:S(2)}) copy-start(f32[1280,128]{1,0:T(8,128)S(1)} %collective-permute-done.19.refs_2_) | copy-start | bytes 1966084
  74.2 12.4 %collective-permute-start.23 = (f32[3840,128]{1,0:T(8,128)S(1)}, f32[3840,128]{1,0:T(8,128)}, u32[]{:S(2)}, u32[]{:S(2)}) collective-permute-start(f32[3840,128]{1,0:T(8,128)S(1)} %pad_maximum_fusion.1), channel_id=1, source_target_pairs={{0,4},{1,5},{2,6},{3,7},{4,0},{5,1},{6,2},{7,3},{8,12},{9,13},{10,... | collective-permute-start | bytes 5898248 | tf_op jit(solution)/shard_map/swap2/ppermute | solution.py:63
  74.3 11.9 %collective-permute-start.21 = (f32[1280,128]{1,0:T(8,128)S(1)}, f32[1280,128]{1,0:T(8,128)S(1)}, u32[]{:S(2)}, u32[]{:S(2)}) collective-permute-start(f32[1280,128]{1,0:T(8,128)S(1)} %collective-permute-done.18.refs_6_), channel_id=1, source_target_pairs={{0,56},{1,57},{2,58},{3,59},{4,12},{5,13},{6,14},{7,15},{8,16},{9,... | collective-permute-start | bytes 1966088 | tf_op jit(solution)/shard_map/tz3/ppermute | solution.py:63
  75.5 11.1 %collective-permute-start.22 = (f32[1280,128]{1,0:T(8,128)S(1)}, f32[1280,128]{1,0:T(8,128)S(1)}, u32[]{:S(2)}, u32[]{:S(2)}) collective-permute-start(f32[1280,128]{1,0:T(8,128)S(1)} %collective-permute-done.17.refs_1_), channel_id=1, source_target_pairs={{0,3},{1,2},{2,1},{3,0},{4,5},{5,4},{6,7},{7,6},{8,11},{9,10},{10,... | collective-permute-start | bytes 1966088 | tf_op jit(solution)/shard_map/hx2/ppermute | solution.py:63
  86.2 3.5 %copy-start.8 = (f32[1280,128]{1,0:T(8,128)}, f32[1280,128]{1,0:T(8,128)S(1)}, u32[]{:S(2)}) copy-start(f32[1280,128]{1,0:T(8,128)S(1)} %collective-permute-done.21.refs_7_) | copy-start | bytes 1966084
  86.7 3.1 %copy-start.9 = (f32[1280,128]{1,0:T(8,128)}, f32[1280,128]{1,0:T(8,128)S(1)}, u32[]{:S(2)}) copy-start(f32[1280,128]{1,0:T(8,128)S(1)} %collective-permute-done.22.refs_3_) | copy-start | bytes 1966084
  86.7 2.1 %collective-permute-start.24 = (f32[1280,128]{1,0:T(8,128)S(1)}, f32[1280,128]{1,0:T(8,128)S(1)}, u32[]{:S(2)}, u32[]{:S(2)}) collective-permute-start(f32[1280,128]{1,0:T(8,128)S(1)} %collective-permute-done.21.refs_7_), channel_id=1, source_target_pairs={{0,4},{1,5},{2,6},{3,7},{4,0},{5,1},{6,2},{7,3},{8,12},{9,13},{10,... | collective-permute-start | bytes 1966088 | tf_op jit(solution)/shard_map/swap_t3/ppermute | solution.py:63
  86.7 3.0 %collective-permute-start.25 = (f32[1280,128]{1,0:T(8,128)S(1)}, f32[1280,128]{1,0:T(8,128)S(1)}, u32[]{:S(2)}, u32[]{:S(2)}) collective-permute-start(f32[1280,128]{1,0:T(8,128)S(1)} %collective-permute-done.22.refs_3_), channel_id=1, source_target_pairs={{0,4},{1,5},{2,6},{3,7},{4,0},{5,1},{6,2},{7,3},{8,12},{9,13},{10,... | collective-permute-start | bytes 1966088 | tf_op jit(solution)/shard_map/swap_h2/ppermute | solution.py:63
  88.8 1.0 copy-start.10
  89.7 0.9 copy-start.11
  111.2 0.7 copy-start.1

commit v5 on v4

--- a/solution.py
+++ b/solution.py
@@ -413,7 +413,7 @@
     hz = send("hz0", step_z(0), h_chunk)
     bx = send("bx0", step_x(0), b_chunk)
     (t_chunk,) = call(merge_kernel, [(Q, 128)], [VMEM] * 4)(y_chunk, y1, y2, y3)
-    h_pair, b_pair = join(h_chunk, hz), tie(join(b_chunk, bx), hz, y1)
+    h_pair, b_pair = join(h_chunk, hz), tie(join(b_chunk, bx), hz, y1, y3)
 
     tx = send("tx0", step_x(0), t_chunk)
     h1 = send("hz1", step_z(1), h_pair)

time: 114 us -> 115 us (level)
  blocking collectives: 19.9 us -> 22.7 us
  waiting for transfers between devices: 36.2 us -> 34.9 us
    all_to_all x1, blocking collectives: 10.8 us -> 12.7 us  [shards(): mixed = lax.all_to_all(mixed, ('deep', 'core'), 0, 0, tiled=True)]
    ppermute x26, waiting for transfers between devices: 36.2 us -> 34.9 us  [permute(): return lax.ppermute(value, ALL, pairs)]
  transfers between devices with their start and end apart: 26 -> 26, of which waited for: 13 -> 14; matrix products, arithmetic and copies ran while one was open for 2% -> 2% of each run, Pallas kernels for 2% -> 2%
where the time goes in v5:
time: 115 us
  waiting for transfers between devices  34.9 us (30%)
  starting transfers between devices  34.5 us (30%)
  blocking collectives  22.7 us (20%)
  Pallas kernels  16.7 us (15%)
  local copies, waits for them, and re-layouts  2.49 us (2%)
  other arithmetic  2.23 us (2%)
    ppermute x26, waiting for transfers between devices, permute(): return lax.ppermute(value, ALL, pairs)  34.9 us
    ppermute x26, starting transfers between devices, permute(): return lax.ppermute(value, ALL, pairs)  34.5 us
    all_to_all x1, blocking collectives, shards(): mixed = lax.all_to_all(mixed, ('deep', 'core'), 0, 0, tiled=True)  12.7 us
    pallas_call x1, Pallas kernels, shards(): call(chain_kernel, [(1, 128)], [VMEM] + [HBM] * 12, [pltpu.VMEM((8, 8 * Q...  11.4 us
    all_gather x1, blocking collectives, shards(): gathered = lax.all_gather(variances, 'panel', axis=0, tiled=True)  10.1 us
    unnamed x30, local copies, waits for them, and re-layouts  2.48 us
  transfers between devices with their start and end apart: 26, of which 14 were waited for; matrix products, arithmetic and copies ran while one was open for 2% of the time, Pallas kernels for 2%

profile of v5, /device:TPU:2, one launch (start us, length us, event | category | flops | bytes accessed | tf_op | source)
XLA Modules:
  0.0 114.5 jit_solution(16943647409034298099)
XLA Ops:
  0.6 2.0 %shard_map.102 = (f32[160,128]{1,0:T(8,128)}, f32[160,128]{1,0:T(8,128)}, f32[480,128]{1,0:T(8,128)}) custom-call(f32[40,160]{1,0:T(8,128)} %d2.1, f32[80,160]{1,0:T(8,128)} %b2.1, f32[160,240]{1,0:T(8,128)} %bitcast.9, f32[80,160]{1,0:T(8,128)} %d3.1, f32[20,160]{1,0:T(8,128)} %d1.1, f32[20,160]{1,0:T(8,128)} %b1.1, f32[10,160]{1,0:T(8,128)} %d0.1), custom_call_target="tpu_custom_call" | custom-call | tf_op jit(solution)/shard_map/pallas_call | solution.py:395
  2.7 2.4 %collective-permute-start.6 = (f32[480,128]{1,0:T(8,128)}, f32[480,128]{1,0:T(8,128)S(1)}, u32[]{:S(2)}, u32[]{:S(2)}) collective-permute-start(f32[480,128]{1,0:T(8,128)} %get-tuple-element.48), channel_id=1, source_target_pairs={{0,1},{1,0},{2,3},{3,2},{4,7},{5,6},{6,5},{7,4},{8,9},{9,8},{10,11... | collective-permute-start | bytes 737288 | tf_op jit(solution)/shard_map/bx0/ppermute | solution.py:63
  5.0 0.0 collective-permute-start
  5.0 3.2 %collective-permute-start.2 = (f32[160,128]{1,0:T(8,128)}, f32[160,128]{1,0:T(8,128)S(1)}, u32[]{:S(2)}, u32[]{:S(2)}) collective-permute-start(f32[160,128]{1,0:T(8,128)} %get-tuple-element.46.own), channel_id=1, source_target_pairs={{0,192},{1,193},{2,194},{3,195},{4,196},{5,197},{6,198},{7,199},{8... | collective-permute-start | bytes 245768 | tf_op jit(solution)/shard_map/y3/ppermute | solution.py:63
  8.3 0.2 collective-permute-start.4
  8.4 1.0 collective-permute-done.6
  9.4 1.0 pad_maximum_fusion.3.pair
  10.4 0.5 collective-permute-done.one
  10.9 0.0 collective-permute-done.2.three
  10.9 2.0 %collective-permute-done.4 = f32[160,128]{1,0:T(8,128)S(1)} collective-permute-done((f32[160,128]{1,0:T(8,128)}, f32[160,128]{1,0:T(8,128)S(1)}, u32[]{:S(2)}, u32[]{:S(2)}) %collective-permute-start.4) | collective-permute-done | bytes 81952 | tf_op jit(solution)/shard_map/hz0/ppermute | solution.py:63
  12.9 0.4 collective-permute-start.7
  13.3 2.0 %collective-permute-start.1 = (f32[160,128]{1,0:T(8,128)}, f32[160,128]{1,0:T(8,128)S(1)}, u32[]{:S(2)}, u32[]{:S(2)}) collective-permute-start(f32[160,128]{1,0:T(8,128)} %get-tuple-element.46.own), channel_id=1, source_target_pairs={{0,128},{1,129},{2,130},{3,131},{4,132},{5,133},{6,134},{7,135},{8... | collective-permute-start | bytes 245768 | tf_op jit(solution)/shard_map/y2/ppermute | solution.py:63
  15.3 0.9 pad_maximum_fusion.6
  16.2 5.9 %collective-permute-start.5 = (f32[320,128]{1,0:T(8,128)S(1)}, f32[320,128]{1,0:T(8,128)S(1)}, u32[]{:S(2)}, u32[]{:S(2)}) collective-permute-start(f32[320,128]{1,0:T(8,128)S(1)} %pad_maximum_fusion.6), channel_id=1, source_target_pairs={{0,56},{1,57},{2,58},{3,59},{4,12},{5,13},{6,14},{7,15},{8,16},{9,... | collective-permute-start | bytes 491528 | tf_op jit(solution)/shard_map/hz1/ppermute | solution.py:63
  22.2 0.9 copy-done
  23.0 0.2 shard_map.103
  23.3 1.5 %collective-permute-start.3 = (f32[160,128]{1,0:T(8,128)S(1)}, f32[160,128]{1,0:T(8,128)S(1)}, u32[]{:S(2)}, u32[]{:S(2)}) collective-permute-start(f32[160,128]{1,0:T(8,128)S(1)} %shard_map.103), channel_id=1, source_target_pairs={{0,1},{1,0},{2,3},{3,2},{4,7},{5,6},{6,5},{7,4},{8,9},{9,8},{10,11... | collective-permute-start | bytes 245768 | tf_op jit(solution)/shard_map/tx0/ppermute | solution.py:63
  24.8 0.0 collective-permute-done.7.last
  24.8 0.2 shard_map.104
  25.0 0.1 collective-permute-start.8
  25.1 2.7 %collective-permute-done.3 = f32[160,128]{1,0:T(8,128)S(1)} collective-permute-done((f32[160,128]{1,0:T(8,128)S(1)}, f32[160,128]{1,0:T(8,128)S(1)}, u32[]{:S(2)}, u32[]{:S(2)}) %collective-permute-start.3) | collective-permute-done | bytes 81952 | tf_op jit(solution)/shard_map/tx0/ppermute | solution.py:63
  27.8 1.4 %collective-permute-done.8 = f32[104,128]{1,0:T(8,128)S(1)} collective-permute-done((f32[104,128]{1,0:T(8,128)S(1)}, f32[104,128]{1,0:T(8,128)S(1)}, u32[]{:S(2)}, u32[]{:S(2)}) %collective-permute-start.8) | collective-permute-done | bytes 53280 | tf_op jit(solution)/shard_map/near1/ppermute | solution.py:63
  29.3 0.1 collective-permute-start.10
  29.4 0.6 collective-permute-start.9
  30.0 2.4 %collective-permute-start.11 = (f32[208,128]{1,0:T(8,128)S(1)}, f32[208,128]{1,0:T(8,128)S(1)}, u32[]{:S(2)}, u32[]{:S(2)}) collective-permute-start(f32[208,128]{1,0:T(8,128)S(1)} %pad_maximum_fusion.8), channel_id=1, source_target_pairs={{0,16},{1,17},{2,18},{3,19},{4,20},{5,21},{6,22},{7,23},{8,24},{9,... | collective-permute-start | bytes 319496 | tf_op jit(solution)/shard_map/near2/ppermute | solution.py:63
  32.4 0.0 collective-permute-start.12
  32.4 5.1 %collective-permute-done.11 = f32[208,128]{1,0:T(8,128)S(1)} collective-permute-done((f32[208,128]{1,0:T(8,128)S(1)}, f32[208,128]{1,0:T(8,128)S(1)}, u32[]{:S(2)}, u32[]{:S(2)}) %collective-permute-start.11) | collective-permute-done | bytes 106528 | tf_op jit(solution)/shard_map/near2/ppermute | solution.py:63
  37.6 0.0 collective-permute-done.12.other_one
  37.6 0.0 collective-permute-done.10
  37.6 0.0 collective-permute-done.9
  37.6 0.2 collective-permute-start.13
  37.8 3.8 %collective-permute-start.14 = (f32[320,128]{1,0:T(8,128)S(1)}, f32[320,128]{1,0:T(8,128)S(1)}, u32[]{:S(2)}, u32[]{:S(2)}) collective-permute-start(f32[320,128]{1,0:T(8,128)S(1)} %collective-permute-done.10), channel_id=1, source_target_pairs={{0,56},{1,57},{2,58},{3,59},{4,12},{5,13},{6,14},{7,15},{8,16},{9,... | collective-permute-start | bytes 491528 | tf_op jit(solution)/shard_map/hz3/ppermute | solution.py:63
  41.7 0.1 collective-permute-start.15
  41.8 1.3 %collective-permute-done.15.other_two = f32[208,128]{1,0:T(8,128)S(1)} collective-permute-done((f32[208,128]{1,0:T(8,128)S(1)}, f32[208,128]{1,0:T(8,128)S(1)}, u32[]{:S(2)}, u32[]{:S(2)}) %collective-permute-start.15) | collective-permute-done | bytes 106528 | tf_op jit(solution)/shard_map/near_swap2/ppermute | solution.py:63
  43.1 1.9 %collective-permute-done.14 = f32[320,128]{1,0:T(8,128)S(1)} collective-permute-done((f32[320,128]{1,0:T(8,128)S(1)}, f32[320,128]{1,0:T(8,128)S(1)}, u32[]{:S(2)}, u32[]{:S(2)}) %collective-permute-start.14) | collective-permute-done | bytes 163872 | tf_op jit(solution)/shard_map/hz3/ppermute | solution.py:63
  44.9 0.0 collective-permute-done.13
  45.0 5.1 %collective-permute-start.16 = (f32[1280,128]{1,0:T(8,128)S(1)}, f32[1280,128]{1,0:T(8,128)S(1)}, u32[]{:S(2)}, u32[]{:S(2)}) collective-permute-start(f32[1280,128]{1,0:T(8,128)S(1)} %pad_maximum_fusion.2.refs_4_), channel_id=1, source_target_pairs={{0,56},{1,57},{2,58},{3,59},{4,12},{5,13},{6,14},{7,15},{8,16},{9,... | collective-permute-start | bytes 1966088 | tf_op jit(solution)/shard_map/tz1/ppermute | solution.py:63
  50.1 3.0 %collective-permute-start.17 = (f32[1280,128]{1,0:T(8,128)S(1)}, f32[1280,128]{1,0:T(8,128)S(1)}, u32[]{:S(2)}, u32[]{:S(2)}) collective-permute-start(f32[1280,128]{1,0:T(8,128)S(1)} %constant_dynamic-update-slice_fusion.refs_0_), channel_id=1, source_target_pairs={{0,1},{1,0},{2,3},{3,2},{4,7},{5,6},{6,5},{7,4},{8,9},{9,8},{10,11... | collective-permute-start | bytes 1966088 | tf_op jit(solution)/shard_map/hx0/ppermute | solution.py:63
  53.1 2.3 %shard_map.105 = f32[8,40,128]{2,1,0:T(8,128)S(1)} custom-call(f32[416,128]{1,0:T(8,128)S(1)} %pad_maximum_fusion.5.near, f32[208,128]{1,0:T(8,128)S(1)} %collective-permute-done.12.other_one, f32[208,128]{1,0:T(8,128)S(1)} %collective-permute-done.15.other_two, f32[960,128]{1,0:T(8,128)S(1)} %pad_maximum_fusion.3.pair, ...), custom_call_target="tpu_custom_call" | custom-call | tf_op jit(solution)/shard_map/pallas_call | solution.py:450
  55.4 3.3 %collective-permute-done.16.refs_5_ = f32[1280,128]{1,0:T(8,128)S(1)} collective-permute-done((f32[1280,128]{1,0:T(8,128)S(1)}, f32[1280,128]{1,0:T(8,128)S(1)}, u32[]{:S(2)}, u32[]{:S(2)}) %collective-permute-start.16) | collective-permute-done | bytes 655392 | tf_op jit(solution)/shard_map/tz1/ppermute | solution.py:63
  58.7 3.0 %collective-permute-done.17.refs_1_ = f32[1280,128]{1,0:T(8,128)S(1)} collective-permute-done((f32[1280,128]{1,0:T(8,128)S(1)}, f32[1280,128]{1,0:T(8,128)S(1)}, u32[]{:S(2)}, u32[]{:S(2)}) %collective-permute-start.17) | collective-permute-done | bytes 655392 | tf_op jit(solution)/shard_map/hx0/ppermute | solution.py:63
  61.7 0.1 pad_maximum_fusion
  61.8 0.3 collective-permute-start.20
  62.1 0.1 collective-permute-start.18
  62.2 0.6 collective-permute-start.19
  62.8 12.7 %all_to_all.5.mixed = f32[8,40,128]{2,1,0:T(8,128)} all-to-all(f32[8,40,128]{2,1,0:T(8,128)S(1)} %shard_map.105), channel_id=1, replica_groups=mesh['row'=4,'high'=2,'deep'=4,'core'=2,'panel'=4] {'deep','core'}, dimensions={0} | all-to-all | bytes 327680 | tf_op jit(solution)/shard_map/all_to_all | solution.py:465
  75.5 0.0 collective-permute-done.18.refs_6_
  75.5 0.0 collective-permute-done.20.refs_8_
  75.6 0.1 pad_maximum_fusion.1
  75.7 0.1 collective-permute-start.23
  75.8 1.5 %collective-permute-start.21 = (f32[1280,128]{1,0:T(8,128)S(1)}, f32[1280,128]{1,0:T(8,128)S(1)}, u32[]{:S(2)}, u32[]{:S(2)}) collective-permute-start(f32[1280,128]{1,0:T(8,128)S(1)} %collective-permute-done.18.refs_6_), channel_id=1, source_target_pairs={{0,56},{1,57},{2,58},{3,59},{4,12},{5,13},{6,14},{7,15},{8,16},{9,... | collective-permute-start | bytes 1966088 | tf_op jit(solution)/shard_map/tz3/ppermute | solution.py:63
  77.3 0.4 collective-permute-start.22
  77.7 10.0 %collective-permute-done.21.refs_7_ = f32[1280,128]{1,0:T(8,128)S(1)} collective-permute-done((f32[1280,128]{1,0:T(8,128)S(1)}, f32[1280,128]{1,0:T(8,128)S(1)}, u32[]{:S(2)}, u32[]{:S(2)}) %collective-permute-start.21) | collective-permute-done | bytes 655392 | tf_op jit(solution)/shard_map/tz3/ppermute | solution.py:63
  87.7 0.2 collective-permute-done.22.refs_3_
  87.9 0.0 collective-permute-done.23.refs_9_
  87.9 0.0 collective-permute-start.24
  87.9 0.5 collective-permute-start.25
  88.4 1.6 %collective-permute-done.24.refs_10_ = f32[1280,128]{1,0:T(8,128)S(1)} collective-permute-done((f32[1280,128]{1,0:T(8,128)S(1)}, f32[1280,128]{1,0:T(8,128)S(1)}, u32[]{:S(2)}, u32[]{:S(2)}) %collective-permute-start.24) | collective-permute-done | bytes 655392 | tf_op jit(solution)/shard_map/swap_t3/ppermute | solution.py:63
  90.0 0.9 collective-permute-done.25.refs_11_
  91.0 0.9 copy-done.11
  91.9 11.4 %shard_map.106.own = f32[1,128]{1,0:T(1,128)} custom-call(f32[8,40,128]{2,1,0:T(8,128)} %all_to_all.5.mixed, f32[1280,128]{1,0:T(8,128)} %copy-done.3, f32[1280,128]{1,0:T(8,128)} %copy-done.5, f32[1280,128]{1,0:T(8,128)} %copy-done.7, f32[1280,128]{1,0:T(8,128)} %copy-done.9, f32[1280,128]{1,0:T(8,128)} %copy-done.2, f32[1280,128]{1,0:T(8,128)} %copy-done.4, ...), custom_call_target="tpu_custom_call" | custom-call | tf_op jit(solution)/shard_map/pallas_call | solution.py:476
  103.2 10.1 %all-gather = f32[4,1,128]{2,1,0:T(1,128)S(1)} all-gather(f32[1,1,128]{2,1,0:T(1,128)} %bitcast.8), channel_id=1, replica_groups=mesh['row'=4,'high'=2,'deep'=4,'core'=2,'panel'=4] {'panel'}, dimensions={0}, use_global_device_ids=true | all-gather | bytes 2560 | tf_op jit(solution)/shard_map/all_gather | solution.py:490
  113.3 0.7 copy-done.1
  113.9 0.6 shard_map.107
  (36 shorter events, 0.2 us)
Async XLA Ops:
  2.7 29.8 %copy-start.12 = (f32[160,128]{1,0:T(8,128)S(1)}, f32[160,128]{1,0:T(8,128)}, u32[]{:S(2)}) copy-start(f32[160,128]{1,0:T(8,128)} %get-tuple-element.47) | copy-start | bytes 245764
  2.7 6.7 %collective-permute-start.6 = (f32[480,128]{1,0:T(8,128)}, f32[480,128]{1,0:T(8,128)S(1)}, u32[]{:S(2)}, u32[]{:S(2)}) collective-permute-start(f32[480,128]{1,0:T(8,128)} %get-tuple-element.48), channel_id=1, source_target_pairs={{0,1},{1,0},{2,3},{3,2},{4,7},{5,6},{6,5},{7,4},{8,9},{9,8},{10,11... | collective-permute-start | bytes 737288 | tf_op jit(solution)/shard_map/bx0/ppermute | solution.py:63
  5.0 5.9 %collective-permute-start = (f32[160,128]{1,0:T(8,128)}, f32[160,128]{1,0:T(8,128)S(1)}, u32[]{:S(2)}, u32[]{:S(2)}) collective-permute-start(f32[160,128]{1,0:T(8,128)} %get-tuple-element.46.own), channel_id=1, source_target_pairs={{0,64},{1,65},{2,66},{3,67},{4,68},{5,69},{6,70},{7,71},{8,72},{9,... | collective-permute-start | bytes 245768 | tf_op jit(solution)/shard_map/y1/ppermute | solution.py:63
  5.0 5.9 %collective-permute-start.2 = (f32[160,128]{1,0:T(8,128)}, f32[160,128]{1,0:T(8,128)S(1)}, u32[]{:S(2)}, u32[]{:S(2)}) collective-permute-start(f32[160,128]{1,0:T(8,128)} %get-tuple-element.46.own), channel_id=1, source_target_pairs={{0,192},{1,193},{2,194},{3,195},{4,196},{5,197},{6,198},{7,199},{8... | collective-permute-start | bytes 245768 | tf_op jit(solution)/shard_map/y3/ppermute | solution.py:63
  8.3 4.7 %collective-permute-start.4 = (f32[160,128]{1,0:T(8,128)}, f32[160,128]{1,0:T(8,128)S(1)}, u32[]{:S(2)}, u32[]{:S(2)}) collective-permute-start(f32[160,128]{1,0:T(8,128)} %get-tuple-element.47), channel_id=1, source_target_pairs={{0,8},{1,9},{2,10},{3,11},{4,60},{5,61},{6,62},{7,63},{8,0},{9,1},... | collective-permute-start | bytes 245768 | tf_op jit(solution)/shard_map/hz0/ppermute | solution.py:63
  12.9 11.9 %collective-permute-start.7 = (f32[960,128]{1,0:T(8,128)S(1)}, f32[960,128]{1,0:T(8,128)S(1)}, u32[]{:S(2)}, u32[]{:S(2)}) collective-permute-start(f32[960,128]{1,0:T(8,128)S(1)} %pad_maximum_fusion.3.pair), channel_id=1, source_target_pairs={{0,3},{1,2},{2,1},{3,0},{4,5},{5,4},{6,7},{7,6},{8,11},{9,10},{10,... | collective-permute-start | bytes 1474568 | tf_op jit(solution)/shard_map/bx1/ppermute | solution.py:63
  13.3 8.8 %collective-permute-start.1 = (f32[160,128]{1,0:T(8,128)}, f32[160,128]{1,0:T(8,128)S(1)}, u32[]{:S(2)}, u32[]{:S(2)}) collective-permute-start(f32[160,128]{1,0:T(8,128)} %get-tuple-element.46.own), channel_id=1, source_target_pairs={{0,128},{1,129},{2,130},{3,131},{4,132},{5,133},{6,134},{7,135},{8... | collective-permute-start | bytes 245768 | tf_op jit(solution)/shard_map/y2/ppermute | solution.py:63
  16.2 11.6 %collective-permute-start.5 = (f32[320,128]{1,0:T(8,128)S(1)}, f32[320,128]{1,0:T(8,128)S(1)}, u32[]{:S(2)}, u32[]{:S(2)}) collective-permute-start(f32[320,128]{1,0:T(8,128)S(1)} %pad_maximum_fusion.6), channel_id=1, source_target_pairs={{0,56},{1,57},{2,58},{3,59},{4,12},{5,13},{6,14},{7,15},{8,16},{9,... | collective-permute-start | bytes 491528 | tf_op jit(solution)/shard_map/hz1/ppermute | solution.py:63
  22.2 0.9 copy-start
  23.3 4.5 %collective-permute-start.3 = (f32[160,128]{1,0:T(8,128)S(1)}, f32[160,128]{1,0:T(8,128)S(1)}, u32[]{:S(2)}, u32[]{:S(2)}) collective-permute-start(f32[160,128]{1,0:T(8,128)S(1)} %shard_map.103), channel_id=1, source_target_pairs={{0,1},{1,0},{2,3},{3,2},{4,7},{5,6},{6,5},{7,4},{8,9},{9,8},{10,11... | collective-permute-start | bytes 245768 | tf_op jit(solution)/shard_map/tx0/ppermute | solution.py:63
  25.0 4.2 %collective-permute-start.8 = (f32[104,128]{1,0:T(8,128)S(1)}, f32[104,128]{1,0:T(8,128)S(1)}, u32[]{:S(2)}, u32[]{:S(2)}) collective-permute-start(f32[104,128]{1,0:T(8,128)S(1)} %shard_map.104), channel_id=1, source_target_pairs={{0,8},{1,9},{2,10},{3,11},{4,12},{5,13},{6,14},{7,15},{8,0},{9,1},... | collective-permute-start | bytes 159752 | tf_op jit(solution)/shard_map/near1/ppermute | solution.py:63
  29.3 8.3 %collective-permute-start.10 = (f32[320,128]{1,0:T(8,128)S(1)}, f32[320,128]{1,0:T(8,128)S(1)}, u32[]{:S(2)}, u32[]{:S(2)}) collective-permute-start(f32[320,128]{1,0:T(8,128)S(1)} %collective-permute-done.5), channel_id=1, source_target_pairs={{0,8},{1,9},{2,10},{3,11},{4,60},{5,61},{6,62},{7,63},{8,0},{9,1},... | collective-permute-start | bytes 491528 | tf_op jit(solution)/shard_map/hz2/ppermute | solution.py:63
  29.4 8.2 %collective-permute-start.9 = (f32[320,128]{1,0:T(8,128)S(1)}, f32[320,128]{1,0:T(8,128)S(1)}, u32[]{:S(2)}, u32[]{:S(2)}) collective-permute-start(f32[320,128]{1,0:T(8,128)S(1)} %pad_maximum_fusion.7), channel_id=1, source_target_pairs={{0,3},{1,2},{2,1},{3,0},{4,5},{5,4},{6,7},{7,6},{8,11},{9,10},{10,... | collective-permute-start | bytes 491528 | tf_op jit(solution)/shard_map/tx1/ppermute | solution.py:63
  30.0 7.6 %collective-permute-start.11 = (f32[208,128]{1,0:T(8,128)S(1)}, f32[208,128]{1,0:T(8,128)S(1)}, u32[]{:S(2)}, u32[]{:S(2)}) collective-permute-start(f32[208,128]{1,0:T(8,128)S(1)} %pad_maximum_fusion.8), channel_id=1, source_target_pairs={{0,16},{1,17},{2,18},{3,19},{4,20},{5,21},{6,22},{7,23},{8,24},{9,... | collective-permute-start | bytes 319496 | tf_op jit(solution)/shard_map/near2/ppermute | solution.py:63
  32.4 5.1 %collective-permute-start.12 = (f32[208,128]{1,0:T(8,128)S(1)}, f32[208,128]{1,0:T(8,128)S(1)}, u32[]{:S(2)}, u32[]{:S(2)}) collective-permute-start(f32[208,128]{1,0:T(8,128)S(1)} %pad_maximum_fusion.8), channel_id=1, source_target_pairs={{0,4},{1,5},{2,6},{3,7},{4,0},{5,1},{6,2},{7,3},{8,12},{9,13},{10,... | collective-permute-start | bytes 319496 | tf_op jit(solution)/shard_map/near_swap1/ppermute | solution.py:63
  37.6 7.3 %collective-permute-start.13 = (f32[640,128]{1,0:T(8,128)S(1)}, f32[640,128]{1,0:T(8,128)S(1)}, u32[]{:S(2)}, u32[]{:S(2)}) collective-permute-start(f32[640,128]{1,0:T(8,128)S(1)} %pad_maximum_fusion.4), channel_id=1, source_target_pairs={{0,8},{1,9},{2,10},{3,11},{4,60},{5,61},{6,62},{7,63},{8,0},{9,1},... | collective-permute-start | bytes 983048 | tf_op jit(solution)/shard_map/tz0/ppermute | solution.py:63
  37.8 7.1 %collective-permute-start.14 = (f32[320,128]{1,0:T(8,128)S(1)}, f32[320,128]{1,0:T(8,128)S(1)}, u32[]{:S(2)}, u32[]{:S(2)}) collective-permute-start(f32[320,128]{1,0:T(8,128)S(1)} %collective-permute-done.10), channel_id=1, source_target_pairs={{0,56},{1,57},{2,58},{3,59},{4,12},{5,13},{6,14},{7,15},{8,16},{9,... | collective-permute-start | bytes 491528 | tf_op jit(solution)/shard_map/hz3/ppermute | solution.py:63
  41.7 1.4 %collective-permute-start.15 = (f32[208,128]{1,0:T(8,128)S(1)}, f32[208,128]{1,0:T(8,128)S(1)}, u32[]{:S(2)}, u32[]{:S(2)}) collective-permute-start(f32[208,128]{1,0:T(8,128)S(1)} %collective-permute-done.11), channel_id=1, source_target_pairs={{0,4},{1,5},{2,6},{3,7},{4,0},{5,1},{6,2},{7,3},{8,12},{9,13},{10,... | collective-permute-start | bytes 319496 | tf_op jit(solution)/shard_map/near_swap2/ppermute | solution.py:63
  45.0 16.8 %copy-start.2 = (f32[1280,128]{1,0:T(8,128)}, f32[1280,128]{1,0:T(8,128)S(1)}, u32[]{:S(2)}) copy-start(f32[1280,128]{1,0:T(8,128)S(1)} %pad_maximum_fusion.2.refs_4_) | copy-start | bytes 1966084
  45.0 17.2 %copy-start.3 = (f32[1280,128]{1,0:T(8,128)}, f32[1280,128]{1,0:T(8,128)S(1)}, u32[]{:S(2)}) copy-start(f32[1280,128]{1,0:T(8,128)S(1)} %constant_dynamic-update-slice_fusion.refs_0_) | copy-start | bytes 1966084
  45.0 13.7 %collective-permute-start.16 = (f32[1280,128]{1,0:T(8,128)S(1)}, f32[1280,128]{1,0:T(8,128)S(1)}, u32[]{:S(2)}, u32[]{:S(2)}) collective-permute-start(f32[1280,128]{1,0:T(8,128)S(1)} %pad_maximum_fusion.2.refs_4_), channel_id=1, source_target_pairs={{0,56},{1,57},{2,58},{3,59},{4,12},{5,13},{6,14},{7,15},{8,16},{9,... | collective-permute-start | bytes 1966088 | tf_op jit(solution)/shard_map/tz1/ppermute | solution.py:63
  50.1 11.5 %collective-permute-start.17 = (f32[1280,128]{1,0:T(8,128)S(1)}, f32[1280,128]{1,0:T(8,128)S(1)}, u32[]{:S(2)}, u32[]{:S(2)}) collective-permute-start(f32[1280,128]{1,0:T(8,128)S(1)} %constant_dynamic-update-slice_fusion.refs_0_), channel_id=1, source_target_pairs={{0,1},{1,0},{2,3},{3,2},{4,7},{5,6},{6,5},{7,4},{8,9},{9,8},{10,11... | collective-permute-start | bytes 1966088 | tf_op jit(solution)/shard_map/hx0/ppermute | solution.py:63
  58.7 16.8 %copy-start.4 = (f32[1280,128]{1,0:T(8,128)}, f32[1280,128]{1,0:T(8,128)S(1)}, u32[]{:S(2)}) copy-start(f32[1280,128]{1,0:T(8,128)S(1)} %collective-permute-done.16.refs_5_) | copy-start | bytes 1966084
  61.7 15.7 %copy-start.5 = (f32[1280,128]{1,0:T(8,128)}, f32[1280,128]{1,0:T(8,128)S(1)}, u32[]{:S(2)}) copy-start(f32[1280,128]{1,0:T(8,128)S(1)} %collective-permute-done.17.refs_1_) | copy-start | bytes 1966084
  61.8 13.7 %collective-permute-start.20 = (f32[3840,128]{1,0:T(8,128)S(1)}, f32[3840,128]{1,0:T(8,128)}, u32[]{:S(2)}, u32[]{:S(2)}) collective-permute-start(f32[3840,128]{1,0:T(8,128)S(1)} %pad_maximum_fusion), channel_id=1, source_target_pairs={{0,4},{1,5},{2,6},{3,7},{4,0},{5,1},{6,2},{7,3},{8,12},{9,13},{10,... | collective-permute-start | bytes 5898248 | tf_op jit(solution)/shard_map/swap1/ppermute | solution.py:63
  62.1 13.4 %collective-permute-start.18 = (f32[1280,128]{1,0:T(8,128)S(1)}, f32[1280,128]{1,0:T(8,128)S(1)}, u32[]{:S(2)}, u32[]{:S(2)}) collective-permute-start(f32[1280,128]{1,0:T(8,128)S(1)} %collective-permute-done.16.refs_5_), channel_id=1, source_target_pairs={{0,8},{1,9},{2,10},{3,11},{4,60},{5,61},{6,62},{7,63},{8,0},{9,1},... | collective-permute-start | bytes 1966088 | tf_op jit(solution)/shard_map/tz2/ppermute | solution.py:63
  62.2 13.3 %collective-permute-start.19 = (f32[1280,128]{1,0:T(8,128)S(1)}, f32[1280,128]{1,0:T(8,128)S(1)}, u32[]{:S(2)}, u32[]{:S(2)}) collective-permute-start(f32[1280,128]{1,0:T(8,128)S(1)} %constant_dynamic-update-slice_fusion.refs_0_), channel_id=1, source_target_pairs={{0,3},{1,2},{2,1},{3,0},{4,5},{5,4},{6,7},{7,6},{8,11},{9,10},{10,... | collective-permute-start | bytes 1966088 | tf_op jit(solution)/shard_map/hx1/ppermute | solution.py:63
  75.5 15.4 %copy-start.6 = (f32[1280,128]{1,0:T(8,128)}, f32[1280,128]{1,0:T(8,128)S(1)}, u32[]{:S(2)}) copy-start(f32[1280,128]{1,0:T(8,128)S(1)} %collective-permute-done.18.refs_6_) | copy-start | bytes 1966084
  75.5 15.4 %copy-start.7 = (f32[1280,128]{1,0:T(8,128)}, f32[1280,128]{1,0:T(8,128)S(1)}, u32[]{:S(2)}) copy-start(f32[1280,128]{1,0:T(8,128)S(1)} %collective-permute-done.19.refs_2_) | copy-start | bytes 1966084
  75.7 12.2 %collective-permute-start.23 = (f32[3840,128]{1,0:T(8,128)S(1)}, f32[3840,128]{1,0:T(8,128)}, u32[]{:S(2)}, u32[]{:S(2)}) collective-permute-start(f32[3840,128]{1,0:T(8,128)S(1)} %pad_maximum_fusion.1), channel_id=1, source_target_pairs={{0,4},{1,5},{2,6},{3,7},{4,0},{5,1},{6,2},{7,3},{8,12},{9,13},{10,... | collective-permute-start | bytes 5898248 | tf_op jit(solution)/shard_map/swap2/ppermute | solution.py:63
  75.8 11.9 %collective-permute-start.21 = (f32[1280,128]{1,0:T(8,128)S(1)}, f32[1280,128]{1,0:T(8,128)S(1)}, u32[]{:S(2)}, u32[]{:S(2)}) collective-permute-start(f32[1280,128]{1,0:T(8,128)S(1)} %collective-permute-done.18.refs_6_), channel_id=1, source_target_pairs={{0,56},{1,57},{2,58},{3,59},{4,12},{5,13},{6,14},{7,15},{8,16},{9,... | collective-permute-start | bytes 1966088 | tf_op jit(solution)/shard_map/tz3/ppermute | solution.py:63
  77.3 10.6 %collective-permute-start.22 = (f32[1280,128]{1,0:T(8,128)S(1)}, f32[1280,128]{1,0:T(8,128)S(1)}, u32[]{:S(2)}, u32[]{:S(2)}) collective-permute-start(f32[1280,128]{1,0:T(8,128)S(1)} %collective-permute-done.17.refs_1_), channel_id=1, source_target_pairs={{0,3},{1,2},{2,1},{3,0},{4,5},{5,4},{6,7},{7,6},{8,11},{9,10},{10,... | collective-permute-start | bytes 1966088 | tf_op jit(solution)/shard_map/hx2/ppermute | solution.py:63
  87.7 3.3 %copy-start.8 = (f32[1280,128]{1,0:T(8,128)}, f32[1280,128]{1,0:T(8,128)S(1)}, u32[]{:S(2)}) copy-start(f32[1280,128]{1,0:T(8,128)S(1)} %collective-permute-done.21.refs_7_) | copy-start | bytes 1966084
  87.9 3.1 %copy-start.9 = (f32[1280,128]{1,0:T(8,128)}, f32[1280,128]{1,0:T(8,128)S(1)}, u32[]{:S(2)}) copy-start(f32[1280,128]{1,0:T(8,128)S(1)} %collective-permute-done.22.refs_3_) | copy-start | bytes 1966084
  87.9 2.1 %collective-permute-start.24 = (f32[1280,128]{1,0:T(8,128)S(1)}, f32[1280,128]{1,0:T(8,128)S(1)}, u32[]{:S(2)}, u32[]{:S(2)}) collective-permute-start(f32[1280,128]{1,0:T(8,128)S(1)} %collective-permute-done.21.refs_7_), channel_id=1, source_target_pairs={{0,4},{1,5},{2,6},{3,7},{4,0},{5,1},{6,2},{7,3},{8,12},{9,13},{10,... | collective-permute-start | bytes 1966088 | tf_op jit(solution)/shard_map/swap_t3/ppermute | solution.py:63
  87.9 3.0 %collective-permute-start.25 = (f32[1280,128]{1,0:T(8,128)S(1)}, f32[1280,128]{1,0:T(8,128)S(1)}, u32[]{:S(2)}, u32[]{:S(2)}) collective-permute-start(f32[1280,128]{1,0:T(8,128)S(1)} %collective-permute-done.22.refs_3_), channel_id=1, source_target_pairs={{0,4},{1,5},{2,6},{3,7},{4,0},{5,1},{6,2},{7,3},{8,12},{9,13},{10,... | collective-permute-start | bytes 1966088 | tf_op jit(solution)/shard_map/swap_h2/ppermute | solution.py:63
  90.0 1.0 copy-start.10
  91.0 0.9 copy-start.11
  113.3 0.7 copy-start.1
